TPU v7x, 512 devices: a whole 4x4x16 slice. The times are simulated.
512 devices in a mesh: event: 16 (over x, z_hi, core), row: 32 (over y, z_lo).
Axes of the slice: x: 4, y: 4, z: 16 (z_hi: 2, z_lo: 8; z = z_hi * 8 + z_lo), core: 2. Of those that a mesh axis runs over, the one named last changes fastest.
Arguments:
- initial_head: float32 [16, 48, 128, 384], P('event', None, 'row'), may hold values from -6 to -1.5
- sat_conductivity: float32 [256], replicated, may hold values from 0.3 to 3
- vg_alpha: float32 [256], replicated, may hold values from 0.25 to 1
- vg_n: float32 [256], replicated, may hold values from 1.3 to 2.5
- zone_map: int32 [64, 192], P('row'), may hold values from 0 to 255, as said below
- forcing_plan: int32 [16, 2, 64], P('event', None, 'row'), may hold values from 0 to 3
- tensiometer_cells: int32 [16, 8192], P('event', 'row'), may hold values from 0 to 73727
- tensiometer_heads: float32 [16, 8192], P('event', 'row'), may hold values from -6 to -1
Outputs:
- final_head: float32 [16, 48, 128, 384], P('event', None, 'row')
- misfit: float32 [], replicated
- grad_conductivity: float32 [256], replicated
- grad_alpha: float32 [256], replicated
- grad_n: float32 [256], replicated
Inputs may be any that keep to these rules, and one draw needn't show every extreme that they name: `zone_map`: the zone of a block in block row a lies among the 16 zones from a * 2 * 2 onward, taken modulo 256. `tensiometer_cells`: tensiometer j lies in the rows j // 256 * 4 to j // 256 * 4 + 3; the entry is its offset inside that block of rows, as depth * 4 * 384 + row offset * 384 + column.
All inputs are finite; a program needn't handle non-finite values.
Results may differ from a plain program's by a relative error of at most 0.0003.
Values sent between devices are 32-bit elements; how exact they have to be, the bound alone decides.
No kernel may reach another device: no remote copies, remote signals or barrier semaphores. Data moves between devices by JAX's collectives and lax.ppermute only.
A program may use at most 64 MiB of HBM per device.

v0:
```python
import jax
import jax.numpy as jnp
from jax import lax
from jax.experimental import pallas as pl
from jax.experimental.pallas import tpu as pltpu
from jax.sharding import PartitionSpec as P

CFL = 0.4
IRRIGATION = 0.2
WATER_RANGE = 0.35

TILES = 6
SUB = 8
WIDTH = 384
ROWS = 8
FIELD = (ROWS, TILES, SUB, WIDTH)
OWN = (4, TILES, SUB, WIDTH)
NEAR = 28
ZONES = 256
KS, AL, N, N1, M, MP, IC0, IN1, LEV0, LEV1, IKS, IAL = range(12)
F32 = jnp.float32


def device(x, z_hi, core, y, z_lo):
    return ((x * 2 + z_hi) * 2 + core) * 32 + y * 8 + z_lo


PLANES = [
    [device(x, z_hi, core, y, z_lo) for y in range(4) for x in range(4) for core in range(2)]
    for z_hi in range(2)
    for z_lo in range(8)
]
RINGS = [
    [device(x, z_hi, core, y, z_lo) for z_hi in range(2) for z_lo in range(8)]
    for x in range(4)
    for core in range(2)
    for y in range(4)
]


def lanes_left(x):
    return pltpu.roll(x, WIDTH - 1, 1)


def lanes_right(x):
    return pltpu.roll(x, 1, 1)


def subs_up(x):
    return pltpu.roll(x, SUB - 1, 0)


def subs_down(x):
    return pltpu.roll(x, 1, 0)


def iota(shape, dim):
    return lax.broadcasted_iota(jnp.int32, shape, dim)


def split3(x):
    hi = x.astype(jnp.bfloat16)
    rest = x - hi.astype(F32)
    mid = rest.astype(jnp.bfloat16)
    return hi, mid, (rest - mid.astype(F32)).astype(jnp.bfloat16)


def exact_dot(pick, x, dims=(((1,), (0,)), ((), ()))):
    parts = [lax.dot_general(pick, part, dims, preferred_element_type=F32) for part in split3(x)]
    return parts[0] + (parts[1] + parts[2])


def pack_kernel(head, zone, plan, own, up, down, zones):
    for depth in range(TILES * SUB):
        block = head[depth]
        j, s = depth % TILES, depth // TILES
        for row in range(4):
            own[row, j, s : s + 1, :] = block[row : row + 1, :]
    wide = (iota((192, WIDTH), 1) // 2 == iota((192, WIDTH), 0)).astype(F32)
    blocks = jnp.dot(zone[...].astype(F32), wide, preferred_element_type=F32)
    zones[...] = blocks
    sub = iota((SUB, WIDTH), 0)
    for pair, out in ((0, down), (1, up)):
        out[0:TILES] = own[2 * pair]
        out[TILES : 2 * TILES] = own[2 * pair + 1]
        level = plan[0, pair].astype(F32)
        ids = jnp.broadcast_to(blocks[pair : pair + 1, :], (SUB, WIDTH))
        out[2 * TILES] = jnp.where(sub == 0, ids, level)


def cell_math(head, p):
    wet = jnp.log(-p[AL] * head)
    u = jnp.exp(p[N] * wet)
    d = 1.0 + u
    w = jnp.log(d)
    inv = 1.0 / d
    r = u * inv
    mw = p[M] * w
    q = jnp.exp(-0.5 * mw)
    f = jnp.exp(p[N1] * wet - mw)
    t = 1.0 - f
    kq = p[KS] * q * t
    half, twice = -0.5 * t, 2.0 * f
    e1 = p[MP] * w + p[M] * wet * r
    cond = kq * t
    cond_l = kq * p[N1] * (half * r - twice * inv)
    cond_n = kq * (half * e1 - twice * (wet - e1))
    inv_store = d * p[IC0] / f
    store_l = p[N] - r * (2.0 * p[N] - 1.0)
    store_n = p[IN1] + wet - e1 - r * wet
    return cond, cond_l, cond_n, inv_store, store_l, store_n


def row_params(prm, r):
    return [prm[r, i : i + 1, :] for i in range(12)]


def masks():
    last = iota((SUB, WIDTH), 1) == WIDTH - 1
    sub = iota((SUB, WIDTH), 0)
    return last, sub == 0, sub == SUB - 1


def row_open(meta, r):
    low = jnp.where(r == 2, meta[1], jnp.where(r == 6, meta[2], 1)).astype(F32)
    high = jnp.where(r == 5, meta[2], jnp.where(r == 1, meta[1], 1)).astype(F32)
    return low, high


def net_row(h, k, r, top, low, high):
    last, is_top, is_bottom = masks()
    hs = [h[r, j] for j in range(TILES)]
    ks = [k[r, j] for j in range(TILES)]

    def face(j):
        if j < TILES - 1:
            kd = 0.5 * (ks[j] + ks[j + 1])
            return kd, kd * (1.0 + hs[j] - hs[j + 1])
        kd = 0.5 * (ks[j] + subs_up(ks[0]))
        flow = kd * (1.0 + hs[j] - subs_up(hs[0]))
        return jnp.where(is_bottom, ks[j], kd), jnp.where(is_bottom, ks[j], flow)

    final = face(TILES - 1)
    above = (
        jnp.where(is_top, ks[0], subs_down(final[0])),
        jnp.where(is_top, top * ks[0], subs_down(final[1])),
    )
    for j in range(TILES):
        below = final if j == TILES - 1 else face(j)
        hj, kj = hs[j], ks[j]
        kf = jnp.where(last, 0.0, 0.5 * (kj + lanes_left(kj)))
        flow = kf * (lanes_left(hj) - hj)
        k_low = 0.5 * low * (k[r - 1, j] + kj)
        k_high = 0.5 * high * (k[r + 1, j] + kj)
        net = flow - lanes_right(flow) + above[1] - below[1]
        net = net + k_low * (h[r - 1, j] - hj) + k_high * (h[r + 1, j] - hj)
        total = kf + lanes_right(kf) + above[0] + below[0] + k_low + k_high
        above = below
        yield j, net, total


def first_kernel(
    meta, plan, tab_k, tab_a, tab_n, own, zones, from_low, from_high,
    h0, k1, kl1, kn1, ic1, g1, p1, q1, prm, zrel, spread,
):
    position, lower, upper = meta[0], meta[1], meta[2]
    has_low, has_high = lower > 0, upper > 0
    for row in range(2):
        for j in range(TILES):
            h0[row, j] = jnp.where(has_low, from_low[row * TILES + j], own[0, j])
            h0[6 + row, j] = jnp.where(has_high, from_high[row * TILES + j], own[3, j])
    h0[2:6] = own[...]
    extra_low, extra_high = from_low[2 * TILES], from_high[2 * TILES]
    z_low = jnp.where(has_low, extra_low[0:1, :], zones[0:1, :])
    z_high = jnp.where(has_high, extra_high[0:1, :], zones[1:2, :])
    sub = iota((SUB, WIDTH), 0)

    def by_row(a, b, c, d):
        return jnp.where(sub < 4, jnp.where(sub < 2, a, b), jnp.where(sub < 6, c, d))

    zone = by_row(z_low, zones[0:1, :], zones[1:2, :], z_high).astype(jnp.int32)
    base = 8 * position - 4
    rel = (zone - base) & (ZONES - 1)
    zrel[...] = rel
    sat = jnp.ones((SUB, WIDTH), F32)
    alpha, n = sat, 2.0 * sat
    for i in range(NEAR):
        at = (base + i) & (ZONES - 1)
        here = rel == i
        sat = jnp.where(here, tab_k[at], sat)
        alpha = jnp.where(here, tab_a[at], alpha)
        n = jnp.where(here, tab_n[at], n)
    n1 = n - 1.0
    lev_0 = by_row(extra_low[1:2, :], plan[0, 0].astype(F32), plan[0, 1].astype(F32), extra_high[1:2, :])
    lev_1 = by_row(0.0, plan[1, 0].astype(F32), plan[1, 1].astype(F32), 0.0) + 0.0 * sat
    made = (
        sat, alpha, n, n1, 1.0 - 1.0 / n, 1.0 / (n * n), 1.0 / (WATER_RANGE * n1 * alpha), 1.0 / n1,
        IRRIGATION * lev_0, IRRIGATION * lev_1, 1.0 / sat, 1.0 / alpha,
    )
    for i, value in enumerate(made):
        for r in range(ROWS):
            prm[r, i : i + 1, :] = value[r : r + 1, :]

    def cells(r, carry):
        p = row_params(prm, r)
        for j in range(TILES):
            k1[r, j], kl1[r, j], kn1[r, j], ic1[r, j], p1[r, j], q1[r, j] = cell_math(h0[r, j], p)
        return carry

    lax.fori_loop(0, ROWS, cells, 0)

    def flow(r, most):
        low, high = row_open(meta, r)
        is_own = jnp.logical_and(r >= 2, r <= 5)
        real = jnp.logical_or(is_own, jnp.where(r < 2, has_low, has_high))
        for j, net, total in net_row(h0, k1, r, prm[r, LEV0 : LEV0 + 1, :], low, high):
            ic = ic1[r, j]
            g = jnp.where(real, net * ic, 0.0)
            g1[r, j] = g
            p1[r, j] = g * p1[r, j]
            q1[r, j] = g * q1[r, j]
            most = jnp.maximum(most, jnp.where(is_own, total * ic, 0.0))
        return most

    most = lax.fori_loop(1, 7, flow, jnp.zeros((SUB, WIDTH), F32))
    most = jnp.maximum(jnp.maximum(most[:, :128], most[:, 128:256]), most[:, 256:])
    most = jnp.max(most, 0, keepdims=True)
    spread[...] = jnp.broadcast_to(most[None], spread.shape)


def second_kernel(
    meta, rates, sensors, h0, k1, kl1, kn1, ic1, g1, p1, q1, prm, zrel,
    h1_out, g2, spread,
    h1, k2, kl2, kn2, ic2, sl2, sn2, va, vb, wa, wb, w0, w1, w2, maps,
):
    size = CFL / jnp.max(rates[...])
    nothing = jnp.zeros((TILES, SUB, WIDTH), F32)
    for r in (0, ROWS - 1):
        for ref in (h1, k2, w0, w1, w2):
            ref[r] = nothing
    for r in (1, 6):
        for ref in (va, vb, wa, wb):
            ref[r] = nothing
    maps[...] = jnp.zeros(maps.shape, F32)

    def cells(r, carry):
        p = row_params(prm, r)
        for j in range(TILES):
            head = h0[r, j] + size * g1[r, j]
            h1[r, j] = head
            k2[r, j], kl2[r, j], kn2[r, j], ic2[r, j], sl2[r, j], sn2[r, j] = cell_math(head, p)
        return carry

    lax.fori_loop(1, 7, cells, 0)

    def flow(r, most):
        low, high = row_open(meta, r)
        for j, net, total in net_row(h1, k2, r, prm[r, LEV1 : LEV1 + 1, :], low, high):
            ic = ic2[r, j]
            g2[r - 2, j] = net * ic
            h1_out[r - 2, j] = h1[r, j]
            most = jnp.maximum(most, total * ic)
        return most

    most = jnp.max(lax.fori_loop(2, 6, flow, jnp.zeros((SUB, WIDTH), F32)))

    def places(cell):
        line = jnp.floor((cell + 0.5) * (1.0 / WIDTH))
        column = cell - WIDTH * line
        depth = jnp.floor((line + 0.5) * 0.25)
        block = jnp.floor((depth + 0.5) * (1.0 / TILES))
        return (line - 4.0 * depth) * 48.0 + (depth - TILES * block) * 8.0 + block, column

    count = sensors.shape[1]
    wide = sensors[...]
    tall = jnp.transpose(wide)
    line_wide = places(wide[0:1, :])[0].astype(jnp.int32)
    line_tall, column_tall = places(tall[:, 0:1])
    goal = tall[:, 1:2]
    pick = (iota((count, 192), 1) == line_tall.astype(jnp.int32)).astype(F32).astype(jnp.bfloat16)
    put = (iota((192, count), 0) == line_wide).astype(F32).astype(jnp.bfloat16)
    column = iota((count, WIDTH), 1) == column_tall.astype(jnp.int32)
    field_g = g2[...].reshape(192, WIDTH)
    field_h = h1_out[...].reshape(192, WIDTH) + size * field_g
    seen_h = jnp.sum(jnp.where(column, exact_dot(pick, field_h), 0.0), 1, keepdims=True)
    seen_g = jnp.sum(jnp.where(column, exact_dot(pick, field_g), 0.0), 1, keepdims=True)
    diff = seen_h - goal
    events = 16.0
    loss = (
        jnp.sum(diff * diff) * (0.5 / events),
        jnp.sum(diff * seen_g) * (1.0 / events),
        jnp.sum(seen_g * seen_g) * (0.5 / events),
    )
    va[2:6] = exact_dot(put, jnp.where(column, diff * (1.0 / events), 0.0)).reshape(OWN)
    vb[2:6] = exact_dot(put, jnp.where(column, seen_g * (1.0 / events), 0.0)).reshape(OWN)

    def scaled(r, carry):
        for j in range(TILES):
            ic = ic2[r, j]
            wa[r, j] = va[r, j] * ic
            wb[r, j] = vb[r, j] * ic
        return carry

    lax.fori_loop(2, 6, scaled, 0)
    last, is_top, is_bottom = masks()

    def back_two(r, carry):
        low, high = row_open(meta, r)
        top = prm[r, LEV1 : LEV1 + 1, :]
        own = jnp.logical_and(r >= 2, r <= 5)
        hs = [h1[r, j] for j in range(TILES)]
        ks = [k2[r, j] for j in range(TILES)]
        sums = [jnp.zeros((SUB, WIDTH), F32) for _ in range(12)]
        ws = [[w[r, j] for j in range(TILES)] for w in (wa, wb)]

        def face(j):
            if j < TILES - 1:
                half = 0.5 * (1.0 + hs[j] - hs[j + 1])
                kd = 0.5 * (ks[j] + ks[j + 1])
                out = []
                for w in ws:
                    dw = w[j + 1] - w[j]
                    out.append((half * dw, kd * dw))
                return out
            half = 0.5 * (1.0 + hs[j] - subs_up(hs[0]))
            kd = 0.5 * (ks[j] + subs_up(ks[0]))
            out = []
            for w in ws:
                dw = subs_up(w[0]) - w[j]
                out.append((jnp.where(is_bottom, -w[j], half * dw), jnp.where(is_bottom, 0.0, kd * dw)))
            return out

        final = face(TILES - 1)
        above = [
            (jnp.where(is_top, top * w[0], subs_down(f[0])), subs_down(f[1]))
            for w, f in zip(ws, final)
        ]
        for j in range(TILES):
            below = final if j == TILES - 1 else face(j)
            hj, kj = hs[j], ks[j]
            h_low, h_high = h1[r - 1, j], h1[r + 1, j]
            half_c = jnp.where(last, 0.0, 0.5 * (lanes_left(hj) - hj))
            kf = jnp.where(last, 0.0, 0.5 * (lanes_left(kj) + kj))
            half_l, half_h = 0.5 * low * (h_low - hj), 0.5 * high * (h_high - hj)
            k_low, k_high = 0.5 * low * (k2[r - 1, j] + kj), 0.5 * high * (k2[r + 1, j] + kj)
            kl, kn = kl2[r, j], kn2[r, j]
            inv_h = 1.0 / hj
            g = jnp.where(own, g2[jnp.clip(r - 2, 0, 3), j], 0.0)
            gl, gn = g * sl2[r, j], g * sn2[r, j]
            back = []
            for part, (w_ref, v_ref) in enumerate(((wa, va), (wb, vb))):
                w = ws[part][j]
                dw = w - lanes_left(w)
                e, f = half_c * dw, kf * dw
                d_low, d_high = w - w_ref[r - 1, j], w - w_ref[r + 1, j]
                gk = e + lanes_right(e) + below[part][0] + above[part][0]
                gk = gk + half_l * d_low + half_h * d_high
                gh = lanes_right(f) - f + below[part][1] - above[part][1]
                gh = gh - k_low * d_low - k_high * d_high
                v = v_ref[r, j]
                to_l = gk * kl - v * gl
                sums[3 * part] += gk * kj
                sums[3 * part + 1] += to_l
                sums[3 * part + 2] += gk * kn - v * gn
                back.append((v, gh + (to_l + v * g) * inv_h))
            (v_a, j_a), (v_b, j_b) = back
            us = (v_a + size * j_a, v_b + j_a + size * j_b, j_b)
            ic, pp, qq = ic1[r, j], p1[r, j], q1[r, j]
            for i, (u, w_ref) in enumerate(zip(us, (w0, w1, w2))):
                w_ref[r, j] = u * ic
                sums[6 + 2 * i] -= u * pp
                sums[7 + 2 * i] -= u * qq
            above = below
        flat = [jnp.sum(x, 0, keepdims=True) for x in sums]
        for q in range(3):
            of_a, of_b = flat[q], flat[3 + q]
            rows = [size * of_a, of_a + size * of_b, of_b]
            for c in range(3):
                if q > 0:
                    rows[c] = rows[c] + size * flat[6 + 2 * c + q - 1]
                maps[r, 4 * q + c : 4 * q + c + 1, :] = rows[c]
        return carry

    for ref in (wa, wb):
        ref[0] = nothing
        ref[7] = nothing
    lax.fori_loop(1, 7, back_two, 0)

    def back_one(r, carry):
        low, high = row_open(meta, r)
        top = prm[r, LEV0 : LEV0 + 1, :]
        before, after = jnp.maximum(r - 1, 0), jnp.minimum(r + 1, ROWS - 1)
        hs = [h0[r, j] for j in range(TILES)]
        refs = (w0, w1, w2)
        ws = [[w[r, j] for j in range(TILES)] for w in refs]
        sums = [jnp.zeros((SUB, WIDTH), F32) for _ in range(9)]

        def face(j):
            if j < TILES - 1:
                half = 0.5 * (1.0 + hs[j] - hs[j + 1])
                return [half * (w[j + 1] - w[j]) for w in ws]
            half = 0.5 * (1.0 + hs[j] - subs_up(hs[0]))
            return [jnp.where(is_bottom, -w[j], half * (subs_up(w[0]) - w[j])) for w in ws]

        final = face(TILES - 1)
        above = [jnp.where(is_top, top * w[0], subs_down(f)) for w, f in zip(ws, final)]
        for j in range(TILES):
            below = final if j == TILES - 1 else face(j)
            hj = hs[j]
            half_c = jnp.where(last, 0.0, 0.5 * (lanes_left(hj) - hj))
            half_l = 0.5 * low * (h0[before, j] - hj)
            half_h = 0.5 * high * (h0[after, j] - hj)
            kj, kl, kn = k1[r, j], kl1[r, j], kn1[r, j]
            for part, w_ref in enumerate(refs):
                w = ws[part][j]
                e = half_c * (w - lanes_left(w))
                gk = e + lanes_right(e) + below[part] + above[part]
                gk = gk + half_l * (w - w_ref[before, j]) + half_h * (w - w_ref[after, j])
                sums[3 * part] += gk * kj
                sums[3 * part + 1] += gk * kl
                sums[3 * part + 2] += gk * kn
            above = below
        inv_k, inv_a = prm[r, IKS : IKS + 1, :], prm[r, IAL : IAL + 1, :]
        for q in range(3):
            for c in range(3):
                at = 4 * q + c
                row = maps[r, at : at + 1, :] + size * jnp.sum(sums[3 * c + q], 0, keepdims=True)
                maps[r, at : at + 1, :] = row if q == 2 else row * (inv_k if q == 0 else inv_a)
        return carry

    lax.fori_loop(0, ROWS, back_one, 0)

    left = jnp.concatenate([maps[r] for r in range(ROWS)], 1)
    near = zrel[...]
    zone_id = iota((32, WIDTH), 0)
    onehot = jnp.concatenate([(zone_id == near[r : r + 1, :]).astype(F32) for r in range(ROWS)], 1)
    onehot = onehot.astype(jnp.bfloat16)
    nt = (((1,), (1,)), ((), ()))
    parts = [lax.dot_general(part, onehot, nt, preferred_element_type=F32) for part in split3(left)]
    by_zone = parts[0] + (parts[1] + parts[2])
    fields = [by_zone[4 * q : 4 * q + 4, :] for q in range(3)]
    sub4 = iota((4, 32), 0)
    fields.append(jnp.where(sub4 == 0, loss[0], jnp.where(sub4 == 1, loss[1], loss[2])))
    sums = jnp.concatenate(fields, 1)
    state = jnp.where(iota((4, 128), 1) < 64, most, size)
    payload = jnp.where(iota((4, 128), 0) == 3, state, sums)
    spread[...] = jnp.broadcast_to(payload[None], spread.shape)


def ring_kernel(parts, spread):
    lane = iota((SUB, 256), 1)
    total = jnp.zeros((SUB, 256), F32)
    blank = jnp.zeros((SUB, 128), F32)
    most = None
    loss = jnp.zeros((SUB, 256), F32)
    for z in range(8):
        tile = jnp.concatenate([parts[z], parts[8 + z]], 0)
        most = tile if most is None else jnp.maximum(most, tile)
        tile = jnp.concatenate([tile, blank], 1)
        for q in range(3):
            start = 84 * q + 8 * z
            moved = pltpu.roll(tile, (start - 32 * q) % 256, 1)
            total = total + jnp.where(jnp.logical_and(lane >= start, lane < start + NEAR), moved, 0.0)
        loss = loss + tile
    total = jnp.where(lane == 252, pltpu.roll(loss, 252 - 96, 1), total)
    state = jnp.concatenate(
        [jnp.broadcast_to(most[:, 0:1], (SUB, 128)), jnp.broadcast_to(most[:, 64:65], (SUB, 128))], 1
    )
    total = jnp.where(iota((SUB, 256), 0) % 4 == 3, state, total)
    spread[...] = jnp.broadcast_to(total[None], spread.shape)


def last_kernel(meta, parts, h1, g2, final, grad_k, grad_a, grad_n, misfit, rates):
    sub = iota((SUB, 256), 0)
    power = sub % 4
    sums = [jnp.zeros((SUB, 256), F32) for _ in range(4)]
    for pair in range(8):
        tiles = [parts[8 * y + pair] for y in range(4)]
        most = jnp.maximum(jnp.maximum(tiles[0], tiles[1]), jnp.maximum(tiles[2], tiles[3]))
        step = CFL / most
        rates[pair] = step
        moves = []
        for row in (3, 7):
            move = step[row : row + 1, :128] - most[row : row + 1, 128:]
            moves.append(jnp.concatenate([move, move], 1))
        move = jnp.where(sub < 4, moves[0], moves[1])
        weight = jnp.where(power == 0, 1.0, jnp.where(power == 1, move, move * move))
        for y in range(4):
            sums[y] = sums[y] + jnp.where(power == 3, 0.0, tiles[y] * weight)
    lane = iota((1, 256), 1)
    rows = [jnp.sum(x, 0, keepdims=True) for x in sums]
    for q, out in enumerate((grad_k, grad_a, grad_n)):
        total = jnp.zeros((1, 256), F32)
        for y in range(4):
            field = rows[y] if q == 0 else pltpu.roll(rows[y], 256 - 84 * q, 1)
            total = total + pltpu.roll(jnp.where(lane < 84, field, 0.0), (64 * y - 4) % 256, 1)
        out[...] = total
    misfit[0, 0] = jnp.sum(jnp.where(lane == 252, rows[0] + rows[1] + rows[2] + rows[3], 0.0))
    mine = rates[meta[3]]
    size = jnp.where(meta[4] == 0, mine[3:4, :128], mine[7:8, :128])
    size = jnp.concatenate([size, size, size], 1)
    for j in range(TILES):
        for row in range(4):
            tile = h1[row, j] + size * g2[row, j]
            for s in range(SUB):
                final[TILES * s + j, row : row + 1, :] = tile[s : s + 1, :]


VMEM = pl.BlockSpec(memory_space=pltpu.VMEM)
SMEM = pl.BlockSpec(memory_space=pltpu.SMEM)


def call(kernel, name, ins, outs, out_specs=None, scratch=()):
    out_shape = [jax.ShapeDtypeStruct(*o) if isinstance(o, tuple) else o for o in outs]
    return pl.pallas_call(
        kernel,
        name=name,
        in_specs=ins,
        out_specs=out_specs or [VMEM] * len(outs),
        out_shape=out_shape,
        scratch_shapes=scratch,
        compiler_params=pltpu.CompilerParams(vmem_limit_bytes=48 * 1024 * 1024),
    )


def local(
    initial_head,
    sat_conductivity,
    vg_alpha,
    vg_n,
    zone_map,
    forcing_plan,
    tensiometer_cells,
    tensiometer_heads,
):
    position = lax.axis_index("row")
    count = lax.axis_size("row")
    event = lax.axis_index("event")
    meta = jnp.stack(
        [
            position,
            (position > 0).astype(jnp.int32),
            (position < count - 1).astype(jnp.int32),
            event // 4 * 2 + event % 2,
            event // 2 % 2,
        ]
    )
    plan = forcing_plan[0]
    edge = (2 * TILES + 1, SUB, WIDTH)
    own, up, down, zones = call(
        pack_kernel,
        "pack_edges",
        [VMEM, VMEM, SMEM],
        [(OWN, F32), (edge, F32), (edge, F32), ((2, WIDTH), F32)],
    )(initial_head[0], zone_map, plan)
    upward = [(i, i + 1) for i in range(count - 1)]
    from_low = lax.ppermute(up, "row", upward)
    from_high = lax.ppermute(down, "row", [(j, i) for i, j in upward])
    first = call(
        first_kernel,
        "first_step",
        [SMEM] * 5 + [VMEM] * 4,
        [(FIELD, F32)] * 8
        + [((ROWS, 16, WIDTH), F32), ((ROWS, WIDTH), jnp.int32), ((32, 1, 128), F32)],
    )(meta, plan, sat_conductivity, vg_alpha, vg_n, own, zones, from_low, from_high)
    fields, rates = first[:-1], first[-1]
    rates = lax.all_to_all(rates, "row", 0, 0, tiled=True)
    sensors = jnp.concatenate(
        [tensiometer_cells.astype(F32), tensiometer_heads, jnp.zeros((6, 256), F32)], 0
    )
    scratch = [pltpu.VMEM(FIELD, F32)] * 14 + [pltpu.VMEM((ROWS, 16, WIDTH), F32)]
    h1, g2, sums = call(
        second_kernel,
        "second_step_and_adjoint",
        [SMEM] + [VMEM] * 12,
        [(OWN, F32), (OWN, F32), ((16, 4, 128), F32)],
        scratch=scratch,
    )(meta, rates, sensors, *fields)
    sums = lax.all_to_all(sums, ("event", "row"), 0, 0, tiled=True, axis_index_groups=RINGS)
    (sums,) = call(ring_kernel, "ring_sums", [VMEM], [((32, SUB, 256), F32)])(sums)
    sums = lax.all_to_all(sums, ("event", "row"), 0, 0, tiled=True, axis_index_groups=PLANES)
    row = ((1, ZONES), F32)
    final, grad_k, grad_a, grad_n, misfit = call(
        last_kernel,
        "final_head_and_sums",
        [SMEM, VMEM, VMEM, VMEM],
        [((48, 4, WIDTH), F32), row, row, row, ((1, 1), F32)],
        [VMEM] * 4 + [SMEM],
        scratch=[pltpu.VMEM((8, SUB, 256), F32)],
    )(meta, sums, h1, g2)
    return (final[None], misfit[0, 0], grad_k[0], grad_a[0], grad_n[0])


def solution(mesh):
    return jax.shard_map(
        local,
        mesh=mesh,
        in_specs=(
            P("event", None, "row", None),
            P(),
            P(),
            P(),
            P("row", None),
            P("event", None, "row"),
            P("event", "row"),
            P("event", "row"),
        ),
        out_specs=(P("event", None, "row", None), P(), P(), P(), P()),
        check_vma=False,
    )
```

profile of v0, /device:TPU:1, one launch (start us, length us, event | category | flops | bytes accessed | tf_op | source)
XLA Modules:
  0.0 118.1 jit_solution(14703518124345544557)
XLA Ops:
  1.3 1.0 copy-done.4
  2.3 0.8 pack_edges.1
  3.1 0.7 copy-done.5
  3.8 4.4 %collective-permute-start = (f32[13,8,384]{2,1,0:T(8,128)S(1)}, f32[13,8,384]{2,1,0:T(8,128)S(1)}, u32[]{:S(2)}, u32[]{:S(2)}) collective-permute-start(f32[13,8,384]{2,1,0:T(8,128)S(1)} %get-tuple-element.30), channel_id=1, source_target_pairs={{0,1},{1,2},{2,3},{3,4},{4,5},{5,6},{6,7},{7,8},{8,9},{9,10},{10,1... | collective-permute-start | bytes 479240 | tf_op jit(solution)/shard_map/ppermute | solution.py:557
  8.2 1.3 %collective-permute-start.1 = (f32[13,8,384]{2,1,0:T(8,128)S(1)}, f32[13,8,384]{2,1,0:T(8,128)S(1)}, u32[]{:S(2)}, u32[]{:S(2)}) collective-permute-start(f32[13,8,384]{2,1,0:T(8,128)S(1)} %get-tuple-element.31), channel_id=1, source_target_pairs={{1,0},{2,1},{3,2},{4,3},{5,4},{6,5},{7,6},{8,7},{9,8},{10,9},{11,1... | collective-permute-start | bytes 479240 | tf_op jit(solution)/shard_map/ppermute | solution.py:558
  12.2 2.2 %collective-permute-done.1.from_high = f32[13,8,384]{2,1,0:T(8,128)S(1)} collective-permute-done((f32[13,8,384]{2,1,0:T(8,128)S(1)}, f32[13,8,384]{2,1,0:T(8,128)S(1)}, u32[]{:S(2)}, u32[]{:S(2)}) %collective-permute-start.1) | collective-permute-done | bytes 159776 | tf_op jit(solution)/shard_map/ppermute | solution.py:558
  15.7 1.0 copy-done.6
  16.7 0.9 copy-done.10
  17.6 0.9 copy-done.12
  19.2 3.3 %first_step.1 = (f32[8,6,8,384]{3,2,1,0:T(8,128)S(1)}, f32[8,6,8,384]{3,2,1,0:T(8,128)S(1)}, f32[8,6,8,384]{3,2,1,0:T(8,128)S(1)}, f32[8,6,8,384]{3,2,1,0:T(8,12...) custom-call(s32[5]{0:T(128)S(1)} %stack.31.meta, ...), custom_call_target="tpu_custom_call" | custom-call | tf_op jit(solution)/shard_map/first_step/pallas_call | solution.py:559
  22.5 0.8 copy-done
  23.3 0.8 copy-done.2
  26.5 21.8 %all-to-all-start = ((f32[32,1,128]{2,1,0:T(1,128)}), f32[32,1,128]{2,1,0:T(1,128)S(1)}, u32[]{:S(2)}, u32[]{:S(2)}) async-start(f32[32,1,128]{2,1,0:T(1,128)} %copy-done.14), calls=%async_computation | async-start | bytes 32768 | tf_op jit(solution)/shard_map/all_to_all | solution.py:567
  48.3 1.4 %maximum_maximum_fusion.sensors = f32[8,256]{1,0:T(8,128)} fusion(f32[1,256]{1,0:T(1,128)} %param.15, f32[1,256]{1,0:T(1,128)} %convert_element_type.2, f32[8]{0:T(128)} %pad.2.clone), kind=kLoop, calls=%fused_computation | loop fusion | flops 4096 | bytes 10272 | tf_op jit(solution)/shard_map/concatenate | solution.py:568
  49.7 10.0 %all-to-all-done.rates = f32[32,1,128]{2,1,0:T(1,128)S(1)} async-done(((f32[32,1,128]{2,1,0:T(1,128)}), f32[32,1,128]{2,1,0:T(1,128)S(1)}, u32[]{:S(2)}, u32[]{:S(2)}) %all-to-all-start) | async-done | bytes 16416 | tf_op jit(solution)/shard_map/all_to_all | solution.py:567
  59.7 0.7 copy-done.13
  60.4 1.1 copy-done.1
  61.4 1.1 copy-done.3
  62.5 0.9 copy-done.8
  63.4 0.7 copy-done.16
  64.1 10.2 %second_step_and_adjoint.1 = (f32[4,6,8,384]{3,2,1,0:T(8,128)S(1)}, f32[4,6,8,384]{3,2,1,0:T(8,128)S(1)}, f32[16,4,128]{2,1,0:T(4,128)S(1)}) custom-call(s32[5]{0:T(128)S(1)} %copy-done.18, f32[32,1,128]{2,1,0:T(1,128)S(1)} %all-to-all-done.rates, f32[8,256]{1,0:T(8,128)S(1)} %copy-done.13, f32[8,6,8,384]{3,2,1,0:T(8,128)S(1)} %get-tuple-element.33.h0, ...), custom_call_target="tpu_custom_call" | custom-call | tf_op jit(solution)/shard_map/second_step_and_adjoint/pallas_call | solution.py:572
  74.4 23.7 %all_to_all.15.parts = f32[16,4,128]{2,1,0:T(4,128)S(1)} all-to-all(f32[16,4,128]{2,1,0:T(4,128)S(1)} %get-tuple-element.43), channel_id=1, replica_groups={{0,1,2,3,4,5,6,7,64,65,66,67,68,69,70,71},{8,9,10,11,12,13,14,15,72,73,..., dimensions={0} | all-to-all | bytes 65536 | tf_op jit(solution)/shard_map/all_to_all | solution.py:579
  98.2 18.4 %all_to_all.16.parts = f32[32,8,256]{2,1,0:T(8,128)S(1)} all-to-all(f32[32,8,256]{2,1,0:T(8,128)S(1)} %ring_sums.1), channel_id=1, replica_groups={{0,32,128,160,256,288,384,416,8,40,136,168,264,296,392,424,16,48,144,17..., dimensions={0} | all-to-all | bytes 524288 | tf_op jit(solution)/shard_map/all_to_all | solution.py:581
  116.6 1.5 %final_head_and_sums.1 = (f32[48,4,384]{2,1,0:T(4,128)}, f32[1,256]{1,0:T(1,128)}, f32[1,256]{1,0:T(1,128)}, f32[1,256]{1,0:T(1,128)}, f32[1,1]{1,0:T(1,128)}) custom-call(s32[5]{0:T(128)S(1)} %copy-done.18, f32[32,8,256]{2,1,0:T(8,128)S(1)} %all_to_all.16.parts, f32[4,6,8,384]{3,2,1,0:T(8,128)S(1)} %get-tuple-element.44.h1, ...), custom_call_target="tpu_custom_call" | custom-call | tf_op jit(solution)/shard_map/final_head_and_sums/pallas_call | solution.py:583
  (44 shorter events, 7.8 us)
Async XLA Ops:
  0.6 0.7 copy-start.20
  0.6 0.7 copy-start.19
  1.3 1.0 copy-start.4
  3.1 0.7 copy-start.5
  3.8 7.7 %collective-permute-start = (f32[13,8,384]{2,1,0:T(8,128)S(1)}, f32[13,8,384]{2,1,0:T(8,128)S(1)}, u32[]{:S(2)}, u32[]{:S(2)}) collective-permute-start(f32[13,8,384]{2,1,0:T(8,128)S(1)} %get-tuple-element.30), channel_id=1, source_target_pairs={{0,1},{1,2},{2,3},{3,4},{4,5},{5,6},{6,7},{7,8},{8,9},{9,10},{10,1... | collective-permute-start | bytes 479240 | tf_op jit(solution)/shard_map/ppermute | solution.py:557
  8.2 6.2 %collective-permute-start.1 = (f32[13,8,384]{2,1,0:T(8,128)S(1)}, f32[13,8,384]{2,1,0:T(8,128)S(1)}, u32[]{:S(2)}, u32[]{:S(2)}) collective-permute-start(f32[13,8,384]{2,1,0:T(8,128)S(1)} %get-tuple-element.31), channel_id=1, source_target_pairs={{1,0},{2,1},{3,2},{4,3},{5,4},{6,5},{7,6},{8,7},{9,8},{10,9},{11,1... | collective-permute-start | bytes 479240 | tf_op jit(solution)/shard_map/ppermute | solution.py:558
  9.5 0.7 copy-start.24
  11.4 3.7 %copy-start.22 = (f32[256]{0:T(256)S(1)}, f32[256]{0:T(256)}, u32[]{:S(2)}) copy-start(f32[256]{0:T(256)} %tab_a.1) | copy-start | bytes 3076
  11.5 0.7 copy-start.9
  15.0 0.7 copy-start.21
  15.7 1.0 copy-start.6
  16.7 0.9 copy-start.10
  17.6 0.9 copy-start.12
  18.5 0.7 copy-start.23
  22.5 0.8 copy-start
  23.3 0.8 copy-start.2
  24.1 0.7 copy-start.7
  26.5 33.2 %all-to-all-start = ((f32[32,1,128]{2,1,0:T(1,128)}), f32[32,1,128]{2,1,0:T(1,128)S(1)}, u32[]{:S(2)}, u32[]{:S(2)}) async-start(f32[32,1,128]{2,1,0:T(1,128)} %copy-done.14), calls=%async_computation | async-start | bytes 32768 | tf_op jit(solution)/shard_map/all_to_all | solution.py:567
  59.7 0.7 copy-start.13
  59.7 0.7 copy-start.18
  60.4 1.1 copy-start.1
  61.4 1.1 copy-start.3
  62.5 0.9 copy-start.8
  63.4 0.7 copy-start.16
  (4 other events, 2.4 us)
where the time goes:
time: 119 us; the launch traced here: 118 us
  blocking collectives  42.1 us (35%)
  starting transfers between devices  27.5 us (23%)
  local copies, waits for them, and re-layouts  17.7 us (15%)
  Pallas kernels  16 us (13%)
  waiting for transfers between devices  12.2 us (10%)
  other arithmetic  1.92 us (2%)
    all_to_all x2, blocking collectives, local(): lax.all_to_all(sums, ('event', 'row'), 0, 0, tiled=True, axis_index_group...  42.1 us
    all_to_all x1, starting transfers between devices, local(): rates = lax.all_to_all(rates, 'row', 0, 0, tiled=True)  21.8 us
    unnamed x50, local copies, waits for them, and re-layouts  17 us
    pallas_call x1, Pallas kernels, local(): call(second_kernel, 'second_step_and_adjoint', [SMEM] + [VMEM] * 12, [(OW...  10.2 us
    all_to_all x1, waiting for transfers between devices, local(): rates = lax.all_to_all(rates, 'row', 0, 0, tiled=True)  9.98 us
    ppermute x1, starting transfers between devices, local(): from_low = lax.ppermute(up, 'row', upward)  4.37 us
    pallas_call x1, Pallas kernels, local(): call(first_kernel, 'first_step', [SMEM] * 5 + [VMEM] * 4, [(FIELD, F32)]...  3.28 us
  transfers between devices with their start and end apart: 3, of which 2 were waited for; matrix products, arithmetic and copies ran while one was open for 2% of the time, Pallas kernels for 0%

commit v1 on v0

--- a/solution.py
+++ b/solution.py
@@ -70,25 +70,50 @@
     return parts[0] + (parts[1] + parts[2])
 
 
-def pack_kernel(head, zone, plan, own, up, down, zones):
+def axes():
+    event = lax.axis_index("event")
+    return lax.axis_index("row"), event // 4 * 2 + event % 2, event // 2 % 2
+
+
+def pack_kernel(head_in, zone_in, plan_in, own, send_odd, send_even, zones, head, zone, plan, sems):
+    copies = [
+        pltpu.make_async_copy(src, dst, sems.at[i])
+        for i, (src, dst) in enumerate(((head_in, head), (zone_in, zone), (plan_in, plan)))
+    ]
+    for copy in copies:
+        copy.start()
+    wide = (iota((192, WIDTH), 1) // 2 == iota((192, WIDTH), 0)).astype(F32)
+    copies[1].wait()
+    copies[2].wait()
+    blocks = jnp.dot(zone[...].astype(F32), wide, preferred_element_type=F32)
+    zones[...] = blocks
+    level = plan[...].astype(F32)
+    copies[0].wait()
     for depth in range(TILES * SUB):
         block = head[depth]
         j, s = depth % TILES, depth // TILES
         for row in range(4):
             own[row, j, s : s + 1, :] = block[row : row + 1, :]
-    wide = (iota((192, WIDTH), 1) // 2 == iota((192, WIDTH), 0)).astype(F32)
-    blocks = jnp.dot(zone[...].astype(F32), wide, preferred_element_type=F32)
-    zones[...] = blocks
     sub = iota((SUB, WIDTH), 0)
-    for pair, out in ((0, down), (1, up)):
+    odd = lax.axis_index("row") % 2 == 1
+
+    def fill(out, pair):
         out[0:TILES] = own[2 * pair]
         out[TILES : 2 * TILES] = own[2 * pair + 1]
-        level = plan[0, pair].astype(F32)
-        ids = jnp.broadcast_to(blocks[pair : pair + 1, :], (SUB, WIDTH))
-        out[2 * TILES] = jnp.where(sub == 0, ids, level)
-
-
-def cell_math(head, p):
+        out[2 * TILES] = jnp.where(sub == 0, blocks[pair : pair + 1, :], level[0:1, pair : pair + 1])
+
+    @pl.when(odd)
+    def _():
+        fill(send_odd, 1)
+        fill(send_even, 0)
+
+    @pl.when(jnp.logical_not(odd))
+    def _():
+        fill(send_odd, 0)
+        fill(send_even, 1)
+
+
+def cell_math(head, p, with_store=True):
     wet = jnp.log(-p[AL] * head)
     u = jnp.exp(p[N] * wet)
     d = 1.0 + u
@@ -105,14 +130,23 @@
     cond = kq * t
     cond_l = kq * p[N1] * (half * r - twice * inv)
     cond_n = kq * (half * e1 - twice * (wet - e1))
+    if not with_store:
+        return cond, cond_l, cond_n
     inv_store = d * p[IC0] / f
     store_l = p[N] - r * (2.0 * p[N] - 1.0)
     store_n = p[IN1] + wet - e1 - r * wet
     return cond, cond_l, cond_n, inv_store, store_l, store_n
 
 
+def derived(sat, alpha, n):
+    n1 = n - 1.0
+    return (
+        sat, alpha, n, n1, 1.0 - 1.0 / n, 1.0 / (n * n), 1.0 / (WATER_RANGE * n1 * alpha), 1.0 / n1,
+    )
+
+
 def row_params(prm, r):
-    return [prm[r, i : i + 1, :] for i in range(12)]
+    return [prm[r, i : i + 1, :] for i in range(8)]
 
 
 def masks():
@@ -121,9 +155,11 @@
     return last, sub == 0, sub == SUB - 1
 
 
-def row_open(meta, r):
-    low = jnp.where(r == 2, meta[1], jnp.where(r == 6, meta[2], 1)).astype(F32)
-    high = jnp.where(r == 5, meta[2], jnp.where(r == 1, meta[1], 1)).astype(F32)
+def row_open(position, r):
+    lower = (position > 0).astype(jnp.int32)
+    upper = (position < lax.axis_size("row") - 1).astype(jnp.int32)
+    low = jnp.where(r == 2, lower, jnp.where(r == 6, upper, 1)).astype(F32)
+    high = jnp.where(r == 5, upper, jnp.where(r == 1, lower, 1)).astype(F32)
     return low, high
 
 
@@ -159,66 +195,113 @@
         yield j, net, total
 
 
-def first_kernel(
-    meta, plan, tab_k, tab_a, tab_n, own, zones, from_low, from_high,
-    h0, k1, kl1, kn1, ic1, g1, p1, q1, prm, zrel, spread,
-):
-    position, lower, upper = meta[0], meta[1], meta[2]
-    has_low, has_high = lower > 0, upper > 0
-    for row in range(2):
-        for j in range(TILES):
-            h0[row, j] = jnp.where(has_low, from_low[row * TILES + j], own[0, j])
-            h0[6 + row, j] = jnp.where(has_high, from_high[row * TILES + j], own[3, j])
-    h0[2:6] = own[...]
-    extra_low, extra_high = from_low[2 * TILES], from_high[2 * TILES]
-    z_low = jnp.where(has_low, extra_low[0:1, :], zones[0:1, :])
-    z_high = jnp.where(has_high, extra_high[0:1, :], zones[1:2, :])
+def own_kernel(tab_k, tab_a, tab_n, own, zones, k, kl, kn, ic, sl, sn, prm, near):
+    base = 8 * lax.axis_index("row") - 4
     sub = iota((SUB, WIDTH), 0)
-
-    def by_row(a, b, c, d):
-        return jnp.where(sub < 4, jnp.where(sub < 2, a, b), jnp.where(sub < 6, c, d))
-
-    zone = by_row(z_low, zones[0:1, :], zones[1:2, :], z_high).astype(jnp.int32)
-    base = 8 * position - 4
-    rel = (zone - base) & (ZONES - 1)
-    zrel[...] = rel
+    rel = (jnp.where(sub < 2, zones[0:1, :], zones[1:2, :]).astype(jnp.int32) - base) & (ZONES - 1)
     sat = jnp.ones((SUB, WIDTH), F32)
     alpha, n = sat, 2.0 * sat
+    lane = iota((SUB, 128), 1)
+    line = iota((SUB, 128), 0)
+    table = jnp.ones((SUB, 128), F32)
     for i in range(NEAR):
         at = (base + i) & (ZONES - 1)
         here = rel == i
         sat = jnp.where(here, tab_k[at], sat)
         alpha = jnp.where(here, tab_a[at], alpha)
         n = jnp.where(here, tab_n[at], n)
-    n1 = n - 1.0
+        column = jnp.where(line == 0, tab_k[at], jnp.where(line == 1, tab_a[at], tab_n[at]))
+        table = jnp.where(lane == i, column, table)
+    near[...] = table
+    for i, value in enumerate(derived(sat, alpha, n)):
+        for r in range(4):
+            prm[r, i : i + 1, :] = value[r : r + 1, :]
+
+    def cells(r, carry):
+        p = row_params(prm, r)
+        for j in range(TILES):
+            k[r, j], kl[r, j], kn[r, j], ic[r, j], sl[r, j], sn[r, j] = cell_math(own[r, j], p)
+        return carry
+
+    lax.fori_loop(0, 4, cells, 0)
+
+
+def first_kernel(
+    plan, near, own, zones, own_prm, k, kl, kn, ic, sl, sn, got_odd, got_even,
+    h0, k1, kl1, kn1, ic1, g1, p1, q1, prm, zrel, spread,
+):
+    position = lax.axis_index("row")
+    has_low, has_high = position > 0, position < lax.axis_size("row") - 1
+    odd = position % 2 == 1
+    for row in range(2):
+        for j in range(TILES):
+            at = row * TILES + j
+            one, other = got_odd[at], got_even[at]
+            h0[row, j] = jnp.where(has_low, jnp.where(odd, other, one), own[0, j])
+            h0[6 + row, j] = jnp.where(has_high, jnp.where(odd, one, other), own[3, j])
+    h0[2:6] = own[...]
+    for here, there in ((k, k1), (kl, kl1), (kn, kn1)):
+        there[2:6] = here[...]
+    ic1[1:5] = ic[...]
+    one, other = got_odd[2 * TILES], got_even[2 * TILES]
+    extra_low, extra_high = jnp.where(odd, other, one), jnp.where(odd, one, other)
+    z_low = jnp.where(has_low, extra_low[0:1, :], zones[0:1, :])
+    z_high = jnp.where(has_high, extra_high[0:1, :], zones[1:2, :])
+    sub = iota((SUB, WIDTH), 0)
+
+    def by_row(a, b, c, d):
+        return jnp.where(sub < 4, jnp.where(sub < 2, a, b), jnp.where(sub < 6, c, d))
+
+    zone = by_row(z_low, zones[0:1, :], zones[1:2, :], z_high).astype(jnp.int32)
+    rel = (zone - (8 * position - 4)) & (ZONES - 1)
+    zrel[...] = rel
+    ids = iota((32, WIDTH), 0)
+    sides = []
+    for r in (0, 7):
+        pick = (ids == rel[r : r + 1, :]).astype(F32).astype(jnp.bfloat16)
+        parts = [jnp.dot(x, pick, preferred_element_type=F32) for x in split3(near[:, :32])]
+        sides.append(parts[0] + (parts[1] + parts[2]))
+    sat, alpha, n = (
+        by_row(sides[0][i : i + 1, :], own_prm[0, i : i + 1, :], own_prm[2, i : i + 1, :], sides[1][i : i + 1, :])
+        for i in range(3)
+    )
     lev_0 = by_row(extra_low[1:2, :], plan[0, 0].astype(F32), plan[0, 1].astype(F32), extra_high[1:2, :])
     lev_1 = by_row(0.0, plan[1, 0].astype(F32), plan[1, 1].astype(F32), 0.0) + 0.0 * sat
-    made = (
-        sat, alpha, n, n1, 1.0 - 1.0 / n, 1.0 / (n * n), 1.0 / (WATER_RANGE * n1 * alpha), 1.0 / n1,
-        IRRIGATION * lev_0, IRRIGATION * lev_1, 1.0 / sat, 1.0 / alpha,
-    )
+    made = derived(sat, alpha, n) + (IRRIGATION * lev_0, IRRIGATION * lev_1, 1.0 / sat, 1.0 / alpha)
     for i, value in enumerate(made):
         for r in range(ROWS):
             prm[r, i : i + 1, :] = value[r : r + 1, :]
 
-    def cells(r, carry):
+    def outer(i, carry):
+        r = 7 * i
         p = row_params(prm, r)
         for j in range(TILES):
-            k1[r, j], kl1[r, j], kn1[r, j], ic1[r, j], p1[r, j], q1[r, j] = cell_math(h0[r, j], p)
-        return carry
-
-    lax.fori_loop(0, ROWS, cells, 0)
+            k1[r, j], kl1[r, j], kn1[r, j] = cell_math(h0[r, j], p, False)
+        return carry
+
+    def inner(i, carry):
+        r = 1 + 5 * i
+        p = row_params(prm, r)
+        for j in range(TILES):
+            values = cell_math(h0[r, j], p)
+            k1[r, j], kl1[r, j], kn1[r, j], ic1[r - 1, j], p1[r - 1, j], q1[r - 1, j] = values
+        return carry
+
+    lax.fori_loop(0, 2, outer, 0)
+    lax.fori_loop(0, 2, inner, 0)
+    p1[1:5] = sl[...]
+    q1[1:5] = sn[...]
 
     def flow(r, most):
-        low, high = row_open(meta, r)
+        low, high = row_open(position, r)
         is_own = jnp.logical_and(r >= 2, r <= 5)
-        real = jnp.logical_or(is_own, jnp.where(r < 2, has_low, has_high))
+        real = jnp.logical_or(is_own, jnp.logical_or(jnp.logical_and(r < 2, has_low), jnp.logical_and(r > 5, has_high)))
         for j, net, total in net_row(h0, k1, r, prm[r, LEV0 : LEV0 + 1, :], low, high):
-            ic = ic1[r, j]
+            ic = ic1[r - 1, j]
             g = jnp.where(real, net * ic, 0.0)
-            g1[r, j] = g
-            p1[r, j] = g * p1[r, j]
-            q1[r, j] = g * q1[r, j]
+            g1[r - 1, j] = g
+            p1[r - 1, j] = g * p1[r - 1, j]
+            q1[r - 1, j] = g * q1[r - 1, j]
             most = jnp.maximum(most, jnp.where(is_own, total * ic, 0.0))
         return most
 
@@ -229,36 +312,47 @@
 
 
 def second_kernel(
-    meta, rates, sensors, h0, k1, kl1, kn1, ic1, g1, p1, q1, prm, zrel,
+    rates, cells_at, goals, h0, k1, kl1, kn1, ic1, g1, p1, q1, prm, zrel,
     h1_out, g2, spread,
     h1, k2, kl2, kn2, ic2, sl2, sn2, va, vb, wa, wb, w0, w1, w2, maps,
 ):
+    position = lax.axis_index("row")
     size = CFL / jnp.max(rates[...])
     nothing = jnp.zeros((TILES, SUB, WIDTH), F32)
     for r in (0, ROWS - 1):
-        for ref in (h1, k2, w0, w1, w2):
+        for ref in (w0, w1, w2):
             ref[r] = nothing
     for r in (1, 6):
-        for ref in (va, vb, wa, wb):
+        for ref in (wa, wb):
             ref[r] = nothing
-    maps[...] = jnp.zeros(maps.shape, F32)
 
     def cells(r, carry):
         p = row_params(prm, r)
         for j in range(TILES):
-            head = h0[r, j] + size * g1[r, j]
+            head = h0[r, j] + size * g1[r - 1, j]
             h1[r, j] = head
-            k2[r, j], kl2[r, j], kn2[r, j], ic2[r, j], sl2[r, j], sn2[r, j] = cell_math(head, p)
-        return carry
-
-    lax.fori_loop(1, 7, cells, 0)
+            h1_out[r - 2, j] = head
+            values = cell_math(head, p)
+            k2[r, j], kl2[r, j], kn2[r, j], ic2[r - 2, j], sl2[r - 2, j], sn2[r - 2, j] = values
+        return carry
+
+    def edge_cells(i, carry):
+        r = 1 + 5 * i
+        p = row_params(prm, r)
+        for j in range(TILES):
+            head = h0[r, j] + size * g1[r - 1, j]
+            h1[r, j] = head
+            k2[r, j], kl2[r, j], kn2[r, j] = cell_math(head, p, False)
+        return carry
+
+    lax.fori_loop(0, 2, edge_cells, 0)
+    lax.fori_loop(2, 6, cells, 0)
 
     def flow(r, most):
-        low, high = row_open(meta, r)
+        low, high = row_open(position, r)
         for j, net, total in net_row(h1, k2, r, prm[r, LEV1 : LEV1 + 1, :], low, high):
-            ic = ic2[r, j]
+            ic = ic2[r - 2, j]
             g2[r - 2, j] = net * ic
-            h1_out[r - 2, j] = h1[r, j]
             most = jnp.maximum(most, total * ic)
         return most
 
@@ -271,8 +365,9 @@
         block = jnp.floor((depth + 0.5) * (1.0 / TILES))
         return (line - 4.0 * depth) * 48.0 + (depth - TILES * block) * 8.0 + block, column
 
-    count = sensors.shape[1]
-    wide = sensors[...]
+    count = cells_at.shape[1]
+    line_of = iota((SUB, count), 0)
+    wide = jnp.where(line_of == 0, cells_at[...].astype(F32), goals[...])
     tall = jnp.transpose(wide)
     line_wide = places(wide[0:1, :])[0].astype(jnp.int32)
     line_tall, column_tall = places(tall[:, 0:1])
@@ -291,23 +386,66 @@
         jnp.sum(diff * seen_g) * (1.0 / events),
         jnp.sum(seen_g * seen_g) * (0.5 / events),
     )
-    va[2:6] = exact_dot(put, jnp.where(column, diff * (1.0 / events), 0.0)).reshape(OWN)
-    vb[2:6] = exact_dot(put, jnp.where(column, seen_g * (1.0 / events), 0.0)).reshape(OWN)
+    va[...] = exact_dot(put, jnp.where(column, diff * (1.0 / events), 0.0)).reshape(OWN)
+    vb[...] = exact_dot(put, jnp.where(column, seen_g * (1.0 / events), 0.0)).reshape(OWN)
 
     def scaled(r, carry):
         for j in range(TILES):
-            ic = ic2[r, j]
-            wa[r, j] = va[r, j] * ic
-            wb[r, j] = vb[r, j] * ic
+            ic = ic2[r - 2, j]
+            wa[r, j] = va[r - 2, j] * ic
+            wb[r, j] = vb[r - 2, j] * ic
         return carry
 
     lax.fori_loop(2, 6, scaled, 0)
     last, is_top, is_bottom = masks()
 
+    def store_two(r, sums):
+        flat = [jnp.sum(x, 0, keepdims=True) for x in sums]
+        for q in range(3):
+            of_a, of_b = flat[q], flat[3 + q]
+            rows = [size * of_a, of_a + size * of_b, of_b]
+            for c in range(3):
+                if q > 0:
+                    rows[c] = rows[c] - size * flat[6 + 2 * c + q - 1]
+                maps[r, 4 * q + c : 4 * q + c + 1, :] = rows[c]
+
+    def store_heads(r, j, back, sums):
+        (v_a, j_a), (v_b, j_b) = back
+        us = (v_a + size * j_a, v_b + j_a + size * j_b, j_b)
+        ic, pp, qq = ic1[r - 1, j], p1[r - 1, j], q1[r - 1, j]
+        for i, (u, w_ref) in enumerate(zip(us, (w0, w1, w2))):
+            w_ref[r, j] = u * ic
+            sums[6 + 2 * i] += u * pp
+            sums[7 + 2 * i] += u * qq
+
+    def edge_two(i, carry):
+        r = 1 + 5 * i
+        near = 2 + 3 * i
+        low, high = row_open(position, r)
+        is_open = jnp.where(i == 0, high, low)
+        sums = [jnp.zeros((SUB, WIDTH), F32) for _ in range(12)]
+        for j in range(TILES):
+            hj = h1[r, j]
+            half = (0.5 * is_open) * (h1[near, j] - hj)
+            kd = (0.5 * is_open) * (k2[near, j] + k2[r, j])
+            kj, kl, kn = k2[r, j], kl2[r, j], kn2[r, j]
+            inv_h = 1.0 / hj
+            back = []
+            for part, w_ref in enumerate((wa, wb)):
+                w = w_ref[near, j]
+                gk, gh = -half * w, kd * w
+                to_l = gk * kl
+                sums[3 * part] += gk * kj
+                sums[3 * part + 1] += to_l
+                sums[3 * part + 2] += gk * kn
+                back.append((0.0, gh + to_l * inv_h))
+            store_heads(r, j, back, sums)
+        store_two(r, sums)
+        return carry
+
     def back_two(r, carry):
-        low, high = row_open(meta, r)
+        low, high = row_open(position, r)
         top = prm[r, LEV1 : LEV1 + 1, :]
-        own = jnp.logical_and(r >= 2, r <= 5)
         hs = [h1[r, j] for j in range(TILES)]
         ks = [k2[r, j] for j in range(TILES)]
         sums = [jnp.zeros((SUB, WIDTH), F32) for _ in range(12)]
@@ -338,15 +476,14 @@
         for j in range(TILES):
             below = final if j == TILES - 1 else face(j)
             hj, kj = hs[j], ks[j]
-            h_low, h_high = h1[r - 1, j], h1[r + 1, j]
             half_c = jnp.where(last, 0.0, 0.5 * (lanes_left(hj) - hj))
             kf = jnp.where(last, 0.0, 0.5 * (lanes_left(kj) + kj))
-            half_l, half_h = 0.5 * low * (h_low - hj), 0.5 * high * (h_high - hj)
-            k_low, k_high = 0.5 * low * (k2[r - 1, j] + kj), 0.5 * high * (k2[r + 1, j] + kj)
+            half_l, half_h = (0.5 * low) * (h1[r - 1, j] - hj), (0.5 * high) * (h1[r + 1, j] - hj)
+            k_low, k_high = (0.5 * low) * (k2[r - 1, j] + kj), (0.5 * high) * (k2[r + 1, j] + kj)
             kl, kn = kl2[r, j], kn2[r, j]
             inv_h = 1.0 / hj
-            g = jnp.where(own, g2[jnp.clip(r - 2, 0, 3), j], 0.0)
-            gl, gn = g * sl2[r, j], g * sn2[r, j]
+            g = g2[r - 2, j]
+            gl, gn = g * sl2[r - 2, j], g * sn2[r - 2, j]
             back = []
             for part, (w_ref, v_ref) in enumerate(((wa, va), (wb, vb))):
                 w = ws[part][j]
@@ -357,41 +494,51 @@
                 gk = gk + half_l * d_low + half_h * d_high
                 gh = lanes_right(f) - f + below[part][1] - above[part][1]
                 gh = gh - k_low * d_low - k_high * d_high
-                v = v_ref[r, j]
+                v = v_ref[r - 2, j]
                 to_l = gk * kl - v * gl
                 sums[3 * part] += gk * kj
                 sums[3 * part + 1] += to_l
                 sums[3 * part + 2] += gk * kn - v * gn
                 back.append((v, gh + (to_l + v * g) * inv_h))
-            (v_a, j_a), (v_b, j_b) = back
-            us = (v_a + size * j_a, v_b + j_a + size * j_b, j_b)
-            ic, pp, qq = ic1[r, j], p1[r, j], q1[r, j]
-            for i, (u, w_ref) in enumerate(zip(us, (w0, w1, w2))):
-                w_ref[r, j] = u * ic
-                sums[6 + 2 * i] -= u * pp
-                sums[7 + 2 * i] -= u * qq
+            store_heads(r, j, back, sums)
             above = below
-        flat = [jnp.sum(x, 0, keepdims=True) for x in sums]
+        store_two(r, sums)
+        return carry
+
+    lax.fori_loop(0, 2, edge_two, 0)
+    lax.fori_loop(2, 6, back_two, 0)
+
+    refs = (w0, w1, w2)
+
+    def store_one(r, sums, first):
+        inv_k, inv_a = prm[r, IKS : IKS + 1, :], prm[r, IAL : IAL + 1, :]
         for q in range(3):
-            of_a, of_b = flat[q], flat[3 + q]
-            rows = [size * of_a, of_a + size * of_b, of_b]
             for c in range(3):
-                if q > 0:
-                    rows[c] = rows[c] + size * flat[6 + 2 * c + q - 1]
-                maps[r, 4 * q + c : 4 * q + c + 1, :] = rows[c]
-        return carry
-
-    for ref in (wa, wb):
-        ref[0] = nothing
-        ref[7] = nothing
-    lax.fori_loop(1, 7, back_two, 0)
+                at = 4 * q + c
+                row = size * jnp.sum(sums[3 * c + q], 0, keepdims=True)
+                if not first:
+                    row = row + maps[r, at : at + 1, :]
+                maps[r, at : at + 1, :] = row if q == 2 else row * (inv_k if q == 0 else inv_a)
+
+    def edge_one(i, carry):
+        r = 7 * i
+        near = 1 + 5 * i
+        sums = [jnp.zeros((SUB, WIDTH), F32) for _ in range(9)]
+        for j in range(TILES):
+            half = 0.5 * (h0[r, j] - h0[near, j])
+            kj, kl, kn = k1[r, j], kl1[r, j], kn1[r, j]
+            for part, w_ref in enumerate(refs):
+                gk = half * w_ref[near, j]
+                sums[3 * part] += gk * kj
+                sums[3 * part + 1] += gk * kl
+                sums[3 * part + 2] += gk * kn
+        store_one(r, sums, True)
+        return carry
 
     def back_one(r, carry):
-        low, high = row_open(meta, r)
+        low, high = row_open(position, r)
         top = prm[r, LEV0 : LEV0 + 1, :]
-        before, after = jnp.maximum(r - 1, 0), jnp.minimum(r + 1, ROWS - 1)
         hs = [h0[r, j] for j in range(TILES)]
-        refs = (w0, w1, w2)
         ws = [[w[r, j] for j in range(TILES)] for w in refs]
         sums = [jnp.zeros((SUB, WIDTH), F32) for _ in range(9)]
 
@@ -408,27 +555,27 @@
             below = final if j == TILES - 1 else face(j)
             hj = hs[j]
             half_c = jnp.where(last, 0.0, 0.5 * (lanes_left(hj) - hj))
-            half_l = 0.5 * low * (h0[before, j] - hj)
-            half_h = 0.5 * high * (h0[after, j] - hj)
+            half_l = (0.5 * low) * (h0[r - 1, j] - hj)
+            half_h = (0.5 * high) * (h0[r + 1, j] - hj)
             kj, kl, kn = k1[r, j], kl1[r, j], kn1[r, j]
             for part, w_ref in enumerate(refs):
                 w = ws[part][j]
                 e = half_c * (w - lanes_left(w))
                 gk = e + lanes_right(e) + below[part] + above[part]
-                gk = gk + half_l * (w - w_ref[before, j]) + half_h * (w - w_ref[after, j])
+                gk = gk + half_l * (w - w_ref[r - 1, j]) + half_h * (w - w_ref[r + 1, j])
                 sums[3 * part] += gk * kj
                 sums[3 * part + 1] += gk * kl
                 sums[3 * part + 2] += gk * kn
             above = below
-        inv_k, inv_a = prm[r, IKS : IKS + 1, :], prm[r, IAL : IAL + 1, :]
-        for q in range(3):
-            for c in range(3):
-                at = 4 * q + c
-                row = maps[r, at : at + 1, :] + size * jnp.sum(sums[3 * c + q], 0, keepdims=True)
-                maps[r, at : at + 1, :] = row if q == 2 else row * (inv_k if q == 0 else inv_a)
-        return carry
-
-    lax.fori_loop(0, ROWS, back_one, 0)
+        store_one(r, sums, False)
+        return carry
+
+    for r in range(ROWS):
+        for at in (3, 7, 11):
+            maps[r, at : at + 1, :] = jnp.zeros((1, WIDTH), F32)
+        maps[r, 12:16, :] = jnp.zeros((4, WIDTH), F32)
+    lax.fori_loop(0, 2, edge_one, 0)
+    lax.fori_loop(1, 7, back_one, 0)
 
     left = jnp.concatenate([maps[r] for r in range(ROWS)], 1)
     near = zrel[...]
@@ -470,7 +617,7 @@
     spread[...] = jnp.broadcast_to(total[None], spread.shape)
 
 
-def last_kernel(meta, parts, h1, g2, final, grad_k, grad_a, grad_n, misfit, rates):
+def last_kernel(parts, h1, g2, final, grad_k, grad_a, grad_n, misfit, rates):
     sub = iota((SUB, 256), 0)
     power = sub % 4
     sums = [jnp.zeros((SUB, 256), F32) for _ in range(4)]
@@ -496,8 +643,9 @@
             total = total + pltpu.roll(jnp.where(lane < 84, field, 0.0), (64 * y - 4) % 256, 1)
         out[...] = total
     misfit[0, 0] = jnp.sum(jnp.where(lane == 252, rows[0] + rows[1] + rows[2] + rows[3], 0.0))
-    mine = rates[meta[3]]
-    size = jnp.where(meta[4] == 0, mine[3:4, :128], mine[7:8, :128])
+    _, pair, z_hi = axes()
+    mine = rates[pair]
+    size = jnp.where(z_hi == 0, mine[3:4, :128], mine[7:8, :128])
     size = jnp.concatenate([size, size, size], 1)
     for j in range(TILES):
         for row in range(4):
@@ -510,16 +658,16 @@
 SMEM = pl.BlockSpec(memory_space=pltpu.SMEM)
 
 
-def call(kernel, name, ins, outs, out_specs=None, scratch=()):
-    out_shape = [jax.ShapeDtypeStruct(*o) if isinstance(o, tuple) else o for o in outs]
+def call(kernel, name, ins, outs, out_specs=None, scratch=(), cost=None):
     return pl.pallas_call(
         kernel,
         name=name,
         in_specs=ins,
         out_specs=out_specs or [VMEM] * len(outs),
-        out_shape=out_shape,
+        out_shape=[jax.ShapeDtypeStruct(shape, dtype) for shape, dtype in outs],
         scratch_shapes=scratch,
-        compiler_params=pltpu.CompilerParams(vmem_limit_bytes=48 * 1024 * 1024),
+        cost_estimate=cost,
+        compiler_params=pltpu.CompilerParams(vmem_limit_bytes=32 * 1024 * 1024),
     )
 
 
@@ -533,49 +681,54 @@
     tensiometer_cells,
     tensiometer_heads,
 ):
-    position = lax.axis_index("row")
     count = lax.axis_size("row")
-    event = lax.axis_index("event")
-    meta = jnp.stack(
-        [
-            position,
-            (position > 0).astype(jnp.int32),
-            (position < count - 1).astype(jnp.int32),
-            event // 4 * 2 + event % 2,
-            event // 2 % 2,
-        ]
-    )
     plan = forcing_plan[0]
     edge = (2 * TILES + 1, SUB, WIDTH)
-    own, up, down, zones = call(
+    own, send_odd, send_even, zones = call(
         pack_kernel,
         "pack_edges",
-        [VMEM, VMEM, SMEM],
+        [pl.BlockSpec(memory_space=pl.ANY)] * 3,
         [(OWN, F32), (edge, F32), (edge, F32), ((2, WIDTH), F32)],
+        scratch=[
+            pltpu.VMEM((48, 4, WIDTH), F32),
+            pltpu.VMEM((2, 192), jnp.int32),
+            pltpu.VMEM((2, 2), jnp.int32),
+            pltpu.SemaphoreType.DMA((3,)),
+        ],
     )(initial_head[0], zone_map, plan)
-    upward = [(i, i + 1) for i in range(count - 1)]
-    from_low = lax.ppermute(up, "row", upward)
-    from_high = lax.ppermute(down, "row", [(j, i) for i, j in upward])
+    odd = [(i, i + 1) for i in range(1, count - 1, 2)]
+    even = [(i, i + 1) for i in range(0, count, 2)]
+    got_odd = lax.ppermute(send_odd, "row", odd + [(j, i) for i, j in odd])
+    got_even = lax.ppermute(send_even, "row", even + [(j, i) for i, j in even])
+    own_fields = call(
+        own_kernel,
+        "own_cells",
+        [SMEM] * 3 + [VMEM] * 2,
+        [(OWN, F32)] * 6 + [((4, 16, WIDTH), F32), ((SUB, 128), F32)],
+        cost=pl.CostEstimate(flops=100_000_000, bytes_accessed=8_000_000, transcendentals=600_000),
+    )(sat_conductivity, vg_alpha, vg_n, own, zones)
+    own_prm, near = own_fields[6:]
+    wide = (6, TILES, SUB, WIDTH)
     first = call(
         first_kernel,
         "first_step",
-        [SMEM] * 5 + [VMEM] * 4,
-        [(FIELD, F32)] * 8
+        [SMEM] + [VMEM] * 12,
+        [(FIELD, F32)] * 4
+        + [(wide, F32)] * 4
         + [((ROWS, 16, WIDTH), F32), ((ROWS, WIDTH), jnp.int32), ((32, 1, 128), F32)],
-    )(meta, plan, sat_conductivity, vg_alpha, vg_n, own, zones, from_low, from_high)
+    )(plan, near, own, zones, own_prm, *own_fields[:6], got_odd, got_even)
     fields, rates = first[:-1], first[-1]
     rates = lax.all_to_all(rates, "row", 0, 0, tiled=True)
-    sensors = jnp.concatenate(
-        [tensiometer_cells.astype(F32), tensiometer_heads, jnp.zeros((6, 256), F32)], 0
-    )
-    scratch = [pltpu.VMEM(FIELD, F32)] * 14 + [pltpu.VMEM((ROWS, 16, WIDTH), F32)]
     h1, g2, sums = call(
         second_kernel,
         "second_step_and_adjoint",
-        [SMEM] + [VMEM] * 12,
+        [VMEM] * 13,
         [(OWN, F32), (OWN, F32), ((16, 4, 128), F32)],
-        scratch=scratch,
-    )(meta, rates, sensors, *fields)
+        scratch=[pltpu.VMEM(FIELD, F32)] * 4
+        + [pltpu.VMEM(OWN, F32)] * 5
+        + [pltpu.VMEM(FIELD, F32)] * 5
+        + [pltpu.VMEM((ROWS, 16, WIDTH), F32)],
+    )(rates, tensiometer_cells, tensiometer_heads, *fields)
     sums = lax.all_to_all(sums, ("event", "row"), 0, 0, tiled=True, axis_index_groups=RINGS)
     (sums,) = call(ring_kernel, "ring_sums", [VMEM], [((32, SUB, 256), F32)])(sums)
     sums = lax.all_to_all(sums, ("event", "row"), 0, 0, tiled=True, axis_index_groups=PLANES)
@@ -583,11 +736,11 @@
     final, grad_k, grad_a, grad_n, misfit = call(
         last_kernel,
         "final_head_and_sums",
-        [SMEM, VMEM, VMEM, VMEM],
+        [VMEM, VMEM, VMEM],
         [((48, 4, WIDTH), F32), row, row, row, ((1, 1), F32)],
         [VMEM] * 4 + [SMEM],
         scratch=[pltpu.VMEM((8, SUB, 256), F32)],
-    )(meta, sums, h1, g2)
+    )(sums, h1, g2)
     return (final[None], misfit[0, 0], grad_k[0], grad_a[0], grad_n[0])
 
 

time: 119 us -> 97.3 us (0.82)
  blocking collectives: 42.1 us -> 70.5 us
  starting transfers between devices: 27.5 us -> 7.92 us
  local copies, waits for them, and re-layouts: 17.7 us -> 2.99 us
  waiting for transfers between devices: 12.2 us -> 0.68 us
  other arithmetic: 1.92 us -> 0 us
  Pallas kernels: 16 us -> 14.1 us
    all_to_all x0 -> x1, blocking collectives: none -> 31 us  [local(): rates = lax.all_to_all(rates, 'row', 0, 0, tiled=True)]
    all_to_all x1 -> x0, starting transfers between devices: 21.8 us -> none  [local(): rates = lax.all_to_all(rates, 'row', 0, 0, tiled=True)]
    unnamed x50 -> x16, local copies, waits for them, and re-layouts: 17 us -> 2.99 us
    all_to_all x1 -> x0, waiting for transfers between devices: 9.98 us -> none  [local(): rates = lax.all_to_all(rates, 'row', 0, 0, tiled=True)]
    all_to_all x2, blocking collectives: 42.1 us -> 39.5 us  [local(): lax.all_to_all(sums, ('event', 'row'), 0, 0, tiled=True, axis_index_group...]
    ppermute x2, starting transfers between devices: 5.66 us -> 7.92 us  [the longest x1 7.25 us: local(): got_even = lax.ppermute(send_even, 'row', even + [(j, i) for i, j in even])]
    pallas_call x4 -> x5, Pallas kernels: 15.8 us -> 14 us  [the longest x1 8.54 us: local(): call(second_kernel, 'second_step_and_adjoint', [VMEM] * 13, [(OWN, F32),...]
    ppermute x2, waiting for transfers between devices: 2.24 us -> 0.68 us  [the longest x1 0.68 us: local(): got_even = lax.ppermute(send_even, 'row', even + [(j, i) for i, j in even])]
  transfers between devices with their start and end apart: 3 -> 2, of which waited for: 2 -> 1; matrix products, arithmetic and copies ran while one was open for 2% -> 0% of each run, Pallas kernels for 0% -> 1%
where the time goes in v1:
time: 97.3 us; the launch traced here: 97 us
  blocking collectives  70.5 us (72%)
  Pallas kernels  14.1 us (14%)
  starting transfers between devices  7.92 us (8%)
  local copies, waits for them, and re-layouts  2.99 us (3%)
    all_to_all x2, blocking collectives, local(): lax.all_to_all(sums, ('event', 'row'), 0, 0, tiled=True, axis_index_group...  39.5 us
    all_to_all x1, blocking collectives, local(): rates = lax.all_to_all(rates, 'row', 0, 0, tiled=True)  31 us
    pallas_call x1, Pallas kernels, local(): call(second_kernel, 'second_step_and_adjoint', [VMEM] * 13, [(OWN, F32),...  8.54 us
    ppermute x1, starting transfers between devices, local(): got_even = lax.ppermute(send_even, 'row', even + [(j, i) for i, j in even])  7.25 us
    unnamed x16, local copies, waits for them, and re-layouts  2.99 us
    pallas_call x1, Pallas kernels, local(): call(first_kernel, 'first_step', [SMEM] + [VMEM] * 12, [(FIELD, F32)] * 4...  2.79 us
  transfers between devices with their start and end apart: 2, of which 1 were waited for; matrix products, arithmetic and copies ran while one was open for 0% of the time, Pallas kernels for 1%

profile of v1, /device:TPU:1, one launch (start us, length us, event | category | flops | bytes accessed | tf_op | source)
XLA Modules:
  0.0 97.0 jit_solution(14691660263041567811)
XLA Ops:
  0.6 0.0 copy-start.2
  0.6 0.0 copy-start.1
  0.7 0.7 copy-done.2
  1.3 0.0 copy-done.1
  1.3 1.0 copy-done
  2.3 0.4 pack_edges.1
  2.7 0.7 collective-permute-start
  3.4 0.0 copy-start.6
  3.4 0.0 copy-start.7
  3.4 7.2 %collective-permute-start.1 = (f32[13,8,384]{2,1,0:T(8,128)S(1)}, f32[13,8,384]{2,1,0:T(8,128)S(1)}, u32[]{:S(2)}, u32[]{:S(2)}) collective-permute-start(f32[13,8,384]{2,1,0:T(8,128)S(1)} %get-tuple-element.47), channel_id=1, source_target_pairs={{0,1},{2,3},{4,5},{6,7},{8,9},{10,11},{12,13},{14,15},{16,17},{18,... | collective-permute-start | bytes 479240 | tf_op jit(solution)/shard_map/ppermute | solution.py:702
  10.7 0.0 copy-start.5
  10.7 0.7 copy-done.5
  11.4 1.3 %own_cells.1 = (f32[4,6,8,384]{3,2,1,0:T(8,128)S(1)}, f32[4,6,8,384]{3,2,1,0:T(8,128)S(1)}, f32[4,6,8,384]{3,2,1,0:T(8,128)S(1)}, f32[4,6,8,384]{3,2,1,0:T(8,128...) custom-call(f32[256]{0:T(256)S(1)} %copy-done.5, ...), custom_call_target="tpu_custom_call" | custom-call | flops 100000000 | bytes 8000000 | tf_op jit(solution)/shard_map/own_cells/pallas_call | solution.py:703
  12.7 0.0 collective-permute-done.got_odd
  12.7 0.7 collective-permute-done.1.got_even
  13.4 2.8 %first_step.1 = (f32[8,6,8,384]{3,2,1,0:T(8,128)S(1)}, f32[8,6,8,384]{3,2,1,0:T(8,128)S(1)}, f32[8,6,8,384]{3,2,1,0:T(8,128)S(1)}, f32[8,6,8,384]{3,2,1,0:T(8,12...) custom-call(s32[2,2]{1,0:T(2,128)S(1)} %bitcast.9, ...), custom_call_target="tpu_custom_call" | custom-call | tf_op jit(solution)/shard_map/first_step/pallas_call | solution.py:712
  16.2 0.0 copy-start.4
  16.2 31.0 %all_to_all.15.rates = f32[32,1,128]{2,1,0:T(1,128)S(1)} all-to-all(f32[32,1,128]{2,1,0:T(1,128)S(1)} %get-tuple-element.48), channel_id=1, replica_groups=mesh['event'=16,'row'=32] {'row'}, dimensions={0} | all-to-all | bytes 32768 | tf_op jit(solution)/shard_map/all_to_all | solution.py:721
  47.1 0.7 copy-done.3
  47.8 8.5 %second_step_and_adjoint.1 = (f32[4,6,8,384]{3,2,1,0:T(8,128)S(1)}, f32[4,6,8,384]{3,2,1,0:T(8,128)S(1)}, f32[16,4,128]{2,1,0:T(4,128)S(1)}) custom-call(f32[32,1,128]{2,1,0:T(1,128)S(1)} %all_to_all.15.rates, s32[1,256]{1,0:T(1,128)S(1)} %copy-done.3, f32[1,256]{1,0:T(1,128)S(1)} %copy-done.4, f32[8,6,8,384]{3,2,1,0:T(8,128)S(1)} %get-tuple-element.49.h0, ...), custom_call_target="tpu_custom_call" | custom-call | tf_op jit(solution)/shard_map/second_step_and_adjoint/pallas_call | solution.py:722
  56.4 22.4 %all_to_all.16.parts = f32[16,4,128]{2,1,0:T(4,128)S(1)} all-to-all(f32[16,4,128]{2,1,0:T(4,128)S(1)} %get-tuple-element.59), channel_id=1, replica_groups={{0,1,2,3,4,5,6,7,64,65,66,67,68,69,70,71},{8,9,10,11,12,13,14,15,72,73,..., dimensions={0} | all-to-all | bytes 65536 | tf_op jit(solution)/shard_map/all_to_all | solution.py:732
  78.7 0.1 ring_sums.1
  78.8 17.2 %all_to_all.17.parts = f32[32,8,256]{2,1,0:T(8,128)S(1)} all-to-all(f32[32,8,256]{2,1,0:T(8,128)S(1)} %ring_sums.1), channel_id=1, replica_groups={{0,32,128,160,256,288,384,416,8,40,136,168,264,296,392,424,16,48,144,17..., dimensions={0} | all-to-all | bytes 524288 | tf_op jit(solution)/shard_map/all_to_all | solution.py:734
  96.0 1.0 final_head_and_sums.1
  (5 shorter events, 0.0 us)
Async XLA Ops:
  0.6 0.7 copy-start.2
  0.6 0.7 copy-start.1
  1.3 1.0 copy-start
  2.7 9.9 %collective-permute-start = (f32[13,8,384]{2,1,0:T(8,128)S(1)}, f32[13,8,384]{2,1,0:T(8,128)S(1)}, u32[]{:S(2)}, u32[]{:S(2)}) collective-permute-start(f32[13,8,384]{2,1,0:T(8,128)S(1)} %get-tuple-element.46), channel_id=1, source_target_pairs={{1,2},{3,4},{5,6},{7,8},{9,10},{11,12},{13,14},{15,16},{17,18},{19... | collective-permute-start | bytes 479240 | tf_op jit(solution)/shard_map/ppermute | solution.py:701
  3.4 7.3 %copy-start.6 = (f32[256]{0:T(256)S(1)}, f32[256]{0:T(256)}, u32[]{:S(2)}) copy-start(f32[256]{0:T(256)} %tab_a.1) | copy-start | bytes 3076
  3.4 7.3 %copy-start.7 = (f32[256]{0:T(256)S(1)}, f32[256]{0:T(256)}, u32[]{:S(2)}) copy-start(f32[256]{0:T(256)} %tab_n.1) | copy-start | bytes 3076
  3.4 9.9 %collective-permute-start.1 = (f32[13,8,384]{2,1,0:T(8,128)S(1)}, f32[13,8,384]{2,1,0:T(8,128)S(1)}, u32[]{:S(2)}, u32[]{:S(2)}) collective-permute-start(f32[13,8,384]{2,1,0:T(8,128)S(1)} %get-tuple-element.47), channel_id=1, source_target_pairs={{0,1},{2,3},{4,5},{6,7},{8,9},{10,11},{12,13},{14,15},{16,17},{18,... | collective-permute-start | bytes 479240 | tf_op jit(solution)/shard_map/ppermute | solution.py:702
  10.7 0.7 copy-start.5
  16.2 31.0 %copy-start.4 = (f32[1,256]{1,0:T(1,128)S(1)}, f32[1,256]{1,0:T(1,128)}, u32[]{:S(2)}) copy-start(f32[1,256]{1,0:T(1,128)} %goals.1) | copy-start | bytes 3076
  47.1 0.7 copy-start.3

commit v2 on v1

--- a/solution.py
+++ b/solution.py
@@ -75,7 +75,7 @@
     return lax.axis_index("row"), event // 4 * 2 + event % 2, event // 2 % 2
 
 
-def pack_kernel(head_in, zone_in, plan_in, own, send_odd, send_even, zones, head, zone, plan, sems):
+def pack_kernel(head_in, zone_in, plan_in, h0, send_odd, send_even, zones, head, zone, plan, sems):
     copies = [
         pltpu.make_async_copy(src, dst, sems.at[i])
         for i, (src, dst) in enumerate(((head_in, head), (zone_in, zone), (plan_in, plan)))
@@ -93,13 +93,13 @@
         block = head[depth]
         j, s = depth % TILES, depth // TILES
         for row in range(4):
-            own[row, j, s : s + 1, :] = block[row : row + 1, :]
+            h0[2 + row, j, s : s + 1, :] = block[row : row + 1, :]
     sub = iota((SUB, WIDTH), 0)
     odd = lax.axis_index("row") % 2 == 1
 
     def fill(out, pair):
-        out[0:TILES] = own[2 * pair]
-        out[TILES : 2 * TILES] = own[2 * pair + 1]
+        out[0:TILES] = h0[2 + 2 * pair]
+        out[TILES : 2 * TILES] = h0[3 + 2 * pair]
         out[2 * TILES] = jnp.where(sub == 0, blocks[pair : pair + 1, :], level[0:1, pair : pair + 1])
 
     @pl.when(odd)
@@ -141,7 +141,7 @@
 def derived(sat, alpha, n):
     n1 = n - 1.0
     return (
-        sat, alpha, n, n1, 1.0 - 1.0 / n, 1.0 / (n * n), 1.0 / (WATER_RANGE * n1 * alpha), 1.0 / n1,
+        sat, alpha, n, n1, 1.0 - 1.0 / n, 1.0 / (n * n), 0.5 / (WATER_RANGE * n1 * alpha), 1.0 / n1,
     )
 
 
@@ -155,47 +155,51 @@
     return last, sub == 0, sub == SUB - 1
 
 
-def row_open(position, r):
-    lower = (position > 0).astype(jnp.int32)
-    upper = (position < lax.axis_size("row") - 1).astype(jnp.int32)
-    low = jnp.where(r == 2, lower, jnp.where(r == 6, upper, 1)).astype(F32)
-    high = jnp.where(r == 5, upper, jnp.where(r == 1, lower, 1)).astype(F32)
-    return low, high
-
-
-def net_row(h, k, r, top, low, high):
+def net_row(h, k, r, top, beside):
     last, is_top, is_bottom = masks()
     hs = [h[r, j] for j in range(TILES)]
     ks = [k[r, j] for j in range(TILES)]
 
     def face(j):
         if j < TILES - 1:
-            kd = 0.5 * (ks[j] + ks[j + 1])
+            kd = ks[j] + ks[j + 1]
             return kd, kd * (1.0 + hs[j] - hs[j + 1])
-        kd = 0.5 * (ks[j] + subs_up(ks[0]))
+        kd = ks[j] + subs_up(ks[0])
         flow = kd * (1.0 + hs[j] - subs_up(hs[0]))
-        return jnp.where(is_bottom, ks[j], kd), jnp.where(is_bottom, ks[j], flow)
+        return jnp.where(is_bottom, 2.0 * ks[j], kd), jnp.where(is_bottom, 2.0 * ks[j], flow)
 
     final = face(TILES - 1)
     above = (
-        jnp.where(is_top, ks[0], subs_down(final[0])),
+        jnp.where(is_top, 2.0 * ks[0], subs_down(final[0])),
         jnp.where(is_top, top * ks[0], subs_down(final[1])),
     )
     for j in range(TILES):
         below = final if j == TILES - 1 else face(j)
         hj, kj = hs[j], ks[j]
-        kf = jnp.where(last, 0.0, 0.5 * (kj + lanes_left(kj)))
+        kf = jnp.where(last, 0.0, kj + lanes_left(kj))
         flow = kf * (lanes_left(hj) - hj)
-        k_low = 0.5 * low * (k[r - 1, j] + kj)
-        k_high = 0.5 * high * (k[r + 1, j] + kj)
         net = flow - lanes_right(flow) + above[1] - below[1]
-        net = net + k_low * (h[r - 1, j] - hj) + k_high * (h[r + 1, j] - hj)
-        total = kf + lanes_right(kf) + above[0] + below[0] + k_low + k_high
+        total = kf + lanes_right(kf) + above[0] + below[0]
+        for other in beside:
+            kx = k[other, j] + kj
+            net = net + kx * (h[other, j] - hj)
+            total = total + kx
         above = below
         yield j, net, total
 
 
-def own_kernel(tab_k, tab_a, tab_n, own, zones, k, kl, kn, ic, sl, sn, prm, near):
+def places(cell):
+    line = jnp.floor((cell + 0.5) * (1.0 / WIDTH))
+    column = cell - WIDTH * line
+    depth = jnp.floor((line + 0.5) * 0.25)
+    block = jnp.floor((depth + 0.5) * (1.0 / TILES))
+    return (line - 4.0 * depth) * 48.0 + (depth - TILES * block) * 8.0 + block, column
+
+
+def own_kernel(
+    tab_k, tab_a, tab_n, plan, h0, zones, cells_at, goals,
+    k1, kl1, kn1, ic1, g1, p1, q1, prm, part, most_out, near, pick, put, column, goal,
+):
     base = 8 * lax.axis_index("row") - 4
     sub = iota((SUB, WIDTH), 0)
     rel = (jnp.where(sub < 2, zones[0:1, :], zones[1:2, :]).astype(jnp.int32) - base) & (ZONES - 1)
@@ -210,24 +214,59 @@
         sat = jnp.where(here, tab_k[at], sat)
         alpha = jnp.where(here, tab_a[at], alpha)
         n = jnp.where(here, tab_n[at], n)
-        column = jnp.where(line == 0, tab_k[at], jnp.where(line == 1, tab_a[at], tab_n[at]))
-        table = jnp.where(lane == i, column, table)
+        entry = jnp.where(line == 0, tab_k[at], jnp.where(line == 1, tab_a[at], tab_n[at]))
+        table = jnp.where(lane == i, entry, table)
     near[...] = table
-    for i, value in enumerate(derived(sat, alpha, n)):
+    levels = [
+        2.0 * IRRIGATION * jnp.where(sub < 2, plan[step, 0].astype(F32), plan[step, 1].astype(F32))
+        for step in range(2)
+    ]
+    for i, value in enumerate(derived(sat, alpha, n) + (*levels, 1.0 / sat, 1.0 / alpha)):
         for r in range(4):
-            prm[r, i : i + 1, :] = value[r : r + 1, :]
+            prm[2 + r, i : i + 1, :] = value[r : r + 1, :]
 
     def cells(r, carry):
         p = row_params(prm, r)
         for j in range(TILES):
-            k[r, j], kl[r, j], kn[r, j], ic[r, j], sl[r, j], sn[r, j] = cell_math(own[r, j], p)
-        return carry
-
-    lax.fori_loop(0, 4, cells, 0)
+            values = cell_math(h0[r, j], p)
+            k1[r, j], kl1[r, j], kn1[r, j], ic1[r - 1, j], p1[r - 1, j], q1[r - 1, j] = values
+        return carry
+
+    lax.fori_loop(2, 6, cells, 0)
+
+    def flow(r, most):
+        for j, net, total in net_row(h0, k1, r, prm[r, LEV0 : LEV0 + 1, :], (r - 1, r + 1)):
+            ic = ic1[r - 1, j]
+            g = net * ic
+            g1[r - 1, j] = g
+            p1[r - 1, j] = g * p1[r - 1, j]
+            q1[r - 1, j] = g * q1[r - 1, j]
+            most = jnp.maximum(most, total * ic)
+        return most
+
+    def edge_flow(i, carry):
+        r = 2 + 3 * i
+        for j, net, total in net_row(h0, k1, r, prm[r, LEV0 : LEV0 + 1, :], (3 + i,)):
+            g1[r - 1, j] = net
+            part[i, j] = total
+        return carry
+
+    most_out[...] = lax.fori_loop(3, 5, flow, jnp.zeros((SUB, WIDTH), F32))
+    lax.fori_loop(0, 2, edge_flow, 0)
+
+    count = cells_at.shape[1]
+    wide = jnp.where(iota((SUB, count), 0) == 0, cells_at[...].astype(F32), goals[...])
+    tall = jnp.transpose(wide)
+    line_wide = places(wide[0:1, :])[0].astype(jnp.int32)
+    line_tall, column_tall = places(tall[:, 0:1])
+    pick[...] = (iota((count, 192), 1) == line_tall.astype(jnp.int32)).astype(F32).astype(jnp.bfloat16)
+    put[...] = (iota((192, count), 0) == line_wide).astype(F32).astype(jnp.bfloat16)
+    column[...] = (iota((count, WIDTH), 1) == column_tall.astype(jnp.int32)).astype(F32)
+    goal[...] = jnp.broadcast_to(tall[:, 1:2], goal.shape)
 
 
 def first_kernel(
-    plan, near, own, zones, own_prm, k, kl, kn, ic, sl, sn, got_odd, got_even,
+    near, zones, part, most_in, got_odd, got_even, _h0, _k1, _kl1, _kn1, _ic1, _g1, _p1, _q1, _prm,
     h0, k1, kl1, kn1, ic1, g1, p1, q1, prm, zrel, spread,
 ):
     position = lax.axis_index("row")
@@ -237,39 +276,32 @@
         for j in range(TILES):
             at = row * TILES + j
             one, other = got_odd[at], got_even[at]
-            h0[row, j] = jnp.where(has_low, jnp.where(odd, other, one), own[0, j])
-            h0[6 + row, j] = jnp.where(has_high, jnp.where(odd, one, other), own[3, j])
-    h0[2:6] = own[...]
-    for here, there in ((k, k1), (kl, kl1), (kn, kn1)):
-        there[2:6] = here[...]
-    ic1[1:5] = ic[...]
+            h0[row, j] = jnp.where(has_low, jnp.where(odd, other, one), h0[2, j])
+            h0[6 + row, j] = jnp.where(has_high, jnp.where(odd, one, other), h0[5, j])
     one, other = got_odd[2 * TILES], got_even[2 * TILES]
     extra_low, extra_high = jnp.where(odd, other, one), jnp.where(odd, one, other)
     z_low = jnp.where(has_low, extra_low[0:1, :], zones[0:1, :])
     z_high = jnp.where(has_high, extra_high[0:1, :], zones[1:2, :])
     sub = iota((SUB, WIDTH), 0)
-
-    def by_row(a, b, c, d):
-        return jnp.where(sub < 4, jnp.where(sub < 2, a, b), jnp.where(sub < 6, c, d))
-
-    zone = by_row(z_low, zones[0:1, :], zones[1:2, :], z_high).astype(jnp.int32)
+    zone = jnp.where(
+        sub < 4,
+        jnp.where(sub < 2, z_low, zones[0:1, :]),
+        jnp.where(sub < 6, zones[1:2, :], z_high),
+    ).astype(jnp.int32)
     rel = (zone - (8 * position - 4)) & (ZONES - 1)
     zrel[...] = rel
     ids = iota((32, WIDTH), 0)
     sides = []
     for r in (0, 7):
-        pick = (ids == rel[r : r + 1, :]).astype(F32).astype(jnp.bfloat16)
-        parts = [jnp.dot(x, pick, preferred_element_type=F32) for x in split3(near[:, :32])]
+        here = (ids == rel[r : r + 1, :]).astype(F32).astype(jnp.bfloat16)
+        parts = [jnp.dot(x, here, preferred_element_type=F32) for x in split3(near[:, :32])]
         sides.append(parts[0] + (parts[1] + parts[2]))
     sat, alpha, n = (
-        by_row(sides[0][i : i + 1, :], own_prm[0, i : i + 1, :], own_prm[2, i : i + 1, :], sides[1][i : i + 1, :])
-        for i in range(3)
+        jnp.where(sub < 4, sides[0][i : i + 1, :], sides[1][i : i + 1, :]) for i in range(3)
     )
-    lev_0 = by_row(extra_low[1:2, :], plan[0, 0].astype(F32), plan[0, 1].astype(F32), extra_high[1:2, :])
-    lev_1 = by_row(0.0, plan[1, 0].astype(F32), plan[1, 1].astype(F32), 0.0) + 0.0 * sat
-    made = derived(sat, alpha, n) + (IRRIGATION * lev_0, IRRIGATION * lev_1, 1.0 / sat, 1.0 / alpha)
-    for i, value in enumerate(made):
-        for r in range(ROWS):
+    level = 2.0 * IRRIGATION * jnp.where(sub < 4, extra_low[1:2, :], extra_high[1:2, :])
+    for i, value in enumerate(derived(sat, alpha, n) + (level, level, 1.0 / sat, 1.0 / alpha)):
+        for r in (0, 1, 6, 7):
             prm[r, i : i + 1, :] = value[r : r + 1, :]
 
     def outer(i, carry):
@@ -280,39 +312,42 @@
         return carry
 
     def inner(i, carry):
-        r = 1 + 5 * i
+        r, own = 1 + 5 * i, 2 + 3 * i
+        real = jnp.where(i == 0, has_low, has_high)
         p = row_params(prm, r)
         for j in range(TILES):
-            values = cell_math(h0[r, j], p)
-            k1[r, j], kl1[r, j], kn1[r, j], ic1[r - 1, j], p1[r - 1, j], q1[r - 1, j] = values
+            cond, kl1[r, j], kn1[r, j], ic1[r - 1, j], p1[r - 1, j], q1[r - 1, j] = cell_math(h0[r, j], p)
+            k1[r, j] = jnp.where(real, cond, -k1[own, j])
         return carry
 
     lax.fori_loop(0, 2, outer, 0)
     lax.fori_loop(0, 2, inner, 0)
-    p1[1:5] = sl[...]
-    q1[1:5] = sn[...]
-
-    def flow(r, most):
-        low, high = row_open(position, r)
-        is_own = jnp.logical_and(r >= 2, r <= 5)
-        real = jnp.logical_or(is_own, jnp.logical_or(jnp.logical_and(r < 2, has_low), jnp.logical_and(r > 5, has_high)))
-        for j, net, total in net_row(h0, k1, r, prm[r, LEV0 : LEV0 + 1, :], low, high):
-            ic = ic1[r - 1, j]
-            g = jnp.where(real, net * ic, 0.0)
+
+    def flow(i, most):
+        r, own = 1 + 5 * i, 2 + 3 * i
+        real = jnp.where(i == 0, has_low, has_high)
+        for j, net, _ in net_row(h0, k1, r, prm[r, LEV0 : LEV0 + 1, :], (r - 1, r + 1)):
+            g = jnp.where(real, net * ic1[r - 1, j], 0.0)
             g1[r - 1, j] = g
             p1[r - 1, j] = g * p1[r - 1, j]
             q1[r - 1, j] = g * q1[r - 1, j]
-            most = jnp.maximum(most, jnp.where(is_own, total * ic, 0.0))
+            kx = k1[r, j] + k1[own, j]
+            ic = ic1[own - 1, j]
+            g = (g1[own - 1, j] + kx * (h0[r, j] - h0[own, j])) * ic
+            g1[own - 1, j] = g
+            p1[own - 1, j] = g * p1[own - 1, j]
+            q1[own - 1, j] = g * q1[own - 1, j]
+            most = jnp.maximum(most, (part[i, j] + kx) * ic)
         return most
 
-    most = lax.fori_loop(1, 7, flow, jnp.zeros((SUB, WIDTH), F32))
+    most = lax.fori_loop(0, 2, flow, most_in[...])
     most = jnp.maximum(jnp.maximum(most[:, :128], most[:, 128:256]), most[:, 256:])
     most = jnp.max(most, 0, keepdims=True)
     spread[...] = jnp.broadcast_to(most[None], spread.shape)
 
 
 def second_kernel(
-    rates, cells_at, goals, h0, k1, kl1, kn1, ic1, g1, p1, q1, prm, zrel,
+    rates, pick, put, column, goal, h0, k1, kl1, kn1, ic1, g1, p1, q1, prm, zrel,
     h1_out, g2, spread,
     h1, k2, kl2, kn2, ic2, sl2, sn2, va, vb, wa, wb, w0, w1, w2, maps,
 ):
@@ -339,18 +374,20 @@
     def edge_cells(i, carry):
         r = 1 + 5 * i
         p = row_params(prm, r)
-        for j in range(TILES):
-            head = h0[r, j] + size * g1[r - 1, j]
+        own = 2 + 3 * i
+        real = jnp.where(i == 0, position > 0, position < lax.axis_size("row") - 1)
+        for j in range(TILES):
+            head = jnp.where(real, h0[r, j] + size * g1[r - 1, j], h1[own, j])
             h1[r, j] = head
-            k2[r, j], kl2[r, j], kn2[r, j] = cell_math(head, p, False)
-        return carry
-
+            cond, kl2[r, j], kn2[r, j] = cell_math(head, p, False)
+            k2[r, j] = jnp.where(real, cond, -k2[own, j])
+        return carry
+
+    lax.fori_loop(2, 6, cells, 0)
     lax.fori_loop(0, 2, edge_cells, 0)
-    lax.fori_loop(2, 6, cells, 0)
 
     def flow(r, most):
-        low, high = row_open(position, r)
-        for j, net, total in net_row(h1, k2, r, prm[r, LEV1 : LEV1 + 1, :], low, high):
+        for j, net, total in net_row(h1, k2, r, prm[r, LEV1 : LEV1 + 1, :], (r - 1, r + 1)):
             ic = ic2[r - 2, j]
             g2[r - 2, j] = net * ic
             most = jnp.maximum(most, total * ic)
@@ -358,36 +395,19 @@
 
     most = jnp.max(lax.fori_loop(2, 6, flow, jnp.zeros((SUB, WIDTH), F32)))
 
-    def places(cell):
-        line = jnp.floor((cell + 0.5) * (1.0 / WIDTH))
-        column = cell - WIDTH * line
-        depth = jnp.floor((line + 0.5) * 0.25)
-        block = jnp.floor((depth + 0.5) * (1.0 / TILES))
-        return (line - 4.0 * depth) * 48.0 + (depth - TILES * block) * 8.0 + block, column
-
-    count = cells_at.shape[1]
-    line_of = iota((SUB, count), 0)
-    wide = jnp.where(line_of == 0, cells_at[...].astype(F32), goals[...])
-    tall = jnp.transpose(wide)
-    line_wide = places(wide[0:1, :])[0].astype(jnp.int32)
-    line_tall, column_tall = places(tall[:, 0:1])
-    goal = tall[:, 1:2]
-    pick = (iota((count, 192), 1) == line_tall.astype(jnp.int32)).astype(F32).astype(jnp.bfloat16)
-    put = (iota((192, count), 0) == line_wide).astype(F32).astype(jnp.bfloat16)
-    column = iota((count, WIDTH), 1) == column_tall.astype(jnp.int32)
     field_g = g2[...].reshape(192, WIDTH)
     field_h = h1_out[...].reshape(192, WIDTH) + size * field_g
-    seen_h = jnp.sum(jnp.where(column, exact_dot(pick, field_h), 0.0), 1, keepdims=True)
-    seen_g = jnp.sum(jnp.where(column, exact_dot(pick, field_g), 0.0), 1, keepdims=True)
-    diff = seen_h - goal
+    seen_h = jnp.sum(column[...] * exact_dot(pick[...], field_h), 1, keepdims=True)
+    seen_g = jnp.sum(column[...] * exact_dot(pick[...], field_g), 1, keepdims=True)
+    diff = seen_h - goal[:, 0:1]
     events = 16.0
     loss = (
         jnp.sum(diff * diff) * (0.5 / events),
         jnp.sum(diff * seen_g) * (1.0 / events),
         jnp.sum(seen_g * seen_g) * (0.5 / events),
     )
-    va[...] = exact_dot(put, jnp.where(column, diff * (1.0 / events), 0.0)).reshape(OWN)
-    vb[...] = exact_dot(put, jnp.where(column, seen_g * (1.0 / events), 0.0)).reshape(OWN)
+    va[...] = exact_dot(put[...], column[...] * (diff * (1.0 / events))).reshape(OWN)
+    vb[...] = exact_dot(put[...], column[...] * (seen_g * (1.0 / events))).reshape(OWN)
 
     def scaled(r, carry):
         for j in range(TILES):
@@ -421,13 +441,11 @@
     def edge_two(i, carry):
         r = 1 + 5 * i
         near = 2 + 3 * i
-        low, high = row_open(position, r)
-        is_open = jnp.where(i == 0, high, low)
         sums = [jnp.zeros((SUB, WIDTH), F32) for _ in range(12)]
         for j in range(TILES):
             hj = h1[r, j]
-            half = (0.5 * is_open) * (h1[near, j] - hj)
-            kd = (0.5 * is_open) * (k2[near, j] + k2[r, j])
+            half = h1[near, j] - hj
+            kd = k2[near, j] + k2[r, j]
             kj, kl, kn = k2[r, j], kl2[r, j], kn2[r, j]
             inv_h = 1.0 / hj
             back = []
@@ -444,7 +462,6 @@
         return carry
 
     def back_two(r, carry):
-        low, high = row_open(position, r)
         top = prm[r, LEV1 : LEV1 + 1, :]
         hs = [h1[r, j] for j in range(TILES)]
         ks = [k2[r, j] for j in range(TILES)]
@@ -453,19 +470,19 @@
 
         def face(j):
             if j < TILES - 1:
-                half = 0.5 * (1.0 + hs[j] - hs[j + 1])
-                kd = 0.5 * (ks[j] + ks[j + 1])
+                half = 1.0 + hs[j] - hs[j + 1]
+                kd = ks[j] + ks[j + 1]
                 out = []
                 for w in ws:
                     dw = w[j + 1] - w[j]
                     out.append((half * dw, kd * dw))
                 return out
-            half = 0.5 * (1.0 + hs[j] - subs_up(hs[0]))
-            kd = 0.5 * (ks[j] + subs_up(ks[0]))
+            half = 1.0 + hs[j] - subs_up(hs[0])
+            kd = ks[j] + subs_up(ks[0])
             out = []
             for w in ws:
                 dw = subs_up(w[0]) - w[j]
-                out.append((jnp.where(is_bottom, -w[j], half * dw), jnp.where(is_bottom, 0.0, kd * dw)))
+                out.append((jnp.where(is_bottom, -2.0 * w[j], half * dw), jnp.where(is_bottom, 0.0, kd * dw)))
             return out
 
         final = face(TILES - 1)
@@ -476,10 +493,10 @@
         for j in range(TILES):
             below = final if j == TILES - 1 else face(j)
             hj, kj = hs[j], ks[j]
-            half_c = jnp.where(last, 0.0, 0.5 * (lanes_left(hj) - hj))
-            kf = jnp.where(last, 0.0, 0.5 * (lanes_left(kj) + kj))
-            half_l, half_h = (0.5 * low) * (h1[r - 1, j] - hj), (0.5 * high) * (h1[r + 1, j] - hj)
-            k_low, k_high = (0.5 * low) * (k2[r - 1, j] + kj), (0.5 * high) * (k2[r + 1, j] + kj)
+            half_c = jnp.where(last, 0.0, lanes_left(hj) - hj)
+            kf = jnp.where(last, 0.0, lanes_left(kj) + kj)
+            half_l, half_h = h1[r - 1, j] - hj, h1[r + 1, j] - hj
+            k_low, k_high = k2[r - 1, j] + kj, k2[r + 1, j] + kj
             kl, kn = kl2[r, j], kn2[r, j]
             inv_h = 1.0 / hj
             g = g2[r - 2, j]
@@ -525,7 +542,7 @@
         near = 1 + 5 * i
         sums = [jnp.zeros((SUB, WIDTH), F32) for _ in range(9)]
         for j in range(TILES):
-            half = 0.5 * (h0[r, j] - h0[near, j])
+            half = h0[r, j] - h0[near, j]
             kj, kl, kn = k1[r, j], kl1[r, j], kn1[r, j]
             for part, w_ref in enumerate(refs):
                 gk = half * w_ref[near, j]
@@ -536,7 +553,6 @@
         return carry
 
     def back_one(r, carry):
-        low, high = row_open(position, r)
         top = prm[r, LEV0 : LEV0 + 1, :]
         hs = [h0[r, j] for j in range(TILES)]
         ws = [[w[r, j] for j in range(TILES)] for w in refs]
@@ -544,19 +560,18 @@
 
         def face(j):
             if j < TILES - 1:
-                half = 0.5 * (1.0 + hs[j] - hs[j + 1])
+                half = 1.0 + hs[j] - hs[j + 1]
                 return [half * (w[j + 1] - w[j]) for w in ws]
-            half = 0.5 * (1.0 + hs[j] - subs_up(hs[0]))
-            return [jnp.where(is_bottom, -w[j], half * (subs_up(w[0]) - w[j])) for w in ws]
+            half = 1.0 + hs[j] - subs_up(hs[0])
+            return [jnp.where(is_bottom, -2.0 * w[j], half * (subs_up(w[0]) - w[j])) for w in ws]
 
         final = face(TILES - 1)
         above = [jnp.where(is_top, top * w[0], subs_down(f)) for w, f in zip(ws, final)]
         for j in range(TILES):
             below = final if j == TILES - 1 else face(j)
             hj = hs[j]
-            half_c = jnp.where(last, 0.0, 0.5 * (lanes_left(hj) - hj))
-            half_l = (0.5 * low) * (h0[r - 1, j] - hj)
-            half_h = (0.5 * high) * (h0[r + 1, j] - hj)
+            half_c = jnp.where(last, 0.0, lanes_left(hj) - hj)
+            half_l, half_h = h0[r - 1, j] - hj, h0[r + 1, j] - hj
             kj, kl, kn = k1[r, j], kl1[r, j], kn1[r, j]
             for part, w_ref in enumerate(refs):
                 w = ws[part][j]
@@ -610,32 +625,34 @@
             total = total + jnp.where(jnp.logical_and(lane >= start, lane < start + NEAR), moved, 0.0)
         loss = loss + tile
     total = jnp.where(lane == 252, pltpu.roll(loss, 252 - 96, 1), total)
-    state = jnp.concatenate(
-        [jnp.broadcast_to(most[:, 0:1], (SUB, 128)), jnp.broadcast_to(most[:, 64:65], (SUB, 128))], 1
-    )
-    total = jnp.where(iota((SUB, 256), 0) % 4 == 3, state, total)
-    spread[...] = jnp.broadcast_to(total[None], spread.shape)
+    rows = []
+    one = iota((1, 256), 1)
+    for z_hi in range(2):
+        state = most[4 * z_hi + 3 : 4 * z_hi + 4, :]
+        for power in range(3):
+            row = total[4 * z_hi + power : 4 * z_hi + power + 1, :]
+            row = jnp.where(one == 253, state[:, 0:1], row)
+            rows.append(jnp.where(one == 254, state[:, 64:65], row))
+    rows = jnp.concatenate(rows, 1)
+    spread[...] = jnp.broadcast_to(rows[None], spread.shape)
 
 
 def last_kernel(parts, h1, g2, final, grad_k, grad_a, grad_n, misfit, rates):
-    sub = iota((SUB, 256), 0)
-    power = sub % 4
-    sums = [jnp.zeros((SUB, 256), F32) for _ in range(4)]
+    sums = [jnp.zeros((1, 256), F32) for _ in range(4)]
     for pair in range(8):
         tiles = [parts[8 * y + pair] for y in range(4)]
-        most = jnp.maximum(jnp.maximum(tiles[0], tiles[1]), jnp.maximum(tiles[2], tiles[3]))
-        step = CFL / most
-        rates[pair] = step
-        moves = []
-        for row in (3, 7):
-            move = step[row : row + 1, :128] - most[row : row + 1, 128:]
-            moves.append(jnp.concatenate([move, move], 1))
-        move = jnp.where(sub < 4, moves[0], moves[1])
-        weight = jnp.where(power == 0, 1.0, jnp.where(power == 1, move, move * move))
-        for y in range(4):
-            sums[y] = sums[y] + jnp.where(power == 3, 0.0, tiles[y] * weight)
+        for z_hi in range(2):
+            powers = [[tile[:, 256 * (3 * z_hi + i) : 256 * (3 * z_hi + i + 1)] for i in range(3)] for tile in tiles]
+            first = [part[0] for part in powers]
+            most = jnp.maximum(jnp.maximum(first[0], first[1]), jnp.maximum(first[2], first[3]))
+            step = CFL / most[:, 253:254]
+            rates[2 * pair + z_hi] = jnp.broadcast_to(step, (1, 128))
+            move = step - first[0][:, 254:255]
+            for y in range(4):
+                a, b, c = powers[y]
+                sums[y] = sums[y] + (a + move * (b + move * c))
     lane = iota((1, 256), 1)
-    rows = [jnp.sum(x, 0, keepdims=True) for x in sums]
+    rows = sums
     for q, out in enumerate((grad_k, grad_a, grad_n)):
         total = jnp.zeros((1, 256), F32)
         for y in range(4):
@@ -644,8 +661,7 @@
         out[...] = total
     misfit[0, 0] = jnp.sum(jnp.where(lane == 252, rows[0] + rows[1] + rows[2] + rows[3], 0.0))
     _, pair, z_hi = axes()
-    mine = rates[pair]
-    size = jnp.where(z_hi == 0, mine[3:4, :128], mine[7:8, :128])
+    size = rates[2 * pair + z_hi]
     size = jnp.concatenate([size, size, size], 1)
     for j in range(TILES):
         for row in range(4):
@@ -658,7 +674,7 @@
 SMEM = pl.BlockSpec(memory_space=pltpu.SMEM)
 
 
-def call(kernel, name, ins, outs, out_specs=None, scratch=(), cost=None):
+def call(kernel, name, ins, outs, out_specs=None, scratch=(), cost=None, in_place=None):
     return pl.pallas_call(
         kernel,
         name=name,
@@ -667,6 +683,7 @@
         out_shape=[jax.ShapeDtypeStruct(shape, dtype) for shape, dtype in outs],
         scratch_shapes=scratch,
         cost_estimate=cost,
+        input_output_aliases=in_place or {},
         compiler_params=pltpu.CompilerParams(vmem_limit_bytes=32 * 1024 * 1024),
     )
 
@@ -684,11 +701,11 @@
     count = lax.axis_size("row")
     plan = forcing_plan[0]
     edge = (2 * TILES + 1, SUB, WIDTH)
-    own, send_odd, send_even, zones = call(
+    h0, send_odd, send_even, zones = call(
         pack_kernel,
         "pack_edges",
-        [pl.BlockSpec(memory_space=pl.ANY)] * 3,
-        [(OWN, F32), (edge, F32), (edge, F32), ((2, WIDTH), F32)],
+        [pl.BlockSpec(memory_space=pltpu.HBM)] * 3,
+        [(FIELD, F32), (edge, F32), (edge, F32), ((2, WIDTH), F32)],
         scratch=[
             pltpu.VMEM((48, 4, WIDTH), F32),
             pltpu.VMEM((2, 192), jnp.int32),
@@ -700,37 +717,40 @@
     even = [(i, i + 1) for i in range(0, count, 2)]
     got_odd = lax.ppermute(send_odd, "row", odd + [(j, i) for i, j in odd])
     got_even = lax.ppermute(send_even, "row", even + [(j, i) for i, j in even])
-    own_fields = call(
+    wide = (6, TILES, SUB, WIDTH)
+    fields = [(FIELD, F32)] * 3 + [(wide, F32)] * 4 + [((ROWS, 16, WIDTH), F32)]
+    seen = tensiometer_cells.shape[1]
+    own = call(
         own_kernel,
         "own_cells",
-        [SMEM] * 3 + [VMEM] * 2,
-        [(OWN, F32)] * 6 + [((4, 16, WIDTH), F32), ((SUB, 128), F32)],
-        cost=pl.CostEstimate(flops=100_000_000, bytes_accessed=8_000_000, transcendentals=600_000),
-    )(sat_conductivity, vg_alpha, vg_n, own, zones)
-    own_prm, near = own_fields[6:]
-    wide = (6, TILES, SUB, WIDTH)
+        [SMEM] * 4 + [VMEM] * 4,
+        fields
+        + [((2, TILES, SUB, WIDTH), F32), ((SUB, WIDTH), F32), ((SUB, 128), F32)]
+        + [((seen, 192), jnp.bfloat16), ((192, seen), jnp.bfloat16), ((seen, WIDTH), F32), ((seen, 128), F32)],
+        cost=pl.CostEstimate(flops=200_000_000, bytes_accessed=8_000_000, transcendentals=600_000),
+    )(sat_conductivity, vg_alpha, vg_n, plan, h0, zones, tensiometer_cells, tensiometer_heads)
+    own_fields, (part, most, near), sensors = own[:8], own[8:11], own[11:]
     first = call(
         first_kernel,
         "first_step",
-        [SMEM] + [VMEM] * 12,
-        [(FIELD, F32)] * 4
-        + [(wide, F32)] * 4
-        + [((ROWS, 16, WIDTH), F32), ((ROWS, WIDTH), jnp.int32), ((32, 1, 128), F32)],
-    )(plan, near, own, zones, own_prm, *own_fields[:6], got_odd, got_even)
+        [VMEM] * 15,
+        [(FIELD, F32)] + fields + [((ROWS, WIDTH), jnp.int32), ((32, 1, 128), F32)],
+        in_place={6 + i: i for i in range(9)},
+    )(near, zones, part, most, got_odd, got_even, h0, *own_fields)
     fields, rates = first[:-1], first[-1]
     rates = lax.all_to_all(rates, "row", 0, 0, tiled=True)
     h1, g2, sums = call(
         second_kernel,
         "second_step_and_adjoint",
-        [VMEM] * 13,
+        [VMEM] * 15,
         [(OWN, F32), (OWN, F32), ((16, 4, 128), F32)],
         scratch=[pltpu.VMEM(FIELD, F32)] * 4
         + [pltpu.VMEM(OWN, F32)] * 5
         + [pltpu.VMEM(FIELD, F32)] * 5
         + [pltpu.VMEM((ROWS, 16, WIDTH), F32)],
-    )(rates, tensiometer_cells, tensiometer_heads, *fields)
+    )(rates, *sensors, *fields)
     sums = lax.all_to_all(sums, ("event", "row"), 0, 0, tiled=True, axis_index_groups=RINGS)
-    (sums,) = call(ring_kernel, "ring_sums", [VMEM], [((32, SUB, 256), F32)])(sums)
+    (sums,) = call(ring_kernel, "ring_sums", [VMEM], [((32, 1, 6 * 256), F32)])(sums)
     sums = lax.all_to_all(sums, ("event", "row"), 0, 0, tiled=True, axis_index_groups=PLANES)
     row = ((1, ZONES), F32)
     final, grad_k, grad_a, grad_n, misfit = call(
@@ -739,7 +759,7 @@
         [VMEM, VMEM, VMEM],
         [((48, 4, WIDTH), F32), row, row, row, ((1, 1), F32)],
         [VMEM] * 4 + [SMEM],
-        scratch=[pltpu.VMEM((8, SUB, 256), F32)],
+        scratch=[pltpu.VMEM((16, 1, 128), F32)],
     )(sums, h1, g2)
     return (final[None], misfit[0, 0], grad_k[0], grad_a[0], grad_n[0])
 

time: 97.3 us -> 94.5 us (0.971)
  blocking collectives: 70.5 us -> 69.1 us
  transfers between devices with their start and end apart: 2 -> 2, of which waited for: 1 -> 0; matrix products, arithmetic and copies ran while one was open for 0% -> 0% of each run, Pallas kernels for 1% -> 3%
where the time goes in v2:
time: 94.5 us; the launch traced here: 94.2 us
  blocking collectives  69.1 us (73%)
  Pallas kernels  13.9 us (15%)
  starting transfers between devices  8.05 us (9%)
  local copies, waits for them, and re-layouts  2.3 us (2%)
    all_to_all x2, blocking collectives, local(): lax.all_to_all(sums, ('event', 'row'), 0, 0, tiled=True, axis_index_group...  38.9 us
    all_to_all x1, blocking collectives, local(): rates = lax.all_to_all(rates, 'row', 0, 0, tiled=True)  30.2 us
    pallas_call x1, Pallas kernels, local(): call(second_kernel, 'second_step_and_adjoint', [VMEM] * 15, [(OWN, F32),...  8.35 us
    ppermute x1, starting transfers between devices, local(): got_even = lax.ppermute(send_even, 'row', even + [(j, i) for i, j in even])  7.38 us
    pallas_call x1, Pallas kernels, local(): call(own_kernel, 'own_cells', [SMEM] * 4 + [VMEM] * 4, fields + [((2, TIL...  2.53 us
    unnamed x16, local copies, waits for them, and re-layouts  2.3 us
  transfers between devices with their start and end apart: 2, of which 0 were waited for; matrix products, arithmetic and copies ran while one was open for 0% of the time, Pallas kernels for 3%

profile of v2, /device:TPU:1, one launch (start us, length us, event | category | flops | bytes accessed | tf_op | source)
XLA Modules:
  0.0 94.2 jit_solution(584316819837804624)
XLA Ops:
  0.6 0.0 copy-start.1
  0.6 0.0 copy-start.2
  0.7 0.7 copy-done.1
  1.3 0.0 copy-done.2
  1.3 1.0 %copy-done = f32[1,48,4,384]{3,2,1,0:T(4,128)S(1)} copy-done((f32[1,48,4,384]{3,2,1,0:T(4,128)S(1)}, f32[1,48,4,384]{3,2,1,0:T(4,128)}, u32[]{:S(2)}) %copy-start) | copy-done | bytes 294936
  2.3 0.4 pack_edges.1
  2.7 0.7 collective-permute-start
  3.4 0.0 copy-start.4
  3.4 0.0 copy-start.5
  3.4 0.0 copy-start.6
  3.5 0.0 copy-start.7
  3.5 7.4 %collective-permute-start.1 = (f32[13,8,384]{2,1,0:T(8,128)S(1)}, f32[13,8,384]{2,1,0:T(8,128)S(1)}, u32[]{:S(2)}, u32[]{:S(2)}) collective-permute-start(f32[13,8,384]{2,1,0:T(8,128)S(1)} %get-tuple-element.49), channel_id=1, source_target_pairs={{0,1},{2,3},{4,5},{6,7},{8,9},{10,11},{12,13},{14,15},{16,17},{18,... | collective-permute-start | bytes 479240 | tf_op jit(solution)/shard_map/ppermute | solution.py:719
  10.9 0.0 copy-start.3
  10.9 0.6 copy-done.3
  11.5 2.5 %own_cells.1 = (f32[8,6,8,384]{3,2,1,0:T(8,128)S(1)}, f32[8,6,8,384]{3,2,1,0:T(8,128)S(1)}, f32[8,6,8,384]{3,2,1,0:T(8,128)S(1)}, f32[6,6,8,384]{3,2,1,0:T(8,128...) custom-call(f32[256]{0:T(256)S(1)} %copy-done.3, ...), custom_call_target="tpu_custom_call" | custom-call | flops 200000000 | bytes 8000000 | tf_op jit(solution)/shard_map/own_cells/pallas_call | solution.py:723
  14.1 0.0 collective-permute-done.got_odd
  14.1 0.0 collective-permute-done.1.got_even
  14.1 1.3 %first_step.1 = (f32[8,6,8,384]{3,2,1,0:T(8,128)S(1)}, f32[8,6,8,384]{3,2,1,0:T(8,128)S(1)}, f32[8,6,8,384]{3,2,1,0:T(8,128)S(1)}, f32[8,6,8,384]{3,2,1,0:T(8,12...) custom-call(f32[8,128]{1,0:T(8,128)S(1)} %get-tuple-element.45.near,, ...), custom_call_target="tpu_custom_call", output_to_operand_aliasing={{0}: (6, {}), {1}: (7, {}), {2}: (8, {}), {3}: (9, {}), {4}... | custom-call | tf_op jit(solution)/shard_map/first_step/pallas_call | solution.py:733
  15.4 30.2 %all_to_all.15.rates = f32[32,1,128]{2,1,0:T(1,128)S(1)} all-to-all(f32[32,1,128]{2,1,0:T(1,128)S(1)} %get-tuple-element.58), channel_id=1, replica_groups=mesh['event'=16,'row'=32] {'row'}, dimensions={0} | all-to-all | bytes 32768 | tf_op jit(solution)/shard_map/all_to_all | solution.py:741
  45.6 8.3 %second_step_and_adjoint.1 = (f32[4,6,8,384]{3,2,1,0:T(8,128)S(1)}, f32[4,6,8,384]{3,2,1,0:T(8,128)S(1)}, f32[16,4,128]{2,1,0:T(4,128)S(1)}) custom-call(f32[32,1,128]{2,1,0:T(1,128)S(1)} %all_to_all.15.rates, bf16[256,192]{1,0:T(8,128)(2,1)S(1)} %get-tuple-element.59.pick, bf16[192,256]{1,0:T(8,128)(2,1)S(1)} %get-tuple-element.60.put, ...), custom_call_target="tpu_custom_call" | custom-call | tf_op jit(solution)/shard_map/second_step_and_adjoint/pallas_call | solution.py:742
  54.0 22.4 %all_to_all.16.parts = f32[16,4,128]{2,1,0:T(4,128)S(1)} all-to-all(f32[16,4,128]{2,1,0:T(4,128)S(1)} %get-tuple-element.73), channel_id=1, replica_groups={{0,1,2,3,4,5,6,7,64,65,66,67,68,69,70,71},{8,9,10,11,12,13,14,15,72,73,..., dimensions={0} | all-to-all | bytes 65536 | tf_op jit(solution)/shard_map/all_to_all | solution.py:752
  76.3 0.1 ring_sums.1
  76.5 16.5 %all_to_all.17.parts = f32[32,1,1536]{2,1,0:T(1,128)S(1)} all-to-all(f32[32,1,1536]{2,1,0:T(1,128)S(1)} %ring_sums.1), channel_id=1, replica_groups={{0,32,128,160,256,288,384,416,8,40,136,168,264,296,392,424,16,48,144,17..., dimensions={0} | all-to-all | bytes 393216 | tf_op jit(solution)/shard_map/all_to_all | solution.py:754
  93.0 1.1 %final_head_and_sums.1 = (f32[48,4,384]{2,1,0:T(4,128)}, f32[1,256]{1,0:T(1,128)}, f32[1,256]{1,0:T(1,128)}, f32[1,256]{1,0:T(1,128)}, f32[1,1]{1,0:T(1,128)}) custom-call(f32[32,1,1536]{2,1,0:T(1,128)S(1)} %all_to_all.17.parts, f32[4,6,8,384]{3,2,1,0:T(8,128)S(1)} %get-tuple-element.74.h1, f32[4,6,8,384]{3,2,1,0:T(8,128)S(1)} %get-tuple-element.75.g2), custom_call_target="tpu_custom_call" | custom-call | tf_op jit(solution)/shard_map/final_head_and_sums/pallas_call | solution.py:756
  (5 shorter events, 0.0 us)
Async XLA Ops:
  0.6 0.7 copy-start.1
  0.6 0.7 copy-start.2
  1.3 1.0 %copy-start = (f32[1,48,4,384]{3,2,1,0:T(4,128)S(1)}, f32[1,48,4,384]{3,2,1,0:T(4,128)}, u32[]{:S(2)}) copy-start(f32[1,48,4,384]{3,2,1,0:T(4,128)} %param.8) | copy-start | bytes 884740
  2.7 11.3 %collective-permute-start = (f32[13,8,384]{2,1,0:T(8,128)S(1)}, f32[13,8,384]{2,1,0:T(8,128)S(1)}, u32[]{:S(2)}, u32[]{:S(2)}) collective-permute-start(f32[13,8,384]{2,1,0:T(8,128)S(1)} %get-tuple-element.48), channel_id=1, source_target_pairs={{1,2},{3,4},{5,6},{7,8},{9,10},{11,12},{13,14},{15,16},{17,18},{19... | collective-permute-start | bytes 479240 | tf_op jit(solution)/shard_map/ppermute | solution.py:718
  3.4 7.5 %copy-start.4 = (f32[256]{0:T(256)S(1)}, f32[256]{0:T(256)}, u32[]{:S(2)}) copy-start(f32[256]{0:T(256)} %tab_a.1) | copy-start | bytes 3076
  3.4 7.5 %copy-start.5 = (f32[256]{0:T(256)S(1)}, f32[256]{0:T(256)}, u32[]{:S(2)}) copy-start(f32[256]{0:T(256)} %tab_n.1) | copy-start | bytes 3076
  3.4 7.4 %copy-start.6 = (s32[1,256]{1,0:T(1,128)S(1)}, s32[1,256]{1,0:T(1,128)}, u32[]{:S(2)}) copy-start(s32[1,256]{1,0:T(1,128)} %cells_at.1) | copy-start | bytes 3076
  3.5 7.4 %copy-start.7 = (f32[1,256]{1,0:T(1,128)S(1)}, f32[1,256]{1,0:T(1,128)}, u32[]{:S(2)}) copy-start(f32[1,256]{1,0:T(1,128)} %goals.1) | copy-start | bytes 3076
  3.5 10.6 %collective-permute-start.1 = (f32[13,8,384]{2,1,0:T(8,128)S(1)}, f32[13,8,384]{2,1,0:T(8,128)S(1)}, u32[]{:S(2)}, u32[]{:S(2)}) collective-permute-start(f32[13,8,384]{2,1,0:T(8,128)S(1)} %get-tuple-element.49), channel_id=1, source_target_pairs={{0,1},{2,3},{4,5},{6,7},{8,9},{10,11},{12,13},{14,15},{16,17},{18,... | collective-permute-start | bytes 479240 | tf_op jit(solution)/shard_map/ppermute | solution.py:719
  10.9 0.7 copy-start.3

commit v3 on v2

--- a/solution.py
+++ b/solution.py
@@ -188,6 +188,45 @@
         yield j, net, total
 
 
+def reach_row(h, phis, ic, psi, r, same, foreign, top):
+    lane = iota((SUB, WIDTH), 1)
+    even = lane % 2 == 0
+    ends = jnp.logical_or(lane == 0, lane == WIDTH - 1)
+    _, is_top, is_bottom = masks()
+
+    def beside(x):
+        left, right = lanes_right(x), lanes_left(x)
+        return jnp.where(even, right, left), jnp.where(even, left, right)
+
+    for j in range(TILES):
+        hj, half = h[r, j], ic[r - 1, j]
+        inner, outer = beside(hj)
+        d_in = inner - hj
+        d_out = jnp.where(ends, 0.0, outer - hj)
+        h_below = h[r, j + 1] if j < TILES - 1 else subs_up(h[r, 0])
+        h_above = h[r, j - 1] if j > 0 else subs_down(h[r, TILES - 1])
+        d_below, d_above = h_below - hj - 1.0, 1.0 + h_above - hj
+        self_below, self_above = d_below, d_above
+        if j == TILES - 1:
+            self_below, d_below = jnp.where(is_bottom, -2.0, d_below), jnp.where(is_bottom, 0.0, d_below)
+        if j == 0:
+            self_above, d_above = jnp.where(is_top, top, d_above), jnp.where(is_top, 0.0, d_above)
+        d_same = h[same, j] - hj
+        whole = d_in + d_out + self_below + self_above + d_same
+        if foreign is not None:
+            d_far = h[foreign, j] - hj
+            whole = whole + d_far
+        for i, phi in enumerate(phis):
+            below = phi[r, j + 1] if j < TILES - 1 else subs_up(phi[r, 0])
+            above = phi[r, j - 1] if j > 0 else subs_down(phi[r, TILES - 1])
+            inner, outer = beside(phi[r, j])
+            own = whole * phi[r, j] + d_in * inner + d_below * below + d_above * above + d_same * phi[same, j]
+            psi[i][r - 1, j] = half * own
+            psi[3 + i][r - 1, j] = (half * d_out) * outer
+            if foreign is not None:
+                psi[6 + i][r - 1, j] = (half * d_far) * phi[foreign, j]
+
+
 def places(cell):
     line = jnp.floor((cell + 0.5) * (1.0 / WIDTH))
     column = cell - WIDTH * line
@@ -198,8 +237,10 @@
 
 def own_kernel(
     tab_k, tab_a, tab_n, plan, h0, zones, cells_at, goals,
-    k1, kl1, kn1, ic1, g1, p1, q1, prm, part, most_out, near, pick, put, column, goal,
+    g1, *rest,
 ):
+    psi, rest = rest[:9], rest[9:]
+    prm, most_out, near, pick, put, column, goal, k1, kl1, kn1, ic1, p1, q1 = rest
     base = 8 * lax.axis_index("row") - 4
     sub = iota((SUB, WIDTH), 0)
     rel = (jnp.where(sub < 2, zones[0:1, :], zones[1:2, :]).astype(jnp.int32) - base) & (ZONES - 1)
@@ -248,11 +289,32 @@
         r = 2 + 3 * i
         for j, net, total in net_row(h0, k1, r, prm[r, LEV0 : LEV0 + 1, :], (3 + i,)):
             g1[r - 1, j] = net
-            part[i, j] = total
+            g1[5 * i, j] = total
+            for at, value in enumerate((k1[r, j], kl1[r, j], kn1[r, j])):
+                psi[at][5 * i, j] = value
+            for at, value in enumerate((ic1[r - 1, j], p1[r - 1, j], q1[r - 1, j])):
+                psi[3 + at][5 * i, j] = value
         return carry
 
     most_out[...] = lax.fori_loop(3, 5, flow, jnp.zeros((SUB, WIDTH), F32))
     lax.fori_loop(0, 2, edge_flow, 0)
+    phis = (k1, kl1, kn1)
+
+    def reach(i, carry):
+        r = 3 + i
+        reach_row(h0, phis, ic1, psi, r, 2 + 3 * i, 4 - i, prm[r, LEV0 : LEV0 + 1, :])
+        for j in range(TILES):
+            psi[1][r - 1, j] = psi[1][r - 1, j] - p1[r - 1, j]
+            psi[2][r - 1, j] = psi[2][r - 1, j] - q1[r - 1, j]
+        return carry
+
+    def edge_reach(i, carry):
+        r = 2 + 3 * i
+        reach_row(h0, phis, ic1, psi, r, 3 + i, None, prm[r, LEV0 : LEV0 + 1, :])
+        return carry
+
+    lax.fori_loop(0, 2, reach, 0)
+    lax.fori_loop(0, 2, edge_reach, 0)
 
     count = cells_at.shape[1]
     wide = jnp.where(iota((SUB, count), 0) == 0, cells_at[...].astype(F32), goals[...])
@@ -261,14 +323,15 @@
     line_tall, column_tall = places(tall[:, 0:1])
     pick[...] = (iota((count, 192), 1) == line_tall.astype(jnp.int32)).astype(F32).astype(jnp.bfloat16)
     put[...] = (iota((192, count), 0) == line_wide).astype(F32).astype(jnp.bfloat16)
-    column[...] = (iota((count, WIDTH), 1) == column_tall.astype(jnp.int32)).astype(F32)
+    column[...] = (iota((count, WIDTH), 1) == column_tall.astype(jnp.int32)).astype(F32).astype(jnp.bfloat16)
     goal[...] = jnp.broadcast_to(tall[:, 1:2], goal.shape)
 
 
 def first_kernel(
-    near, zones, part, most_in, got_odd, got_even, _h0, _k1, _kl1, _kn1, _ic1, _g1, _p1, _q1, _prm,
-    h0, k1, kl1, kn1, ic1, g1, p1, q1, prm, zrel, spread,
+    near, zones, most_in, got_odd, got_even, *rest
 ):
+    h0, g1, *psi = rest[12:23]
+    prm, zrel, spread, k1, kl1, kn1, ic1, sl, sn, part, edge = rest[23:]
     position = lax.axis_index("row")
     has_low, has_high = position > 0, position < lax.axis_size("row") - 1
     odd = position % 2 == 1
@@ -278,6 +341,11 @@
             one, other = got_odd[at], got_even[at]
             h0[row, j] = jnp.where(has_low, jnp.where(odd, other, one), h0[2, j])
             h0[6 + row, j] = jnp.where(has_high, jnp.where(odd, one, other), h0[5, j])
+    for i in range(2):
+        part[i] = g1[5 * i]
+        for at, phi in enumerate((k1, kl1, kn1)):
+            phi[2 + 3 * i] = psi[at][5 * i]
+            edge[at, i] = psi[3 + at][5 * i]
     one, other = got_odd[2 * TILES], got_even[2 * TILES]
     extra_low, extra_high = jnp.where(odd, other, one), jnp.where(odd, one, other)
     z_low = jnp.where(has_low, extra_low[0:1, :], zones[0:1, :])
@@ -316,7 +384,7 @@
         real = jnp.where(i == 0, has_low, has_high)
         p = row_params(prm, r)
         for j in range(TILES):
-            cond, kl1[r, j], kn1[r, j], ic1[r - 1, j], p1[r - 1, j], q1[r - 1, j] = cell_math(h0[r, j], p)
+            cond, kl1[r, j], kn1[r, j], ic1[r - 1, j], sl[i, j], sn[i, j] = cell_math(h0[r, j], p)
             k1[r, j] = jnp.where(real, cond, -k1[own, j])
         return carry
 
@@ -326,17 +394,23 @@
     def flow(i, most):
         r, own = 1 + 5 * i, 2 + 3 * i
         real = jnp.where(i == 0, has_low, has_high)
+        reach_row(h0, (k1, kl1, kn1), ic1, psi, r, 7 * i, own, prm[r, LEV0 : LEV0 + 1, :])
         for j, net, _ in net_row(h0, k1, r, prm[r, LEV0 : LEV0 + 1, :], (r - 1, r + 1)):
             g = jnp.where(real, net * ic1[r - 1, j], 0.0)
             g1[r - 1, j] = g
-            p1[r - 1, j] = g * p1[r - 1, j]
-            q1[r - 1, j] = g * q1[r - 1, j]
+            psi[1][r - 1, j] = psi[1][r - 1, j] - g * sl[i, j]
+            psi[2][r - 1, j] = psi[2][r - 1, j] - g * sn[i, j]
             kx = k1[r, j] + k1[own, j]
-            ic = ic1[own - 1, j]
-            g = (g1[own - 1, j] + kx * (h0[r, j] - h0[own, j])) * ic
+            ic = edge[0, i, j]
+            d = h0[r, j] - h0[own, j]
+            g = (g1[own - 1, j] + kx * d) * ic
             g1[own - 1, j] = g
-            p1[own - 1, j] = g * p1[own - 1, j]
-            q1[own - 1, j] = g * q1[own - 1, j]
+            d = d * ic
+            psi[0][own - 1, j] = psi[0][own - 1, j] + d * k1[own, j]
+            psi[1][own - 1, j] = psi[1][own - 1, j] + d * kl1[own, j] - g * edge[1, i, j]
+            psi[2][own - 1, j] = psi[2][own - 1, j] + d * kn1[own, j] - g * edge[2, i, j]
+            for q, phi in enumerate((k1, kl1, kn1)):
+                psi[6 + q][own - 1, j] = d * phi[r, j]
             most = jnp.maximum(most, (part[i, j] + kx) * ic)
         return most
 
@@ -346,17 +420,13 @@
     spread[...] = jnp.broadcast_to(most[None], spread.shape)
 
 
-def second_kernel(
-    rates, pick, put, column, goal, h0, k1, kl1, kn1, ic1, g1, p1, q1, prm, zrel,
-    h1_out, g2, spread,
-    h1, k2, kl2, kn2, ic2, sl2, sn2, va, vb, wa, wb, w0, w1, w2, maps,
-):
+def second_kernel(rates, pick, put, column_in, goal, h0, g1, *rest):
+    psi, rest = rest[:9], rest[9:]
+    prm, zrel, h1_out, g2, spread, *rest = rest
+    h1, k2, kl2, kn2, ic2, sl2, sn2, va, vb, wa, wb, u0, u1, u2, maps, maps_f, maps_g = rest
     position = lax.axis_index("row")
     size = CFL / jnp.max(rates[...])
     nothing = jnp.zeros((TILES, SUB, WIDTH), F32)
-    for r in (0, ROWS - 1):
-        for ref in (w0, w1, w2):
-            ref[r] = nothing
     for r in (1, 6):
         for ref in (wa, wb):
             ref[r] = nothing
@@ -395,10 +465,11 @@
 
     most = jnp.max(lax.fori_loop(2, 6, flow, jnp.zeros((SUB, WIDTH), F32)))
 
+    column = column_in[...].astype(F32)
     field_g = g2[...].reshape(192, WIDTH)
     field_h = h1_out[...].reshape(192, WIDTH) + size * field_g
-    seen_h = jnp.sum(column[...] * exact_dot(pick[...], field_h), 1, keepdims=True)
-    seen_g = jnp.sum(column[...] * exact_dot(pick[...], field_g), 1, keepdims=True)
+    seen_h = jnp.sum(column * exact_dot(pick[...], field_h), 1, keepdims=True)
+    seen_g = jnp.sum(column * exact_dot(pick[...], field_g), 1, keepdims=True)
     diff = seen_h - goal[:, 0:1]
     events = 16.0
     loss = (
@@ -406,8 +477,8 @@
         jnp.sum(diff * seen_g) * (1.0 / events),
         jnp.sum(seen_g * seen_g) * (0.5 / events),
     )
-    va[...] = exact_dot(put[...], column[...] * (diff * (1.0 / events))).reshape(OWN)
-    vb[...] = exact_dot(put[...], column[...] * (seen_g * (1.0 / events))).reshape(OWN)
+    va[...] = exact_dot(put[...], column * (diff * (1.0 / events))).reshape(OWN)
+    vb[...] = exact_dot(put[...], column * (seen_g * (1.0 / events))).reshape(OWN)
 
     def scaled(r, carry):
         for j in range(TILES):
@@ -423,25 +494,19 @@
         flat = [jnp.sum(x, 0, keepdims=True) for x in sums]
         for q in range(3):
             of_a, of_b = flat[q], flat[3 + q]
-            rows = [size * of_a, of_a + size * of_b, of_b]
-            for c in range(3):
-                if q > 0:
-                    rows[c] = rows[c] - size * flat[6 + 2 * c + q - 1]
-                maps[r, 4 * q + c : 4 * q + c + 1, :] = rows[c]
-
-    def store_heads(r, j, back, sums):
+            for c, row in enumerate((size * of_a, of_a + size * of_b, of_b)):
+                maps[r - 1, 4 * q + c : 4 * q + c + 1, :] = row
+
+    def store_heads(r, j, back):
         (v_a, j_a), (v_b, j_b) = back
-        us = (v_a + size * j_a, v_b + j_a + size * j_b, j_b)
-        ic, pp, qq = ic1[r - 1, j], p1[r - 1, j], q1[r - 1, j]
-        for i, (u, w_ref) in enumerate(zip(us, (w0, w1, w2))):
-            w_ref[r, j] = u * ic
-            sums[6 + 2 * i] += u * pp
-            sums[7 + 2 * i] += u * qq
+        u0[r - 1, j] = v_a + size * j_a
+        u1[r - 1, j] = v_b + j_a + size * j_b
+        u2[r - 1, j] = j_b
 
     def edge_two(i, carry):
         r = 1 + 5 * i
         near = 2 + 3 * i
-        sums = [jnp.zeros((SUB, WIDTH), F32) for _ in range(12)]
+        sums = [jnp.zeros((SUB, WIDTH), F32) for _ in range(6)]
         for j in range(TILES):
             hj = h1[r, j]
             half = h1[near, j] - hj
@@ -457,7 +522,7 @@
                 sums[3 * part + 1] += to_l
                 sums[3 * part + 2] += gk * kn
                 back.append((0.0, gh + to_l * inv_h))
-            store_heads(r, j, back, sums)
+            store_heads(r, j, back)
         store_two(r, sums)
         return carry
 
@@ -465,7 +530,7 @@
         top = prm[r, LEV1 : LEV1 + 1, :]
         hs = [h1[r, j] for j in range(TILES)]
         ks = [k2[r, j] for j in range(TILES)]
-        sums = [jnp.zeros((SUB, WIDTH), F32) for _ in range(12)]
+        sums = [jnp.zeros((SUB, WIDTH), F32) for _ in range(6)]
         ws = [[w[r, j] for j in range(TILES)] for w in (wa, wb)]
 
         def face(j):
@@ -517,7 +582,7 @@
                 sums[3 * part + 1] += to_l
                 sums[3 * part + 2] += gk * kn - v * gn
                 back.append((v, gh + (to_l + v * g) * inv_h))
-            store_heads(r, j, back, sums)
+            store_heads(r, j, back)
             above = below
         store_two(r, sums)
         return carry
@@ -525,77 +590,44 @@
     lax.fori_loop(0, 2, edge_two, 0)
     lax.fori_loop(2, 6, back_two, 0)
 
-    refs = (w0, w1, w2)
-
-    def store_one(r, sums, first):
-        inv_k, inv_a = prm[r, IKS : IKS + 1, :], prm[r, IAL : IAL + 1, :]
+    for ref in (maps, maps_f, maps_g):
+        for r in range(6):
+            for at in (3, 7, 11):
+                ref[r, at : at + 1, :] = jnp.zeros((1, WIDTH), F32)
+            ref[r, 12:16, :] = jnp.zeros((4, WIDTH), F32)
+
+    def first_part(r, carry):
         for q in range(3):
+            sums = [[jnp.zeros((SUB, WIDTH), F32) for _ in range(3)] for _ in range(3)]
+            for j in range(TILES):
+                us = [ref[r, j] for ref in (u0, u1, u2)]
+                for kind in range(3):
+                    factor = psi[3 * kind + q][r, j]
+                    for c in range(3):
+                        sums[kind][c] += us[c] * factor
             for c in range(3):
                 at = 4 * q + c
-                row = size * jnp.sum(sums[3 * c + q], 0, keepdims=True)
-                if not first:
-                    row = row + maps[r, at : at + 1, :]
-                maps[r, at : at + 1, :] = row if q == 2 else row * (inv_k if q == 0 else inv_a)
-
-    def edge_one(i, carry):
-        r = 7 * i
-        near = 1 + 5 * i
-        sums = [jnp.zeros((SUB, WIDTH), F32) for _ in range(9)]
-        for j in range(TILES):
-            half = h0[r, j] - h0[near, j]
-            kj, kl, kn = k1[r, j], kl1[r, j], kn1[r, j]
-            for part, w_ref in enumerate(refs):
-                gk = half * w_ref[near, j]
-                sums[3 * part] += gk * kj
-                sums[3 * part + 1] += gk * kl
-                sums[3 * part + 2] += gk * kn
-        store_one(r, sums, True)
-        return carry
-
-    def back_one(r, carry):
-        top = prm[r, LEV0 : LEV0 + 1, :]
-        hs = [h0[r, j] for j in range(TILES)]
-        ws = [[w[r, j] for j in range(TILES)] for w in refs]
-        sums = [jnp.zeros((SUB, WIDTH), F32) for _ in range(9)]
-
-        def face(j):
-            if j < TILES - 1:
-                half = 1.0 + hs[j] - hs[j + 1]
-                return [half * (w[j + 1] - w[j]) for w in ws]
-            half = 1.0 + hs[j] - subs_up(hs[0])
-            return [jnp.where(is_bottom, -2.0 * w[j], half * (subs_up(w[0]) - w[j])) for w in ws]
-
-        final = face(TILES - 1)
-        above = [jnp.where(is_top, top * w[0], subs_down(f)) for w, f in zip(ws, final)]
-        for j in range(TILES):
-            below = final if j == TILES - 1 else face(j)
-            hj = hs[j]
-            half_c = jnp.where(last, 0.0, lanes_left(hj) - hj)
-            half_l, half_h = h0[r - 1, j] - hj, h0[r + 1, j] - hj
-            kj, kl, kn = k1[r, j], kl1[r, j], kn1[r, j]
-            for part, w_ref in enumerate(refs):
-                w = ws[part][j]
-                e = half_c * (w - lanes_left(w))
-                gk = e + lanes_right(e) + below[part] + above[part]
-                gk = gk + half_l * (w - w_ref[r - 1, j]) + half_h * (w - w_ref[r + 1, j])
-                sums[3 * part] += gk * kj
-                sums[3 * part + 1] += gk * kl
-                sums[3 * part + 2] += gk * kn
-            above = below
-        store_one(r, sums, False)
-        return carry
-
-    for r in range(ROWS):
-        for at in (3, 7, 11):
-            maps[r, at : at + 1, :] = jnp.zeros((1, WIDTH), F32)
-        maps[r, 12:16, :] = jnp.zeros((4, WIDTH), F32)
-    lax.fori_loop(0, 2, edge_one, 0)
-    lax.fori_loop(1, 7, back_one, 0)
-
-    left = jnp.concatenate([maps[r] for r in range(ROWS)], 1)
+                own, column_off, row_off = (jnp.sum(sums[kind][c], 0, keepdims=True) for kind in range(3))
+                maps[r, at : at + 1, :] = maps[r, at : at + 1, :] + size * own
+                maps_f[r, at : at + 1, :] = size * column_off
+                maps_g[r, at : at + 1, :] = size * row_off
+        return carry
+
+    lax.fori_loop(0, 6, first_part, 0)
+
+    odd = iota((16, WIDTH), 1) % 2 == 1
+    which = iota((16, WIDTH), 0)
+    pieces = []
+    for r in range(6):
+        off = maps_f[r]
+        off = jnp.where(odd, lanes_left(off), lanes_right(off))
+        other = r + 1 if r % 2 == 0 else r - 1
+        scale = jnp.where(which < 4, prm[r + 1, IKS : IKS + 1, :], jnp.where(which < 8, prm[r + 1, IAL : IAL + 1, :], 1.0))
+        pieces.append((maps[r] + off + maps_g[other]) * scale)
+    left = jnp.concatenate(pieces, 1)
     near = zrel[...]
     zone_id = iota((32, WIDTH), 0)
-    onehot = jnp.concatenate([(zone_id == near[r : r + 1, :]).astype(F32) for r in range(ROWS)], 1)
+    onehot = jnp.concatenate([(zone_id == near[r : r + 1, :]).astype(F32) for r in range(1, 7)], 1)
     onehot = onehot.astype(jnp.bfloat16)
     nt = (((1,), (1,)), ((), ()))
     parts = [lax.dot_general(part, onehot, nt, preferred_element_type=F32) for part in split3(left)]
@@ -674,7 +706,7 @@
 SMEM = pl.BlockSpec(memory_space=pltpu.SMEM)
 
 
-def call(kernel, name, ins, outs, out_specs=None, scratch=(), cost=None, in_place=None):
+def call(kernel, name, ins, outs, out_specs=None, scratch=(), cost=None, in_place=None, room=8):
     return pl.pallas_call(
         kernel,
         name=name,
@@ -684,7 +716,7 @@
         scratch_shapes=scratch,
         cost_estimate=cost,
         input_output_aliases=in_place or {},
-        compiler_params=pltpu.CompilerParams(vmem_limit_bytes=32 * 1024 * 1024),
+        compiler_params=pltpu.CompilerParams(vmem_limit_bytes=room * 1024 * 1024),
     )
 
 
@@ -718,36 +750,42 @@
     got_odd = lax.ppermute(send_odd, "row", odd + [(j, i) for i, j in odd])
     got_even = lax.ppermute(send_even, "row", even + [(j, i) for i, j in even])
     wide = (6, TILES, SUB, WIDTH)
-    fields = [(FIELD, F32)] * 3 + [(wide, F32)] * 4 + [((ROWS, 16, WIDTH), F32)]
+    fields = [(wide, F32)] * 10 + [((ROWS, 16, WIDTH), F32)]
+    pair = (2, TILES, SUB, WIDTH)
+    whole = [pltpu.VMEM(FIELD, F32)] * 3 + [pltpu.VMEM(wide, F32)]
     seen = tensiometer_cells.shape[1]
     own = call(
         own_kernel,
         "own_cells",
         [SMEM] * 4 + [VMEM] * 4,
         fields
-        + [((2, TILES, SUB, WIDTH), F32), ((SUB, WIDTH), F32), ((SUB, 128), F32)]
-        + [((seen, 192), jnp.bfloat16), ((192, seen), jnp.bfloat16), ((seen, WIDTH), F32), ((seen, 128), F32)],
+        + [((SUB, WIDTH), F32), ((SUB, 128), F32)]
+        + [((seen, 192), jnp.bfloat16), ((192, seen), jnp.bfloat16), ((seen, WIDTH), jnp.bfloat16), ((seen, 128), F32)],
+        scratch=whole + [pltpu.VMEM(wide, F32)] * 2,
         cost=pl.CostEstimate(flops=200_000_000, bytes_accessed=8_000_000, transcendentals=600_000),
     )(sat_conductivity, vg_alpha, vg_n, plan, h0, zones, tensiometer_cells, tensiometer_heads)
-    own_fields, (part, most, near), sensors = own[:8], own[8:11], own[11:]
+    own_fields, (most, near), sensors = own[:11], own[11:13], own[13:]
     first = call(
         first_kernel,
         "first_step",
-        [VMEM] * 15,
+        [VMEM] * 17,
         [(FIELD, F32)] + fields + [((ROWS, WIDTH), jnp.int32), ((32, 1, 128), F32)],
-        in_place={6 + i: i for i in range(9)},
-    )(near, zones, part, most, got_odd, got_even, h0, *own_fields)
+        scratch=whole + [pltpu.VMEM(pair, F32)] * 3 + [pltpu.VMEM((3, *pair), F32)],
+        in_place={5 + i: i for i in range(12)},
+    )(near, zones, most, got_odd, got_even, h0, *own_fields)
     fields, rates = first[:-1], first[-1]
     rates = lax.all_to_all(rates, "row", 0, 0, tiled=True)
     h1, g2, sums = call(
         second_kernel,
         "second_step_and_adjoint",
-        [VMEM] * 15,
+        [VMEM] * 18,
         [(OWN, F32), (OWN, F32), ((16, 4, 128), F32)],
         scratch=[pltpu.VMEM(FIELD, F32)] * 4
         + [pltpu.VMEM(OWN, F32)] * 5
-        + [pltpu.VMEM(FIELD, F32)] * 5
-        + [pltpu.VMEM((ROWS, 16, WIDTH), F32)],
+        + [pltpu.VMEM(FIELD, F32)] * 2
+        + [pltpu.VMEM(wide, F32)] * 3
+        + [pltpu.VMEM((6, 16, WIDTH), F32)] * 3,
+        room=20,
     )(rates, *sensors, *fields)
     sums = lax.all_to_all(sums, ("event", "row"), 0, 0, tiled=True, axis_index_groups=RINGS)
     (sums,) = call(ring_kernel, "ring_sums", [VMEM], [((32, 1, 6 * 256), F32)])(sums)

time: 94.5 us -> 93.7 us (level)
  blocking collectives: 69.1 us -> 68.1 us
    all_to_all x1, blocking collectives: 30.2 us -> 29.2 us  [local(): rates = lax.all_to_all(rates, 'row', 0, 0, tiled=True)]
  transfers between devices with their start and end apart: 2 -> 2, of which waited for: 0 -> 0; matrix products, arithmetic and copies ran while one was open for 0% -> 0% of each run, Pallas kernels for 3% -> 4%
where the time goes in v3:
time: 93.7 us; the launch traced here: 93.3 us
  blocking collectives  68.1 us (73%)
  Pallas kernels  14.1 us (15%)
  starting transfers between devices  8.05 us (9%)
  local copies, waits for them, and re-layouts  2.3 us (2%)
    all_to_all x2, blocking collectives, local(): lax.all_to_all(sums, ('event', 'row'), 0, 0, tiled=True, axis_index_group...  38.9 us
    all_to_all x1, blocking collectives, local(): rates = lax.all_to_all(rates, 'row', 0, 0, tiled=True)  29.2 us
    ppermute x1, starting transfers between devices, local(): got_even = lax.ppermute(send_even, 'row', even + [(j, i) for i, j in even])  7.38 us
    pallas_call x1, Pallas kernels, local(): call(second_kernel, 'second_step_and_adjoint', [VMEM] * 18, [(OWN, F32),...  7.02 us
    pallas_call x1, Pallas kernels, local(): call(own_kernel, 'own_cells', [SMEM] * 4 + [VMEM] * 4, fields + [((SUB, W...  3.53 us
    unnamed x16, local copies, waits for them, and re-layouts  2.3 us
  transfers between devices with their start and end apart: 2, of which 0 were waited for; matrix products, arithmetic and copies ran while one was open for 0% of the time, Pallas kernels for 4%

profile of v3, /device:TPU:1, one launch (start us, length us, event | category | flops | bytes accessed | tf_op | source)
XLA Modules:
  0.0 93.3 jit_solution(3578742597892372700)
XLA Ops:
  0.6 0.0 copy-start.1
  0.6 0.0 copy-start.2
  0.7 0.7 copy-done.1
  1.3 0.0 copy-done.2
  1.3 1.0 %copy-done = f32[1,48,4,384]{3,2,1,0:T(4,128)S(1)} copy-done((f32[1,48,4,384]{3,2,1,0:T(4,128)S(1)}, f32[1,48,4,384]{3,2,1,0:T(4,128)}, u32[]{:S(2)}) %copy-start) | copy-done | bytes 294936
  2.3 0.4 pack_edges.1
  2.7 0.7 collective-permute-start
  3.4 0.0 copy-start.4
  3.4 0.0 copy-start.5
  3.4 0.0 copy-start.6
  3.5 0.0 copy-start.7
  3.5 7.4 %collective-permute-start.1 = (f32[13,8,384]{2,1,0:T(8,128)S(1)}, f32[13,8,384]{2,1,0:T(8,128)S(1)}, u32[]{:S(2)}, u32[]{:S(2)}) collective-permute-start(f32[13,8,384]{2,1,0:T(8,128)S(1)} %get-tuple-element.53), channel_id=1, source_target_pairs={{0,1},{2,3},{4,5},{6,7},{8,9},{10,11},{12,13},{14,15},{16,17},{18,... | collective-permute-start | bytes 479240 | tf_op jit(solution)/shard_map/ppermute | solution.py:751
  10.9 0.0 copy-start.3
  10.9 0.6 copy-done.3
  11.5 3.5 %own_cells.1 = (f32[6,6,8,384]{3,2,1,0:T(8,128)S(1)}, f32[6,6,8,384]{3,2,1,0:T(8,128)S(1)}, f32[6,6,8,384]{3,2,1,0:T(8,128)S(1)}, f32[6,6,8,384]{3,2,1,0:T(8,128...) custom-call(f32[256]{0:T(256)S(1)} %copy-done.3, ...), custom_call_target="tpu_custom_call" | custom-call | flops 200000000 | bytes 8000000 | tf_op jit(solution)/shard_map/own_cells/pallas_call | solution.py:757
  15.1 0.0 collective-permute-done.got_odd
  15.1 0.0 collective-permute-done.1.got_even
  15.1 1.8 %first_step.1 = (f32[8,6,8,384]{3,2,1,0:T(8,128)S(1)}, f32[6,6,8,384]{3,2,1,0:T(8,128)S(1)}, f32[6,6,8,384]{3,2,1,0:T(8,128)S(1)}, f32[6,6,8,384]{3,2,1,0:T(8,12...) custom-call(f32[8,128]{1,0:T(8,128)S(1)} %get-tuple-element.50.near,, ...), custom_call_target="tpu_custom_call", output_to_operand_aliasing={{0}: (5, {}), {1}: (6, {}), {2}: (7, {}), {3}: (8, {}), {4}... | custom-call | tf_op jit(solution)/shard_map/first_step/pallas_call | solution.py:768
  16.9 29.2 %all_to_all.15.rates = f32[32,1,128]{2,1,0:T(1,128)S(1)} all-to-all(f32[32,1,128]{2,1,0:T(1,128)S(1)} %get-tuple-element.65), channel_id=1, replica_groups=mesh['event'=16,'row'=32] {'row'}, dimensions={0} | all-to-all | bytes 32768 | tf_op jit(solution)/shard_map/all_to_all | solution.py:777
  46.1 7.0 %second_step_and_adjoint.1 = (f32[4,6,8,384]{3,2,1,0:T(8,128)S(1)}, f32[4,6,8,384]{3,2,1,0:T(8,128)S(1)}, f32[16,4,128]{2,1,0:T(4,128)S(1)}) custom-call(f32[32,1,128]{2,1,0:T(1,128)S(1)} %all_to_all.15.rates, bf16[256,192]{1,0:T(8,128)(2,1)S(1)} %get-tuple-element.66.pick, bf16[192,256]{1,0:T(8,128)(2,1)S(1)} %get-tuple-element.67.put, ...), custom_call_target="tpu_custom_call" | custom-call | tf_op jit(solution)/shard_map/second_step_and_adjoint/pallas_call | solution.py:778
  53.1 22.4 %all_to_all.16.parts = f32[16,4,128]{2,1,0:T(4,128)S(1)} all-to-all(f32[16,4,128]{2,1,0:T(4,128)S(1)} %get-tuple-element.83), channel_id=1, replica_groups={{0,1,2,3,4,5,6,7,64,65,66,67,68,69,70,71},{8,9,10,11,12,13,14,15,72,73,..., dimensions={0} | all-to-all | bytes 65536 | tf_op jit(solution)/shard_map/all_to_all | solution.py:790
  75.5 0.1 ring_sums.1
  75.7 16.5 %all_to_all.17.parts = f32[32,1,1536]{2,1,0:T(1,128)S(1)} all-to-all(f32[32,1,1536]{2,1,0:T(1,128)S(1)} %ring_sums.1), channel_id=1, replica_groups={{0,32,128,160,256,288,384,416,8,40,136,168,264,296,392,424,16,48,144,17..., dimensions={0} | all-to-all | bytes 393216 | tf_op jit(solution)/shard_map/all_to_all | solution.py:792
  92.2 1.1 %final_head_and_sums.1 = (f32[48,4,384]{2,1,0:T(4,128)}, f32[1,256]{1,0:T(1,128)}, f32[1,256]{1,0:T(1,128)}, f32[1,256]{1,0:T(1,128)}, f32[1,1]{1,0:T(1,128)}) custom-call(f32[32,1,1536]{2,1,0:T(1,128)S(1)} %all_to_all.17.parts, f32[4,6,8,384]{3,2,1,0:T(8,128)S(1)} %get-tuple-element.84.h1, f32[4,6,8,384]{3,2,1,0:T(8,128)S(1)} %get-tuple-element.85.g2), custom_call_target="tpu_custom_call" | custom-call | tf_op jit(solution)/shard_map/final_head_and_sums/pallas_call | solution.py:794
  (5 shorter events, 0.0 us)
Async XLA Ops:
  0.6 0.7 copy-start.1
  0.6 0.7 copy-start.2
  1.3 1.0 %copy-start = (f32[1,48,4,384]{3,2,1,0:T(4,128)S(1)}, f32[1,48,4,384]{3,2,1,0:T(4,128)}, u32[]{:S(2)}) copy-start(f32[1,48,4,384]{3,2,1,0:T(4,128)} %param.8) | copy-start | bytes 884740
  2.7 12.3 %collective-permute-start = (f32[13,8,384]{2,1,0:T(8,128)S(1)}, f32[13,8,384]{2,1,0:T(8,128)S(1)}, u32[]{:S(2)}, u32[]{:S(2)}) collective-permute-start(f32[13,8,384]{2,1,0:T(8,128)S(1)} %get-tuple-element.52), channel_id=1, source_target_pairs={{1,2},{3,4},{5,6},{7,8},{9,10},{11,12},{13,14},{15,16},{17,18},{19... | collective-permute-start | bytes 479240 | tf_op jit(solution)/shard_map/ppermute | solution.py:750
  3.4 7.5 %copy-start.4 = (f32[256]{0:T(256)S(1)}, f32[256]{0:T(256)}, u32[]{:S(2)}) copy-start(f32[256]{0:T(256)} %tab_a.1) | copy-start | bytes 3076
  3.4 7.5 %copy-start.5 = (f32[256]{0:T(256)S(1)}, f32[256]{0:T(256)}, u32[]{:S(2)}) copy-start(f32[256]{0:T(256)} %tab_n.1) | copy-start | bytes 3076
  3.4 7.4 %copy-start.6 = (s32[1,256]{1,0:T(1,128)S(1)}, s32[1,256]{1,0:T(1,128)}, u32[]{:S(2)}) copy-start(s32[1,256]{1,0:T(1,128)} %cells_at.1) | copy-start | bytes 3076
  3.5 7.4 %copy-start.7 = (f32[1,256]{1,0:T(1,128)S(1)}, f32[1,256]{1,0:T(1,128)}, u32[]{:S(2)}) copy-start(f32[1,256]{1,0:T(1,128)} %goals.1) | copy-start | bytes 3076
  3.5 11.6 %collective-permute-start.1 = (f32[13,8,384]{2,1,0:T(8,128)S(1)}, f32[13,8,384]{2,1,0:T(8,128)S(1)}, u32[]{:S(2)}, u32[]{:S(2)}) collective-permute-start(f32[13,8,384]{2,1,0:T(8,128)S(1)} %get-tuple-element.53), channel_id=1, source_target_pairs={{0,1},{2,3},{4,5},{6,7},{8,9},{10,11},{12,13},{14,15},{16,17},{18,... | collective-permute-start | bytes 479240 | tf_op jit(solution)/shard_map/ppermute | solution.py:751
  10.9 0.7 copy-start.3

commit v4 on v3

--- a/solution.py
+++ b/solution.py
@@ -1,3 +1,5 @@
+import functools
+
 import jax
 import jax.numpy as jnp
 from jax import lax
@@ -155,7 +157,7 @@
     return last, sub == 0, sub == SUB - 1
 
 
-def net_row(h, k, r, top, beside):
+def net_row(h, k, r, top, beside, keep=None):
     last, is_top, is_bottom = masks()
     hs = [h[r, j] for j in range(TILES)]
     ks = [k[r, j] for j in range(TILES)]
@@ -177,7 +179,10 @@
         below = final if j == TILES - 1 else face(j)
         hj, kj = hs[j], ks[j]
         kf = jnp.where(last, 0.0, kj + lanes_left(kj))
-        flow = kf * (lanes_left(hj) - hj)
+        difference = jnp.where(last, 0.0, lanes_left(hj) - hj)
+        if keep is not None:
+            keep[0][r - 2, j], keep[1][r - 2, j] = kf, difference
+        flow = kf * difference
         net = flow - lanes_right(flow) + above[1] - below[1]
         total = kf + lanes_right(kf) + above[0] + below[0]
         for other in beside:
@@ -240,10 +245,12 @@
     g1, *rest,
 ):
     psi, rest = rest[:9], rest[9:]
-    prm, most_out, near, pick, put, column, goal, k1, kl1, kn1, ic1, p1, q1 = rest
+    prm, zrel, most_out, near, pick, put, column, goal, k1, kl1, kn1, ic1, p1, q1 = rest
     base = 8 * lax.axis_index("row") - 4
     sub = iota((SUB, WIDTH), 0)
     rel = (jnp.where(sub < 2, zones[0:1, :], zones[1:2, :]).astype(jnp.int32) - base) & (ZONES - 1)
+    for r in range(4):
+        zrel[2 + r : 3 + r, :] = rel[r : r + 1, :]
     sat = jnp.ones((SUB, WIDTH), F32)
     alpha, n = sat, 2.0 * sat
     lane = iota((SUB, 128), 1)
@@ -327,103 +334,71 @@
     goal[...] = jnp.broadcast_to(tall[:, 1:2], goal.shape)
 
 
-def first_kernel(
-    near, zones, most_in, got_odd, got_even, *rest
-):
-    h0, g1, *psi = rest[12:23]
-    prm, zrel, spread, k1, kl1, kn1, ic1, sl, sn, part, edge = rest[23:]
+def side_kernel(exchange, near, zones, most_in, got, *rest):
+    h0, g1, *psi = rest[13:24]
+    prm, zrel, result, k1, kl1, kn1, ic1, sl, sn, part, edge = rest[24:]
     position = lax.axis_index("row")
-    has_low, has_high = position > 0, position < lax.axis_size("row") - 1
-    odd = position % 2 == 1
+    side = position % 2 if exchange == "odd" else 1 - position % 2
+    real = jnp.where(side == 0, position > 0, position < lax.axis_size("row") - 1)
+    far, r, own = 7 * side, 1 + 5 * side, 2 + 3 * side
     for row in range(2):
         for j in range(TILES):
-            at = row * TILES + j
-            one, other = got_odd[at], got_even[at]
-            h0[row, j] = jnp.where(has_low, jnp.where(odd, other, one), h0[2, j])
-            h0[6 + row, j] = jnp.where(has_high, jnp.where(odd, one, other), h0[5, j])
-    for i in range(2):
-        part[i] = g1[5 * i]
-        for at, phi in enumerate((k1, kl1, kn1)):
-            phi[2 + 3 * i] = psi[at][5 * i]
-            edge[at, i] = psi[3 + at][5 * i]
-    one, other = got_odd[2 * TILES], got_even[2 * TILES]
-    extra_low, extra_high = jnp.where(odd, other, one), jnp.where(odd, one, other)
-    z_low = jnp.where(has_low, extra_low[0:1, :], zones[0:1, :])
-    z_high = jnp.where(has_high, extra_high[0:1, :], zones[1:2, :])
-    sub = iota((SUB, WIDTH), 0)
-    zone = jnp.where(
-        sub < 4,
-        jnp.where(sub < 2, z_low, zones[0:1, :]),
-        jnp.where(sub < 6, zones[1:2, :], z_high),
-    ).astype(jnp.int32)
-    rel = (zone - (8 * position - 4)) & (ZONES - 1)
-    zrel[...] = rel
-    ids = iota((32, WIDTH), 0)
-    sides = []
-    for r in (0, 7):
-        here = (ids == rel[r : r + 1, :]).astype(F32).astype(jnp.bfloat16)
-        parts = [jnp.dot(x, here, preferred_element_type=F32) for x in split3(near[:, :32])]
-        sides.append(parts[0] + (parts[1] + parts[2]))
-    sat, alpha, n = (
-        jnp.where(sub < 4, sides[0][i : i + 1, :], sides[1][i : i + 1, :]) for i in range(3)
-    )
-    level = 2.0 * IRRIGATION * jnp.where(sub < 4, extra_low[1:2, :], extra_high[1:2, :])
+            h0[6 * side + row, j] = jnp.where(real, got[row * TILES + j], h0[own, j])
+    part[...] = g1[5 * side]
+    for at, phi in enumerate((k1, kl1, kn1)):
+        phi[own] = psi[at][5 * side]
+        edge[at] = psi[3 + at][5 * side]
+    extra = got[2 * TILES]
+    zone = jnp.where(real, extra[0:1, :], jnp.where(side == 0, zones[0:1, :], zones[1:2, :]))
+    rel = (zone.astype(jnp.int32) - (8 * position - 4)) & (ZONES - 1)
+    zrel[...] = jnp.where(iota((SUB, WIDTH), 0) // 2 == 3 * side, rel, zrel[...])
+    here = (iota((32, WIDTH), 0) == rel).astype(F32).astype(jnp.bfloat16)
+    parts = [jnp.dot(x, here, preferred_element_type=F32) for x in split3(near[:, :32])]
+    values = parts[0] + (parts[1] + parts[2])
+    sat, alpha, n = (values[i : i + 1, :] for i in range(3))
+    level = 2.0 * IRRIGATION * extra[1:2, :]
     for i, value in enumerate(derived(sat, alpha, n) + (level, level, 1.0 / sat, 1.0 / alpha)):
-        for r in (0, 1, 6, 7):
-            prm[r, i : i + 1, :] = value[r : r + 1, :]
-
-    def outer(i, carry):
-        r = 7 * i
-        p = row_params(prm, r)
-        for j in range(TILES):
-            k1[r, j], kl1[r, j], kn1[r, j] = cell_math(h0[r, j], p, False)
-        return carry
-
-    def inner(i, carry):
-        r, own = 1 + 5 * i, 2 + 3 * i
-        real = jnp.where(i == 0, has_low, has_high)
-        p = row_params(prm, r)
-        for j in range(TILES):
-            cond, kl1[r, j], kn1[r, j], ic1[r - 1, j], sl[i, j], sn[i, j] = cell_math(h0[r, j], p)
-            k1[r, j] = jnp.where(real, cond, -k1[own, j])
-        return carry
-
-    lax.fori_loop(0, 2, outer, 0)
-    lax.fori_loop(0, 2, inner, 0)
-
-    def flow(i, most):
-        r, own = 1 + 5 * i, 2 + 3 * i
-        real = jnp.where(i == 0, has_low, has_high)
-        reach_row(h0, (k1, kl1, kn1), ic1, psi, r, 7 * i, own, prm[r, LEV0 : LEV0 + 1, :])
-        for j, net, _ in net_row(h0, k1, r, prm[r, LEV0 : LEV0 + 1, :], (r - 1, r + 1)):
-            g = jnp.where(real, net * ic1[r - 1, j], 0.0)
-            g1[r - 1, j] = g
-            psi[1][r - 1, j] = psi[1][r - 1, j] - g * sl[i, j]
-            psi[2][r - 1, j] = psi[2][r - 1, j] - g * sn[i, j]
-            kx = k1[r, j] + k1[own, j]
-            ic = edge[0, i, j]
-            d = h0[r, j] - h0[own, j]
-            g = (g1[own - 1, j] + kx * d) * ic
-            g1[own - 1, j] = g
-            d = d * ic
-            psi[0][own - 1, j] = psi[0][own - 1, j] + d * k1[own, j]
-            psi[1][own - 1, j] = psi[1][own - 1, j] + d * kl1[own, j] - g * edge[1, i, j]
-            psi[2][own - 1, j] = psi[2][own - 1, j] + d * kn1[own, j] - g * edge[2, i, j]
-            for q, phi in enumerate((k1, kl1, kn1)):
-                psi[6 + q][own - 1, j] = d * phi[r, j]
-            most = jnp.maximum(most, (part[i, j] + kx) * ic)
-        return most
-
-    most = lax.fori_loop(0, 2, flow, most_in[...])
-    most = jnp.maximum(jnp.maximum(most[:, :128], most[:, 128:256]), most[:, 256:])
-    most = jnp.max(most, 0, keepdims=True)
-    spread[...] = jnp.broadcast_to(most[None], spread.shape)
+        for row in range(2):
+            prm[6 * side + row, i : i + 1, :] = value
+
+    p = row_params(prm, far)
+    for j in range(TILES):
+        k1[far, j], kl1[far, j], kn1[far, j] = cell_math(h0[far, j], p, False)
+        cond, kl1[r, j], kn1[r, j], ic1[r - 1, j], sl[j], sn[j] = cell_math(h0[r, j], p)
+        k1[r, j] = jnp.where(real, cond, -k1[own, j])
+
+    phis = (k1, kl1, kn1)
+    most = most_in[...]
+    reach_row(h0, phis, ic1, psi, r, far, own, prm[r, LEV0 : LEV0 + 1, :])
+    for j, net, _ in net_row(h0, k1, r, prm[r, LEV0 : LEV0 + 1, :], (far, own)):
+        g = jnp.where(real, net * ic1[r - 1, j], 0.0)
+        g1[r - 1, j] = g
+        psi[1][r - 1, j] = psi[1][r - 1, j] - g * sl[j]
+        psi[2][r - 1, j] = psi[2][r - 1, j] - g * sn[j]
+        kx = k1[r, j] + k1[own, j]
+        ic = edge[0, j]
+        d = h0[r, j] - h0[own, j]
+        g = (g1[own - 1, j] + kx * d) * ic
+        g1[own - 1, j] = g
+        d = d * ic
+        psi[0][own - 1, j] = psi[0][own - 1, j] + d * k1[own, j]
+        psi[1][own - 1, j] = psi[1][own - 1, j] + d * kl1[own, j] - g * edge[1, j]
+        psi[2][own - 1, j] = psi[2][own - 1, j] + d * kn1[own, j] - g * edge[2, j]
+        for q, phi in enumerate(phis):
+            psi[6 + q][own - 1, j] = d * phi[r, j]
+        most = jnp.maximum(most, (part[j] + kx) * ic)
+    if exchange == "odd":
+        result[...] = most
+    else:
+        most = jnp.maximum(jnp.maximum(most[:, :128], most[:, 128:256]), most[:, 256:])
+        most = jnp.max(most, 0, keepdims=True)
+        result[...] = jnp.broadcast_to(most[None], result.shape)
 
 
 def second_kernel(rates, pick, put, column_in, goal, h0, g1, *rest):
     psi, rest = rest[:9], rest[9:]
     prm, zrel, h1_out, g2, spread, *rest = rest
-    h1, k2, kl2, kn2, ic2, sl2, sn2, va, vb, wa, wb, u0, u1, u2, maps, maps_f, maps_g = rest
+    h1, k2, kl2, kn2, ic2, sl2, sn2, va, vb, kfs, dfs, wa, wb, u0, u1, u2, maps, maps_f, maps_g = rest
     position = lax.axis_index("row")
     size = CFL / jnp.max(rates[...])
     nothing = jnp.zeros((TILES, SUB, WIDTH), F32)
@@ -457,7 +432,7 @@
     lax.fori_loop(0, 2, edge_cells, 0)
 
     def flow(r, most):
-        for j, net, total in net_row(h1, k2, r, prm[r, LEV1 : LEV1 + 1, :], (r - 1, r + 1)):
+        for j, net, total in net_row(h1, k2, r, prm[r, LEV1 : LEV1 + 1, :], (r - 1, r + 1), (kfs, dfs)):
             ic = ic2[r - 2, j]
             g2[r - 2, j] = net * ic
             most = jnp.maximum(most, total * ic)
@@ -488,7 +463,7 @@
         return carry
 
     lax.fori_loop(2, 6, scaled, 0)
-    last, is_top, is_bottom = masks()
+    _, is_top, is_bottom = masks()
 
     def store_two(r, sums):
         flat = [jnp.sum(x, 0, keepdims=True) for x in sums]
@@ -558,8 +533,7 @@
         for j in range(TILES):
             below = final if j == TILES - 1 else face(j)
             hj, kj = hs[j], ks[j]
-            half_c = jnp.where(last, 0.0, lanes_left(hj) - hj)
-            kf = jnp.where(last, 0.0, lanes_left(kj) + kj)
+            kf, half_c = kfs[r - 2, j], dfs[r - 2, j]
             half_l, half_h = h1[r - 1, j] - hj, h1[r + 1, j] - hj
             k_low, k_high = k2[r - 1, j] + kj, k2[r + 1, j] + kj
             kl, kn = kl2[r, j], kn2[r, j]
@@ -750,8 +724,7 @@
     got_odd = lax.ppermute(send_odd, "row", odd + [(j, i) for i, j in odd])
     got_even = lax.ppermute(send_even, "row", even + [(j, i) for i, j in even])
     wide = (6, TILES, SUB, WIDTH)
-    fields = [(wide, F32)] * 10 + [((ROWS, 16, WIDTH), F32)]
-    pair = (2, TILES, SUB, WIDTH)
+    fields = [(wide, F32)] * 10 + [((ROWS, 16, WIDTH), F32), ((ROWS, WIDTH), jnp.int32)]
     whole = [pltpu.VMEM(FIELD, F32)] * 3 + [pltpu.VMEM(wide, F32)]
     seen = tensiometer_cells.shape[1]
     own = call(
@@ -764,16 +737,18 @@
         scratch=whole + [pltpu.VMEM(wide, F32)] * 2,
         cost=pl.CostEstimate(flops=200_000_000, bytes_accessed=8_000_000, transcendentals=600_000),
     )(sat_conductivity, vg_alpha, vg_n, plan, h0, zones, tensiometer_cells, tensiometer_heads)
-    own_fields, (most, near), sensors = own[:11], own[11:13], own[13:]
-    first = call(
-        first_kernel,
-        "first_step",
-        [VMEM] * 17,
-        [(FIELD, F32)] + fields + [((ROWS, WIDTH), jnp.int32), ((32, 1, 128), F32)],
-        scratch=whole + [pltpu.VMEM(pair, F32)] * 3 + [pltpu.VMEM((3, *pair), F32)],
-        in_place={5 + i: i for i in range(12)},
-    )(near, zones, most, got_odd, got_even, h0, *own_fields)
-    fields, rates = first[:-1], first[-1]
+    held, (most, near), sensors = (h0, *own[:12]), own[12:14], own[14:]
+    row = (TILES, SUB, WIDTH)
+    for exchange, got, result in (("odd", got_odd, (SUB, WIDTH)), ("even", got_even, (32, 1, 128))):
+        *held, most = call(
+            functools.partial(side_kernel, exchange),
+            "first_step_" + exchange,
+            [VMEM] * 17,
+            [(FIELD, F32)] + fields + [(result, F32)],
+            scratch=whole + [pltpu.VMEM(row, F32)] * 3 + [pltpu.VMEM((3, *row), F32)],
+            in_place={4 + i: i for i in range(13)},
+        )(near, zones, most, got, *held)
+    fields, rates = held, most
     rates = lax.all_to_all(rates, "row", 0, 0, tiled=True)
     h1, g2, sums = call(
         second_kernel,
@@ -781,7 +756,7 @@
         [VMEM] * 18,
         [(OWN, F32), (OWN, F32), ((16, 4, 128), F32)],
         scratch=[pltpu.VMEM(FIELD, F32)] * 4
-        + [pltpu.VMEM(OWN, F32)] * 5
+        + [pltpu.VMEM(OWN, F32)] * 7
         + [pltpu.VMEM(FIELD, F32)] * 2
         + [pltpu.VMEM(wide, F32)] * 3
         + [pltpu.VMEM((6, 16, WIDTH), F32)] * 3,

time: 93.7 us -> 92.5 us (0.987)
  transfers between devices with their start and end apart: 2 -> 2, of which waited for: 0 -> 0; matrix products, arithmetic and copies ran while one was open for 0% -> 0% of each run, Pallas kernels for 4% -> 5%
where the time goes in v4:
time: 92.5 us; the launch traced here: 92.2 us
  blocking collectives  67.2 us (73%)
  Pallas kernels  13.8 us (15%)
  starting transfers between devices  8.05 us (9%)
  local copies, waits for them, and re-layouts  2.3 us (2%)
    all_to_all x2, blocking collectives, local(): lax.all_to_all(sums, ('event', 'row'), 0, 0, tiled=True, axis_index_group...  38 us
    all_to_all x1, blocking collectives, local(): rates = lax.all_to_all(rates, 'row', 0, 0, tiled=True)  29.2 us
    ppermute x1, starting transfers between devices, local(): got_even = lax.ppermute(send_even, 'row', even + [(j, i) for i, j in even])  7.38 us
    pallas_call x1, Pallas kernels, local(): call(second_kernel, 'second_step_and_adjoint', [VMEM] * 18, [(OWN, F32),...  6.85 us
    pallas_call x1, Pallas kernels, local(): call(own_kernel, 'own_cells', [SMEM] * 4 + [VMEM] * 4, fields + [((SUB, W...  3.55 us
    unnamed x16, local copies, waits for them, and re-layouts  2.3 us
  transfers between devices with their start and end apart: 2, of which 0 were waited for; matrix products, arithmetic and copies ran while one was open for 0% of the time, Pallas kernels for 5%

profile of v4, /device:TPU:1, one launch (start us, length us, event | category | flops | bytes accessed | tf_op | source)
XLA Modules:
  0.0 92.2 jit_solution(10547770872238378172)
XLA Ops:
  0.6 0.0 copy-start.1
  0.7 0.7 copy-done.1
  1.3 0.0 copy-done.2
  1.3 1.0 %copy-done = f32[1,48,4,384]{3,2,1,0:T(4,128)S(1)} copy-done((f32[1,48,4,384]{3,2,1,0:T(4,128)S(1)}, f32[1,48,4,384]{3,2,1,0:T(4,128)}, u32[]{:S(2)}) %copy-start) | copy-done | bytes 294936
  2.3 0.4 pack_edges.1
  2.7 0.7 collective-permute-start
  3.4 0.0 copy-start.4
  3.4 0.0 copy-start.5
  3.4 0.0 copy-start.6
  3.5 0.0 copy-start.7
  3.5 7.4 %collective-permute-start.1 = (f32[13,8,384]{2,1,0:T(8,128)S(1)}, f32[13,8,384]{2,1,0:T(8,128)S(1)}, u32[]{:S(2)}, u32[]{:S(2)}) collective-permute-start(f32[13,8,384]{2,1,0:T(8,128)S(1)} %get-tuple-element.81), channel_id=1, source_target_pairs={{0,1},{2,3},{4,5},{6,7},{8,9},{10,11},{12,13},{14,15},{16,17},{18,... | collective-permute-start | bytes 479240 | tf_op jit(solution)/shard_map/ppermute | solution.py:725
  10.9 0.0 copy-start.3
  10.9 0.6 copy-done.3
  11.5 3.6 %own_cells.1 = (f32[6,6,8,384]{3,2,1,0:T(8,128)S(1)}, f32[6,6,8,384]{3,2,1,0:T(8,128)S(1)}, f32[6,6,8,384]{3,2,1,0:T(8,128)S(1)}, f32[6,6,8,384]{3,2,1,0:T(8,128...) custom-call(f32[256]{0:T(256)S(1)} %copy-done.3, ...), custom_call_target="tpu_custom_call" | custom-call | flops 200000000 | bytes 8000000 | tf_op jit(solution)/shard_map/own_cells/pallas_call | solution.py:730
  15.1 0.0 collective-permute-done.got
  15.1 0.8 first_step_odd.1
  15.9 0.0 collective-permute-done.1.got
  15.9 0.9 first_step_even.1
  16.8 29.2 %all_to_all.15.rates = f32[32,1,128]{2,1,0:T(1,128)S(1)} all-to-all(f32[32,1,128]{2,1,0:T(1,128)S(1)} %get-tuple-element.95), channel_id=1, replica_groups=mesh['event'=16,'row'=32] {'row'}, dimensions={0} | all-to-all | bytes 32768 | tf_op jit(solution)/shard_map/all_to_all | solution.py:752
  46.0 6.9 %second_step_and_adjoint.1 = (f32[4,6,8,384]{3,2,1,0:T(8,128)S(1)}, f32[4,6,8,384]{3,2,1,0:T(8,128)S(1)}, f32[16,4,128]{2,1,0:T(4,128)S(1)}) custom-call(f32[32,1,128]{2,1,0:T(1,128)S(1)} %all_to_all.15.rates, bf16[256,192]{1,0:T(8,128)(2,1)S(1)} %get-tuple-element.96.pick, bf16[192,256]{1,0:T(8,128)(2,1)S(1)} %get-tuple-element.97.put, ...), custom_call_target="tpu_custom_call" | custom-call | tf_op jit(solution)/shard_map/second_step_and_adjoint/pallas_call | solution.py:753
  52.8 21.5 %all_to_all.16.parts = f32[16,4,128]{2,1,0:T(4,128)S(1)} all-to-all(f32[16,4,128]{2,1,0:T(4,128)S(1)} %get-tuple-element.113), channel_id=1, replica_groups={{0,1,2,3,4,5,6,7,64,65,66,67,68,69,70,71},{8,9,10,11,12,13,14,15,72,73,..., dimensions={0} | all-to-all | bytes 65536 | tf_op jit(solution)/shard_map/all_to_all | solution.py:765
  74.3 0.1 ring_sums.1
  74.5 16.5 %all_to_all.17.parts = f32[32,1,1536]{2,1,0:T(1,128)S(1)} all-to-all(f32[32,1,1536]{2,1,0:T(1,128)S(1)} %ring_sums.1), channel_id=1, replica_groups={{0,32,128,160,256,288,384,416,8,40,136,168,264,296,392,424,16,48,144,17..., dimensions={0} | all-to-all | bytes 393216 | tf_op jit(solution)/shard_map/all_to_all | solution.py:767
  91.0 1.1 %final_head_and_sums.1 = (f32[48,4,384]{2,1,0:T(4,128)}, f32[1,256]{1,0:T(1,128)}, f32[1,256]{1,0:T(1,128)}, f32[1,256]{1,0:T(1,128)}, f32[1,1]{1,0:T(1,128)}) custom-call(f32[32,1,1536]{2,1,0:T(1,128)S(1)} %all_to_all.17.parts, f32[4,6,8,384]{3,2,1,0:T(8,128)S(1)} %get-tuple-element.114.h1, f32[4,6,8,384]{3,2,1,0:T(8,128)S(1)} %get-tuple-element.115.g2), custom_call_target="tpu_custom_call" | custom-call | tf_op jit(solution)/shard_map/final_head_and_sums/pallas_call | solution.py:769
  (6 shorter events, 0.0 us)
Async XLA Ops:
  0.6 0.7 copy-start.1
  0.6 0.7 copy-start.2
  1.3 1.0 %copy-start = (f32[1,48,4,384]{3,2,1,0:T(4,128)S(1)}, f32[1,48,4,384]{3,2,1,0:T(4,128)}, u32[]{:S(2)}) copy-start(f32[1,48,4,384]{3,2,1,0:T(4,128)} %param.8) | copy-start | bytes 884740
  2.7 12.4 %collective-permute-start = (f32[13,8,384]{2,1,0:T(8,128)S(1)}, f32[13,8,384]{2,1,0:T(8,128)S(1)}, u32[]{:S(2)}, u32[]{:S(2)}) collective-permute-start(f32[13,8,384]{2,1,0:T(8,128)S(1)} %get-tuple-element.67), channel_id=1, source_target_pairs={{1,2},{3,4},{5,6},{7,8},{9,10},{11,12},{13,14},{15,16},{17,18},{19... | collective-permute-start | bytes 479240 | tf_op jit(solution)/shard_map/ppermute | solution.py:724
  3.4 7.5 %copy-start.4 = (f32[256]{0:T(256)S(1)}, f32[256]{0:T(256)}, u32[]{:S(2)}) copy-start(f32[256]{0:T(256)} %tab_a.1) | copy-start | bytes 3076
  3.4 7.5 %copy-start.5 = (f32[256]{0:T(256)S(1)}, f32[256]{0:T(256)}, u32[]{:S(2)}) copy-start(f32[256]{0:T(256)} %tab_n.1) | copy-start | bytes 3076
  3.4 7.4 %copy-start.6 = (s32[1,256]{1,0:T(1,128)S(1)}, s32[1,256]{1,0:T(1,128)}, u32[]{:S(2)}) copy-start(s32[1,256]{1,0:T(1,128)} %cells_at.1) | copy-start | bytes 3076
  3.5 7.4 %copy-start.7 = (f32[1,256]{1,0:T(1,128)S(1)}, f32[1,256]{1,0:T(1,128)}, u32[]{:S(2)}) copy-start(f32[1,256]{1,0:T(1,128)} %goals.1) | copy-start | bytes 3076
  3.5 12.5 %collective-permute-start.1 = (f32[13,8,384]{2,1,0:T(8,128)S(1)}, f32[13,8,384]{2,1,0:T(8,128)S(1)}, u32[]{:S(2)}, u32[]{:S(2)}) collective-permute-start(f32[13,8,384]{2,1,0:T(8,128)S(1)} %get-tuple-element.81), channel_id=1, source_target_pairs={{0,1},{2,3},{4,5},{6,7},{8,9},{10,11},{12,13},{14,15},{16,17},{18,... | collective-permute-start | bytes 479240 | tf_op jit(solution)/shard_map/ppermute | solution.py:725
  10.9 0.7 copy-start.3

commit v5 on v4

--- a/solution.py
+++ b/solution.py
@@ -443,8 +443,9 @@
     column = column_in[...].astype(F32)
     field_g = g2[...].reshape(192, WIDTH)
     field_h = h1_out[...].reshape(192, WIDTH) + size * field_g
-    seen_h = jnp.sum(column * exact_dot(pick[...], field_h), 1, keepdims=True)
-    seen_g = jnp.sum(column * exact_dot(pick[...], field_g), 1, keepdims=True)
+    seen = exact_dot(pick[...], jnp.concatenate([field_h, field_g], 1))
+    seen_h = jnp.sum(column * seen[:, :WIDTH], 1, keepdims=True)
+    seen_g = jnp.sum(column * seen[:, WIDTH:], 1, keepdims=True)
     diff = seen_h - goal[:, 0:1]
     events = 16.0
     loss = (
@@ -452,8 +453,10 @@
         jnp.sum(diff * seen_g) * (1.0 / events),
         jnp.sum(seen_g * seen_g) * (0.5 / events),
     )
-    va[...] = exact_dot(put[...], column * (diff * (1.0 / events))).reshape(OWN)
-    vb[...] = exact_dot(put[...], column * (seen_g * (1.0 / events))).reshape(OWN)
+    parts = [column * (diff * (1.0 / events)), column * (seen_g * (1.0 / events))]
+    added = exact_dot(put[...], jnp.concatenate(parts, 1))
+    va[...] = added[:, :WIDTH].reshape(OWN)
+    vb[...] = added[:, WIDTH:].reshape(OWN)
 
     def scaled(r, carry):
         for j in range(TILES):

time: 92.5 us -> 92.7 us (level)
  no operation moved by 1% of the time
where the time goes in v5:
time: 92.7 us; the launch traced here: 92.4 us
  blocking collectives  67.2 us (72%)
  Pallas kernels  14 us (15%)
  starting transfers between devices  8.05 us (9%)
  local copies, waits for them, and re-layouts  2.3 us (2%)
    all_to_all x2, blocking collectives, local(): lax.all_to_all(sums, ('event', 'row'), 0, 0, tiled=True, axis_index_group...  38 us
    all_to_all x1, blocking collectives, local(): rates = lax.all_to_all(rates, 'row', 0, 0, tiled=True)  29.2 us
    ppermute x1, starting transfers between devices, local(): got_even = lax.ppermute(send_even, 'row', even + [(j, i) for i, j in even])  7.38 us
    pallas_call x1, Pallas kernels, local(): call(second_kernel, 'second_step_and_adjoint', [VMEM] * 18, [(OWN, F32),...  7.05 us
    pallas_call x1, Pallas kernels, local(): call(own_kernel, 'own_cells', [SMEM] * 4 + [VMEM] * 4, fields + [((SUB, W...  3.55 us
    unnamed x16, local copies, waits for them, and re-layouts  2.3 us
  transfers between devices with their start and end apart: 2, of which 0 were waited for; matrix products, arithmetic and copies ran while one was open for 0% of the time, Pallas kernels for 5%

profile of v5, /device:TPU:1, one launch (start us, length us, event | category | flops | bytes accessed | tf_op | source)
XLA Modules:
  0.0 92.4 jit_solution(16428875797172085907)
XLA Ops:
  0.6 0.0 copy-start.1
  0.7 0.7 copy-done.1
  1.3 0.0 copy-done.2
  1.3 1.0 %copy-done = f32[1,48,4,384]{3,2,1,0:T(4,128)S(1)} copy-done((f32[1,48,4,384]{3,2,1,0:T(4,128)S(1)}, f32[1,48,4,384]{3,2,1,0:T(4,128)}, u32[]{:S(2)}) %copy-start) | copy-done | bytes 294936
  2.3 0.4 pack_edges.1
  2.7 0.7 collective-permute-start
  3.4 0.0 copy-start.4
  3.4 0.0 copy-start.5
  3.4 0.0 copy-start.6
  3.5 0.0 copy-start.7
  3.5 7.4 %collective-permute-start.1 = (f32[13,8,384]{2,1,0:T(8,128)S(1)}, f32[13,8,384]{2,1,0:T(8,128)S(1)}, u32[]{:S(2)}, u32[]{:S(2)}) collective-permute-start(f32[13,8,384]{2,1,0:T(8,128)S(1)} %get-tuple-element.81), channel_id=1, source_target_pairs={{0,1},{2,3},{4,5},{6,7},{8,9},{10,11},{12,13},{14,15},{16,17},{18,... | collective-permute-start | bytes 479240 | tf_op jit(solution)/shard_map/ppermute | solution.py:728
  10.9 0.0 copy-start.3
  10.9 0.6 copy-done.3
  11.5 3.6 %own_cells.1 = (f32[6,6,8,384]{3,2,1,0:T(8,128)S(1)}, f32[6,6,8,384]{3,2,1,0:T(8,128)S(1)}, f32[6,6,8,384]{3,2,1,0:T(8,128)S(1)}, f32[6,6,8,384]{3,2,1,0:T(8,128...) custom-call(f32[256]{0:T(256)S(1)} %copy-done.3, ...), custom_call_target="tpu_custom_call" | custom-call | flops 200000000 | bytes 8000000 | tf_op jit(solution)/shard_map/own_cells/pallas_call | solution.py:733
  15.1 0.0 collective-permute-done.got
  15.1 0.8 first_step_odd.1
  15.9 0.0 collective-permute-done.1.got
  15.9 0.9 first_step_even.1
  16.8 29.2 %all_to_all.15.rates = f32[32,1,128]{2,1,0:T(1,128)S(1)} all-to-all(f32[32,1,128]{2,1,0:T(1,128)S(1)} %get-tuple-element.95), channel_id=1, replica_groups=mesh['event'=16,'row'=32] {'row'}, dimensions={0} | all-to-all | bytes 32768 | tf_op jit(solution)/shard_map/all_to_all | solution.py:755
  46.0 7.1 %second_step_and_adjoint.1 = (f32[4,6,8,384]{3,2,1,0:T(8,128)S(1)}, f32[4,6,8,384]{3,2,1,0:T(8,128)S(1)}, f32[16,4,128]{2,1,0:T(4,128)S(1)}) custom-call(f32[32,1,128]{2,1,0:T(1,128)S(1)} %all_to_all.15.rates, bf16[256,192]{1,0:T(8,128)(2,1)S(1)} %get-tuple-element.96.pick, bf16[192,256]{1,0:T(8,128)(2,1)S(1)} %get-tuple-element.97.put, ...), custom_call_target="tpu_custom_call" | custom-call | tf_op jit(solution)/shard_map/second_step_and_adjoint/pallas_call | solution.py:756
  53.0 21.5 %all_to_all.16.parts = f32[16,4,128]{2,1,0:T(4,128)S(1)} all-to-all(f32[16,4,128]{2,1,0:T(4,128)S(1)} %get-tuple-element.113), channel_id=1, replica_groups={{0,1,2,3,4,5,6,7,64,65,66,67,68,69,70,71},{8,9,10,11,12,13,14,15,72,73,..., dimensions={0} | all-to-all | bytes 65536 | tf_op jit(solution)/shard_map/all_to_all | solution.py:768
  74.5 0.1 ring_sums.1
  74.7 16.5 %all_to_all.17.parts = f32[32,1,1536]{2,1,0:T(1,128)S(1)} all-to-all(f32[32,1,1536]{2,1,0:T(1,128)S(1)} %ring_sums.1), channel_id=1, replica_groups={{0,32,128,160,256,288,384,416,8,40,136,168,264,296,392,424,16,48,144,17..., dimensions={0} | all-to-all | bytes 393216 | tf_op jit(solution)/shard_map/all_to_all | solution.py:770
  91.2 1.1 %final_head_and_sums.1 = (f32[48,4,384]{2,1,0:T(4,128)}, f32[1,256]{1,0:T(1,128)}, f32[1,256]{1,0:T(1,128)}, f32[1,256]{1,0:T(1,128)}, f32[1,1]{1,0:T(1,128)}) custom-call(f32[32,1,1536]{2,1,0:T(1,128)S(1)} %all_to_all.17.parts, f32[4,6,8,384]{3,2,1,0:T(8,128)S(1)} %get-tuple-element.114.h1, f32[4,6,8,384]{3,2,1,0:T(8,128)S(1)} %get-tuple-element.115.g2), custom_call_target="tpu_custom_call" | custom-call | tf_op jit(solution)/shard_map/final_head_and_sums/pallas_call | solution.py:772
  (6 shorter events, 0.0 us)
Async XLA Ops:
  0.6 0.7 copy-start.1
  0.6 0.7 copy-start.2
  1.3 1.0 %copy-start = (f32[1,48,4,384]{3,2,1,0:T(4,128)S(1)}, f32[1,48,4,384]{3,2,1,0:T(4,128)}, u32[]{:S(2)}) copy-start(f32[1,48,4,384]{3,2,1,0:T(4,128)} %param.8) | copy-start | bytes 884740
  2.7 12.4 %collective-permute-start = (f32[13,8,384]{2,1,0:T(8,128)S(1)}, f32[13,8,384]{2,1,0:T(8,128)S(1)}, u32[]{:S(2)}, u32[]{:S(2)}) collective-permute-start(f32[13,8,384]{2,1,0:T(8,128)S(1)} %get-tuple-element.67), channel_id=1, source_target_pairs={{1,2},{3,4},{5,6},{7,8},{9,10},{11,12},{13,14},{15,16},{17,18},{19... | collective-permute-start | bytes 479240 | tf_op jit(solution)/shard_map/ppermute | solution.py:727
  3.4 7.5 %copy-start.4 = (f32[256]{0:T(256)S(1)}, f32[256]{0:T(256)}, u32[]{:S(2)}) copy-start(f32[256]{0:T(256)} %tab_a.1) | copy-start | bytes 3076
  3.4 7.5 %copy-start.5 = (f32[256]{0:T(256)S(1)}, f32[256]{0:T(256)}, u32[]{:S(2)}) copy-start(f32[256]{0:T(256)} %tab_n.1) | copy-start | bytes 3076
  3.4 7.4 %copy-start.6 = (s32[1,256]{1,0:T(1,128)S(1)}, s32[1,256]{1,0:T(1,128)}, u32[]{:S(2)}) copy-start(s32[1,256]{1,0:T(1,128)} %cells_at.1) | copy-start | bytes 3076
  3.5 7.4 %copy-start.7 = (f32[1,256]{1,0:T(1,128)S(1)}, f32[1,256]{1,0:T(1,128)}, u32[]{:S(2)}) copy-start(f32[1,256]{1,0:T(1,128)} %goals.1) | copy-start | bytes 3076
  3.5 12.5 %collective-permute-start.1 = (f32[13,8,384]{2,1,0:T(8,128)S(1)}, f32[13,8,384]{2,1,0:T(8,128)S(1)}, u32[]{:S(2)}, u32[]{:S(2)}) collective-permute-start(f32[13,8,384]{2,1,0:T(8,128)S(1)} %get-tuple-element.81), channel_id=1, source_target_pairs={{0,1},{2,3},{4,5},{6,7},{8,9},{10,11},{12,13},{14,15},{16,17},{18,... | collective-permute-start | bytes 479240 | tf_op jit(solution)/shard_map/ppermute | solution.py:728
  10.9 0.7 copy-start.3

commit v6 on v4

--- a/solution.py
+++ b/solution.py
@@ -608,10 +608,11 @@
     by_zone = parts[0] + (parts[1] + parts[2])
     fields = [by_zone[4 * q : 4 * q + 4, :] for q in range(3)]
     sub4 = iota((4, 32), 0)
-    fields.append(jnp.where(sub4 == 0, loss[0], jnp.where(sub4 == 1, loss[1], loss[2])))
+    lane4 = iota((4, 32), 1)
+    losses = jnp.where(sub4 == 0, loss[0], jnp.where(sub4 == 1, loss[1], loss[2]))
+    fields.append(jnp.where(lane4 == 0, losses, jnp.where(lane4 == 1, most, size)))
     sums = jnp.concatenate(fields, 1)
-    state = jnp.where(iota((4, 128), 1) < 64, most, size)
-    payload = jnp.where(iota((4, 128), 0) == 3, state, sums)
+    payload = jnp.concatenate([sums[i : i + 1, :] for i in range(3)], 1)
     spread[...] = jnp.broadcast_to(payload[None], spread.shape)
 
 
@@ -622,7 +623,10 @@
     most = None
     loss = jnp.zeros((SUB, 256), F32)
     for z in range(8):
-        tile = jnp.concatenate([parts[z], parts[8 + z]], 0)
+        lines = []
+        for part in (parts[z], parts[8 + z]):
+            lines += [part[:, 128 * i : 128 * (i + 1)] for i in range(3)] + [blank[0:1, :]]
+        tile = jnp.concatenate(lines, 0)
         most = tile if most is None else jnp.maximum(most, tile)
         tile = jnp.concatenate([tile, blank], 1)
         for q in range(3):
@@ -634,11 +638,11 @@
     rows = []
     one = iota((1, 256), 1)
     for z_hi in range(2):
-        state = most[4 * z_hi + 3 : 4 * z_hi + 4, :]
+        state = most[4 * z_hi : 4 * z_hi + 1, :]
         for power in range(3):
             row = total[4 * z_hi + power : 4 * z_hi + power + 1, :]
-            row = jnp.where(one == 253, state[:, 0:1], row)
-            rows.append(jnp.where(one == 254, state[:, 64:65], row))
+            row = jnp.where(one == 253, state[:, 97:98], row)
+            rows.append(jnp.where(one == 254, state[:, 98:99], row))
     rows = jnp.concatenate(rows, 1)
     spread[...] = jnp.broadcast_to(rows[None], spread.shape)
 
@@ -754,7 +758,7 @@
         second_kernel,
         "second_step_and_adjoint",
         [VMEM] * 18,
-        [(OWN, F32), (OWN, F32), ((16, 4, 128), F32)],
+        [(OWN, F32), (OWN, F32), ((16, 1, 384), F32)],
         scratch=[pltpu.VMEM(FIELD, F32)] * 4
         + [pltpu.VMEM(OWN, F32)] * 7
         + [pltpu.VMEM(FIELD, F32)] * 2

time: 92.5 us -> 92.4 us (level)
  no operation moved by 1% of the time
where the time goes in v6:
time: 92.4 us; the launch traced here: 92.1 us
  blocking collectives  67.1 us (73%)
  Pallas kernels  13.8 us (15%)
  starting transfers between devices  8.05 us (9%)
  local copies, waits for them, and re-layouts  2.3 us (2%)
    all_to_all x2, blocking collectives, local(): lax.all_to_all(sums, ('event', 'row'), 0, 0, tiled=True, axis_index_group...  38 us
    all_to_all x1, blocking collectives, local(): rates = lax.all_to_all(rates, 'row', 0, 0, tiled=True)  29.2 us
    ppermute x1, starting transfers between devices, local(): got_even = lax.ppermute(send_even, 'row', even + [(j, i) for i, j in even])  7.38 us
    pallas_call x1, Pallas kernels, local(): call(second_kernel, 'second_step_and_adjoint', [VMEM] * 18, [(OWN, F32),...  6.85 us
    pallas_call x1, Pallas kernels, local(): call(own_kernel, 'own_cells', [SMEM] * 4 + [VMEM] * 4, fields + [((SUB, W...  3.54 us
    unnamed x16, local copies, waits for them, and re-layouts  2.3 us
  transfers between devices with their start and end apart: 2, of which 0 were waited for; matrix products, arithmetic and copies ran while one was open for 0% of the time, Pallas kernels for 5%

profile of v6, /device:TPU:1, one launch (start us, length us, event | category | flops | bytes accessed | tf_op | source)
XLA Modules:
  0.0 92.1 jit_solution(776246179052067374)
XLA Ops:
  0.6 0.0 copy-start.1
  0.7 0.7 copy-done.1
  1.3 0.0 copy-done.2
  1.3 1.0 %copy-done = f32[1,48,4,384]{3,2,1,0:T(4,128)S(1)} copy-done((f32[1,48,4,384]{3,2,1,0:T(4,128)S(1)}, f32[1,48,4,384]{3,2,1,0:T(4,128)}, u32[]{:S(2)}) %copy-start) | copy-done | bytes 294936
  2.3 0.4 pack_edges.1
  2.7 0.7 collective-permute-start
  3.4 0.0 copy-start.4
  3.4 0.0 copy-start.5
  3.4 0.0 copy-start.6
  3.5 0.0 copy-start.7
  3.5 7.4 %collective-permute-start.1 = (f32[13,8,384]{2,1,0:T(8,128)S(1)}, f32[13,8,384]{2,1,0:T(8,128)S(1)}, u32[]{:S(2)}, u32[]{:S(2)}) collective-permute-start(f32[13,8,384]{2,1,0:T(8,128)S(1)} %get-tuple-element.81), channel_id=1, source_target_pairs={{0,1},{2,3},{4,5},{6,7},{8,9},{10,11},{12,13},{14,15},{16,17},{18,... | collective-permute-start | bytes 479240 | tf_op jit(solution)/shard_map/ppermute | solution.py:729
  10.9 0.0 copy-start.3
  10.9 0.6 copy-done.3
  11.5 3.5 %own_cells.1 = (f32[6,6,8,384]{3,2,1,0:T(8,128)S(1)}, f32[6,6,8,384]{3,2,1,0:T(8,128)S(1)}, f32[6,6,8,384]{3,2,1,0:T(8,128)S(1)}, f32[6,6,8,384]{3,2,1,0:T(8,128...) custom-call(f32[256]{0:T(256)S(1)} %copy-done.3, ...), custom_call_target="tpu_custom_call" | custom-call | flops 200000000 | bytes 8000000 | tf_op jit(solution)/shard_map/own_cells/pallas_call | solution.py:734
  15.1 0.0 collective-permute-done.got
  15.1 0.8 first_step_odd.1
  15.9 0.0 collective-permute-done.1.got
  15.9 0.9 first_step_even.1
  16.8 29.2 %all_to_all.15.rates = f32[32,1,128]{2,1,0:T(1,128)S(1)} all-to-all(f32[32,1,128]{2,1,0:T(1,128)S(1)} %get-tuple-element.95), channel_id=1, replica_groups=mesh['event'=16,'row'=32] {'row'}, dimensions={0} | all-to-all | bytes 32768 | tf_op jit(solution)/shard_map/all_to_all | solution.py:756
  46.0 6.8 %second_step_and_adjoint.1 = (f32[4,6,8,384]{3,2,1,0:T(8,128)S(1)}, f32[4,6,8,384]{3,2,1,0:T(8,128)S(1)}, f32[16,1,384]{2,1,0:T(1,128)S(1)}) custom-call(f32[32,1,128]{2,1,0:T(1,128)S(1)} %all_to_all.15.rates, bf16[256,192]{1,0:T(8,128)(2,1)S(1)} %get-tuple-element.96.pick, bf16[192,256]{1,0:T(8,128)(2,1)S(1)} %get-tuple-element.97.put, ...), custom_call_target="tpu_custom_call" | custom-call | tf_op jit(solution)/shard_map/second_step_and_adjoint/pallas_call | solution.py:757
  52.9 21.4 %all_to_all.16.parts = f32[16,1,384]{2,1,0:T(1,128)S(1)} all-to-all(f32[16,1,384]{2,1,0:T(1,128)S(1)} %get-tuple-element.113), channel_id=1, replica_groups={{0,1,2,3,4,5,6,7,64,65,66,67,68,69,70,71},{8,9,10,11,12,13,14,15,72,73,..., dimensions={0} | all-to-all | bytes 49152 | tf_op jit(solution)/shard_map/all_to_all | solution.py:769
  74.3 0.1 ring_sums.1
  74.4 16.5 %all_to_all.17.parts = f32[32,1,1536]{2,1,0:T(1,128)S(1)} all-to-all(f32[32,1,1536]{2,1,0:T(1,128)S(1)} %ring_sums.1), channel_id=1, replica_groups={{0,32,128,160,256,288,384,416,8,40,136,168,264,296,392,424,16,48,144,17..., dimensions={0} | all-to-all | bytes 393216 | tf_op jit(solution)/shard_map/all_to_all | solution.py:771
  91.0 1.1 %final_head_and_sums.1 = (f32[48,4,384]{2,1,0:T(4,128)}, f32[1,256]{1,0:T(1,128)}, f32[1,256]{1,0:T(1,128)}, f32[1,256]{1,0:T(1,128)}, f32[1,1]{1,0:T(1,128)}) custom-call(f32[32,1,1536]{2,1,0:T(1,128)S(1)} %all_to_all.17.parts, f32[4,6,8,384]{3,2,1,0:T(8,128)S(1)} %get-tuple-element.114.h1, f32[4,6,8,384]{3,2,1,0:T(8,128)S(1)} %get-tuple-element.115.g2), custom_call_target="tpu_custom_call" | custom-call | tf_op jit(solution)/shard_map/final_head_and_sums/pallas_call | solution.py:773
  (6 shorter events, 0.0 us)
Async XLA Ops:
  0.6 0.7 copy-start.1
  0.6 0.7 copy-start.2
  1.3 1.0 %copy-start = (f32[1,48,4,384]{3,2,1,0:T(4,128)S(1)}, f32[1,48,4,384]{3,2,1,0:T(4,128)}, u32[]{:S(2)}) copy-start(f32[1,48,4,384]{3,2,1,0:T(4,128)} %param.8) | copy-start | bytes 884740
  2.7 12.3 %collective-permute-start = (f32[13,8,384]{2,1,0:T(8,128)S(1)}, f32[13,8,384]{2,1,0:T(8,128)S(1)}, u32[]{:S(2)}, u32[]{:S(2)}) collective-permute-start(f32[13,8,384]{2,1,0:T(8,128)S(1)} %get-tuple-element.67), channel_id=1, source_target_pairs={{1,2},{3,4},{5,6},{7,8},{9,10},{11,12},{13,14},{15,16},{17,18},{19... | collective-permute-start | bytes 479240 | tf_op jit(solution)/shard_map/ppermute | solution.py:728
  3.4 7.5 %copy-start.4 = (f32[256]{0:T(256)S(1)}, f32[256]{0:T(256)}, u32[]{:S(2)}) copy-start(f32[256]{0:T(256)} %tab_a.1) | copy-start | bytes 3076
  3.4 7.5 %copy-start.5 = (f32[256]{0:T(256)S(1)}, f32[256]{0:T(256)}, u32[]{:S(2)}) copy-start(f32[256]{0:T(256)} %tab_n.1) | copy-start | bytes 3076
  3.4 7.4 %copy-start.6 = (s32[1,256]{1,0:T(1,128)S(1)}, s32[1,256]{1,0:T(1,128)}, u32[]{:S(2)}) copy-start(s32[1,256]{1,0:T(1,128)} %cells_at.1) | copy-start | bytes 3076
  3.5 7.4 %copy-start.7 = (f32[1,256]{1,0:T(1,128)S(1)}, f32[1,256]{1,0:T(1,128)}, u32[]{:S(2)}) copy-start(f32[1,256]{1,0:T(1,128)} %goals.1) | copy-start | bytes 3076
  3.5 12.5 %collective-permute-start.1 = (f32[13,8,384]{2,1,0:T(8,128)S(1)}, f32[13,8,384]{2,1,0:T(8,128)S(1)}, u32[]{:S(2)}, u32[]{:S(2)}) collective-permute-start(f32[13,8,384]{2,1,0:T(8,128)S(1)} %get-tuple-element.81), channel_id=1, source_target_pairs={{0,1},{2,3},{4,5},{6,7},{8,9},{10,11},{12,13},{14,15},{16,17},{18,... | collective-permute-start | bytes 479240 | tf_op jit(solution)/shard_map/ppermute | solution.py:729
  10.9 0.7 copy-start.3
